TPU v7x, 256 devices: a whole 4x4x8 slice. The times are simulated.
256 devices in a mesh: scan: 32 (over y, z_hi, core), cuts: 8 (over x, z_lo).
Axes of the slice: x: 4, y: 4, z: 8 (z_hi: 4, z_lo: 2; z = z_hi * 2 + z_lo), core: 2. Of those that a mesh axis runs over, the one named last changes fastest.
Arguments:
- positions: int32 [64, 2], P('scan'), may hold values from 0 to 768, as said below
- probe: float32 [2, 256, 256], replicated, may hold values from -5 to 5
- prop_phase: float32 [256, 256], replicated, may hold values from -3.140625 to 3.140625
- transmission: float32 [2, 16, 8192, 1024], P(None, 'cuts', 'scan'), may hold values from -1 to 1, as said below
- measured: float32 [64, 256, 256], P('scan'), may hold values from 0.05 to 2
Outputs:
- object_grad: float32 [2, 16, 8192, 1024], P(None, 'cuts', 'scan')
- probe_grad: float32 [2, 256, 256], P(None, 'cuts')
Inputs may be any that keep to these rules, and one draw needn't show every extreme that they name: positions[p, 0] is the top row of position p's window within the tile of scan block p // 2 and lies below 256; positions[p, 1] is its left column, at most 768. In every block of 2 rows one row has top row 255 and another has left column 768. `transmission`: entries of modulus at most 1.
All inputs are finite; a program needn't handle non-finite values.
Results may differ from a plain program's by a relative error of at most 0.0003.
Values sent between devices are 32-bit elements; how exact they have to be, the bound alone decides.
No kernel may reach another device: no remote copies, remote signals or barrier semaphores. Data moves between devices by JAX's collectives and lax.ppermute only.
A program may use at most 128 MiB of HBM per device.

v0:
```python
import math

import jax
import jax.numpy as jnp
from jax import lax
from jax.sharding import PartitionSpec as P

accurate = lax.Precision.HIGHEST


def from_behind(value, axis, steps):
    count = lax.axis_size(axis)
    pairs = [(source, (source + steps) % count) for source in range(count)]
    return lax.ppermute(value, axis, pairs)


def from_behind_2(block, axis, distance):
    devices = range(lax.axis_size(axis))
    route = [(i - distance, i) for i in devices if i - distance in devices]
    return lax.ppermute(block, axis, route)


def broadcast(block, axis, source):
    block = jnp.where(lax.axis_index(axis) == source, block, jnp.zeros_like(block))
    return lax.psum(block, axis)


def matmul(left_op, right_op):
    return jnp.dot(left_op, right_op, precision=accurate, preferred_element_type=jnp.float32)


def dft_tables(extent):
    counter = jnp.arange(extent, dtype=jnp.int32)
    turns = counter[:, None] * counter[None, :] % extent
    angles = turns.astype(jnp.float32) * (2.0 * math.pi / extent)
    factor = 1.0 / math.sqrt(extent)
    return (jnp.cos(angles) * factor, -jnp.sin(angles) * factor)


def transform(field, cosine, sine):
    extent = field.shape[1]
    joined = jnp.concatenate([field[0], field[1]], axis=1)
    real_part = matmul(cosine, joined)
    imag_part = matmul(sine, joined)
    upper_re = real_part[:, :extent] - imag_part[:, extent:]
    upper_im = real_part[:, extent:] + imag_part[:, :extent]
    stacked = jnp.concatenate([upper_re, upper_im], axis=0)
    real_part = matmul(stacked, cosine)
    imag_part = matmul(stacked, sine)
    return jnp.stack(
        [real_part[:extent] - imag_part[extent:], real_part[extent:] + imag_part[:extent]]
    )


def complex_mul(first, second):
    return jnp.stack(
        [first[0] * second[0] - first[1] * second[1], first[0] * second[1] + first[1] * second[0]]
    )


def conj_mul(first, second):
    return jnp.stack(
        [first[0] * second[0] + first[1] * second[1], first[0] * second[1] - first[1] * second[0]]
    )


def shards(positions, probe, prop_phase, transmission, measured):
    extent = probe.shape[1]
    layers = transmission.shape[1]
    tile_rows = transmission.shape[2]
    columns = transmission.shape[3]
    count = positions.shape[0]
    cut_count = lax.axis_size("cuts")
    cut_index = lax.axis_index("cuts")
    last_cut = cut_index == cut_count - 1
    first_cut = cut_index == 0
    own_rows = extent // cut_count
    rim_rows = from_behind(transmission, "scan", -1)
    extended = jnp.concatenate([transmission, rim_rows], axis=2)
    cosine, sine = dft_tables(extent)
    kernel = jnp.stack([jnp.cos(prop_phase), jnp.sin(prop_phase)])
    group_size = 1
    block_count = count // group_size
    step_count = block_count + cut_count - 1

    def onward(spectrum):
        return transform(complex_mul(kernel, spectrum), cosine, -sine)

    def adjoint(grad_wave):
        return transform(conj_mul(kernel, transform(grad_wave, cosine, sine)), cosine, -sine)

    def window(offset):
        return jnp.stack(
            [
                lax.dynamic_slice(
                    extended[:, layer_no], (0, offset[0], offset[1]), (2, extent, extent)
                )
                for layer_no in range(layers)
            ]
        )

    def detect(operands):
        spectrum, target = operands
        power = spectrum[0] * spectrum[0] + spectrum[1] * spectrum[1]
        return (jnp.zeros_like(spectrum), transform((power - target) * spectrum, cosine, -sine))

    def pass_on(operands):
        return (onward(operands[0]), jnp.zeros_like(operands[0]))

    def forward_one(wavefield, offset, target):
        patch = window(offset)
        history = []
        seed_grad = jnp.zeros_like(wavefield)
        for layer_no in range(layers):
            history.append(wavefield)
            spectrum = transform(complex_mul(patch[layer_no], wavefield), cosine, sine)
            if layer_no < layers - 1:
                wavefield = onward(spectrum)
            else:
                wavefield, seed_grad = lax.cond(last_cut, detect, pass_on, (spectrum, target))
        return (wavefield, jnp.stack(history), seed_grad)

    def forward_step(step_no, state):
        outgoing, saved, seeds = state
        arrived = from_behind_2(outgoing, "cuts", 1)
        entering = jnp.where(first_cut, jnp.broadcast_to(probe, arrived.shape), arrived)
        block_id = step_no - cut_index
        active = (block_id >= 0) & (block_id < block_count)
        start_row = jnp.clip(block_id, 0, block_count - 1) * group_size

        def forward_work(current):
            offsets = lax.dynamic_slice_in_dim(positions, start_row, group_size, 0)
            targets = lax.dynamic_slice_in_dim(measured, start_row, group_size, 0)
            leaving, fresh, seed_new = jax.vmap(forward_one)(entering, offsets, targets)
            return (
                leaving,
                lax.dynamic_update_slice_in_dim(current[1], fresh, start_row, 0),
                lax.dynamic_update_slice_in_dim(current[2], seed_new, start_row, 0),
            )

        return lax.cond(active, forward_work, lambda current: current, (outgoing, saved, seeds))

    start_forward = (
        jnp.zeros((group_size, 2, extent, extent), jnp.float32),
        jnp.zeros((count, layers, 2, extent, extent), jnp.float32),
        jnp.zeros((count, 2, extent, extent), jnp.float32),
    )
    unused_wave, saved, seeds = lax.fori_loop(0, step_count, forward_step, start_forward)

    def backward_one(grad_in, offset, history, seed_grad):
        patch = window(offset)
        grad_wave = grad_in
        pieces = [None] * layers
        for layer_no in reversed(range(layers)):
            if layer_no == layers - 1:
                chi_grad = lax.cond(
                    last_cut,
                    lambda operands: operands[1],
                    lambda operands: adjoint(operands[0]),
                    (grad_wave, seed_grad),
                )
            else:
                chi_grad = adjoint(grad_wave)
            pieces[layer_no] = conj_mul(history[layer_no], chi_grad)
            grad_wave = conj_mul(patch[layer_no], chi_grad)
        return (grad_wave, jnp.stack(pieces, axis=1))

    def backward_step(step_no, state):
        outgoing, gradient, probe_part = state
        arrived = from_behind_2(outgoing, "cuts", -1)
        block_id = step_no - (cut_count - 1 - cut_index)
        active = (block_id >= 0) & (block_id < block_count)
        start_row = jnp.clip(block_id, 0, block_count - 1) * group_size

        def backward_work(current):
            offsets = lax.dynamic_slice_in_dim(positions, start_row, group_size, 0)
            history = lax.dynamic_slice_in_dim(saved, start_row, group_size, 0)
            seed_block = lax.dynamic_slice_in_dim(seeds, start_row, group_size, 0)
            leaving, pieces = jax.vmap(backward_one)(arrived, offsets, history, seed_block)

            def place(slot_no, accum):
                offset = offsets[slot_no]
                spot = (0, 0, offset[0], offset[1])
                region = lax.dynamic_slice(accum, spot, (2, layers, extent, extent))
                return lax.dynamic_update_slice(accum, region + pieces[slot_no], spot)

            grown = lax.fori_loop(0, group_size, place, current[1])
            added = jnp.where(first_cut, jnp.sum(leaving, axis=0), 0.0)
            return (leaving, grown, current[2] + added)

        return lax.cond(
            active, backward_work, lambda current: current, (outgoing, gradient, probe_part)
        )

    start_backward = (
        jnp.zeros((group_size, 2, extent, extent), jnp.float32),
        jnp.zeros((2, layers, tile_rows + extent, columns), jnp.float32),
        jnp.zeros((2, extent, extent), jnp.float32),
    )
    unused_grad, gradient, probe_part = lax.fori_loop(0, step_count, backward_step, start_backward)
    lower_rows = gradient[:, :, tile_rows:]
    arriving = from_behind(lower_rows, "scan", 1)
    object_grad = gradient[:, :, :tile_rows].at[:, :, :extent].add(arriving)
    row_start = cut_index * own_rows
    summed = lax.psum(probe_part, "scan")
    whole = broadcast(summed, "cuts", 0)
    probe_grad = lax.dynamic_slice_in_dim(whole, row_start, own_rows, 1)
    return (object_grad, probe_grad)


def solution(mesh):
    in_specs = (P("scan", None), P(), P(), P(None, "cuts", "scan", None), P("scan", None, None))
    out_specs = (P(None, "cuts", "scan", None), P(None, "cuts", None))
    return jax.shard_map(shards, mesh=mesh, in_specs=in_specs, out_specs=out_specs, check_vma=False)
```

profile of v0, /device:TPU:32, one launch (start us, length us, event | category | flops | bytes accessed | tf_op | source)
XLA Modules:
  0.0 1383.0 jit_solution(15703007720378043750)
XLA Ops:
  7.2 6.9 fusion.108
  14.2 7.3 collective-permute-start.2
  22.8 88.0 %collective-permute-done.2 = f32[2,2,256,1024]{3,2,0,1:T(8,128)} collective-permute-done((f32[2,2,256,1024]{3,2,0,1:T(8,128)}, f32[2,2,256,1024]{3,2,0,1:T(8,128)}, u32[]{:S(2)}, u32[]{:S(2)}) %collective-permute-start.2) | collective-permute-done | bytes 4194336 | tf_op jit(solution)/shard_map/ppermute | solution.py:14
  110.8 4.8 constant_dynamic-update-slice_fusion.1
  115.6 8.8 copy.21
  127.8 269.7 %while.51 = (s32[]{:T(128)}, f32[1,2,256,256]{3,2,1,0:T(8,128)}, f32[2,2,2,256,256]{3,4,2,1,0:T(8,128)}, f32[2,2,256,256]{3,2,1,0:T(8,128)}, s32[]{:T(128)}, /*i...) while((s32[]{:T(128)}, f32[1,2,256,256]{3,2,1,0:T(8,128)}, ...), condition=%wide.region_5.6_spmd.clone.clone, body=%wide.region_0.5_spmd.clone.clone.sunk | while | flops 6449332224 | bytes 91489552 | solution.py:148
  129.4 5.8 collective-permute-start
  135.4 6.8 collective-permute-done
  143.4 5.3 collective-permute-start
  148.9 25.9 %collective-permute-done = f32[1,2,256,256]{2,3,1,0:T(8,128)S(1)} collective-permute-done((f32[1,2,256,256]{2,3,1,0:T(8,128)S(1)}, f32[1,2,256,256]{2,3,1,0:T(8,128)S(1)}, u32[]{:S(2)}, u32[]{:S(2)}) %collective-permute-start) | collective-permute-done | bytes 524320 | tf_op jit(solution)/shard_map/while/body/eval_jaxpr/ppermute | solution.py:20
  174.8 24.2 %conditional.12 = ((f32[1,2,256,256]{3,2,1,0:T(8,128)}, f32[2,2,2,256,256]{3,4,2,1,0:T(8,128)}, f32[2,2,256,256]{3,2,1,0:T(8,128)})) conditional(s32[]{:T(128)} %convert_element_type.129, (f32[1,2,256,256]{3,2,1,0:T(8,128)}, f32[2,2,2,256,256]{3,4,2,1,0:T(8,128)}, f32[2,2,256,256]{3,2,1,0:T(8,128)}) %tuple.256, (pred[]{:T(512)}, ...), branch_computations={%region_1.1_spmd, %region_2.4_spmd.clone} | conditional | flops 6448414720 | bytes 87819144 | solution.py:141
  178.9 4.5 fusion.104
  202.3 9.0 collective-permute-done
  211.3 24.2 %conditional.12 = ((f32[1,2,256,256]{3,2,1,0:T(8,128)}, f32[2,2,2,256,256]{3,4,2,1,0:T(8,128)}, f32[2,2,256,256]{3,2,1,0:T(8,128)})) conditional(s32[]{:T(128)} %convert_element_type.129, (f32[1,2,256,256]{3,2,1,0:T(8,128)}, f32[2,2,2,256,256]{3,4,2,1,0:T(8,128)}, f32[2,2,256,256]{3,2,1,0:T(8,128)}) %tuple.256, (pred[]{:T(512)}, ...), branch_computations={%region_1.1_spmd, %region_2.4_spmd.clone} | conditional | flops 6448414720 | bytes 87819144 | solution.py:141
  215.5 4.5 fusion.104
  239.7 10.5 collective-permute-done
  251.5 25.5 %collective-permute-start = (f32[1,2,256,256]{2,3,1,0:T(8,128)S(1)}, f32[1,2,256,256]{2,3,1,0:T(8,128)S(1)}, u32[]{:S(2)}, u32[]{:S(2)}) collective-permute-start(f32[1,2,256,256]{2,3,1,0:T(8,128)S(1)} %copy.31), channel_id=1, source_target_pairs={{0,1},{1,2},{2,3},{3,4},{4,5},{5,6},{6,7},{8,9},{9,10},{10,11},{11... | collective-permute-start | bytes 1572872 | tf_op jit(solution)/shard_map/while/body/eval_jaxpr/ppermute | solution.py:20
  277.1 8.9 collective-permute-done
  287.2 5.3 collective-permute-start
  292.7 8.7 collective-permute-done
  302.7 24.7 %collective-permute-start = (f32[1,2,256,256]{2,3,1,0:T(8,128)S(1)}, f32[1,2,256,256]{2,3,1,0:T(8,128)S(1)}, u32[]{:S(2)}, u32[]{:S(2)}) collective-permute-start(f32[1,2,256,256]{2,3,1,0:T(8,128)S(1)} %copy.31), channel_id=1, source_target_pairs={{0,1},{1,2},{2,3},{3,4},{4,5},{5,6},{6,7},{8,9},{9,10},{10,11},{11... | collective-permute-start | bytes 1572872 | tf_op jit(solution)/shard_map/while/body/eval_jaxpr/ppermute | solution.py:20
  327.6 11.5 collective-permute-done
  340.4 5.3 collective-permute-start
  345.9 11.0 collective-permute-done
  358.2 21.5 %collective-permute-start = (f32[1,2,256,256]{2,3,1,0:T(8,128)S(1)}, f32[1,2,256,256]{2,3,1,0:T(8,128)S(1)}, u32[]{:S(2)}, u32[]{:S(2)}) collective-permute-start(f32[1,2,256,256]{2,3,1,0:T(8,128)S(1)} %copy.31), channel_id=1, source_target_pairs={{0,1},{1,2},{2,3},{3,4},{4,5},{5,6},{6,7},{8,9},{9,10},{10,11},{11... | collective-permute-start | bytes 1572872 | tf_op jit(solution)/shard_map/while/body/eval_jaxpr/ppermute | solution.py:20
  379.9 6.5 collective-permute-done
  400.5 4.4 broadcast_in_dim.40
  405.7 483.0 %while.52 = (s32[]{:T(128)}, f32[1,2,256,256]{3,2,1,0:T(8,128)S(1)}, f32[2,2,512,1024]{3,2,0,1:T(8,128)}, f32[2,256,256]{2,1,0:T(8,128)}, s32[]{:T(128)}, /*inde...) while((s32[]{:T(128)}, ...), condition=%wide.region_11.12_spmd.clone.clone, body=%wide.region_6.11_spmd.clone.clone.sunk | while | flops 6450774016 | bytes 78643976 | solution.py:200
  407.8 10.6 collective-permute-done.1
  418.4 4.4 collective-permute-start.1
  423.0 29.5 %collective-permute-done.1 = f32[1,2,256,256]{3,2,1,0:T(8,128)S(1)} collective-permute-done((f32[1,2,256,256]{3,2,1,0:T(8,128)S(1)}, f32[1,2,256,256]{3,2,1,0:T(8,128)S(1)}, u32[]{:S(2)}, u32[]{:S(2)}) %collective-permute-start.1) | collective-permute-done | bytes 524320 | tf_op jit(solution)/shard_map/while/body/eval_jaxpr/ppermute | solution.py:20
  454.6 9.9 collective-permute-done.1
  467.6 31.9 %collective-permute-done.1 = f32[1,2,256,256]{3,2,1,0:T(8,128)S(1)} collective-permute-done((f32[1,2,256,256]{3,2,1,0:T(8,128)S(1)}, f32[1,2,256,256]{3,2,1,0:T(8,128)S(1)}, u32[]{:S(2)}, u32[]{:S(2)}) %collective-permute-start.1) | collective-permute-done | bytes 524320 | tf_op jit(solution)/shard_map/while/body/eval_jaxpr/ppermute | solution.py:20
  501.6 13.1 collective-permute-done.1
  516.9 14.2 %collective-permute-done.1 = f32[1,2,256,256]{3,2,1,0:T(8,128)S(1)} collective-permute-done((f32[1,2,256,256]{3,2,1,0:T(8,128)S(1)}, f32[1,2,256,256]{3,2,1,0:T(8,128)S(1)}, u32[]{:S(2)}, u32[]{:S(2)}) %collective-permute-start.1) | collective-permute-done | bytes 524320 | tf_op jit(solution)/shard_map/while/body/eval_jaxpr/ppermute | solution.py:20
  533.2 251.2 %collective-permute-done.1 = f32[1,2,256,256]{3,2,1,0:T(8,128)S(1)} collective-permute-done((f32[1,2,256,256]{3,2,1,0:T(8,128)S(1)}, f32[1,2,256,256]{3,2,1,0:T(8,128)S(1)}, u32[]{:S(2)}, u32[]{:S(2)}) %collective-permute-start.1) | collective-permute-done | bytes 524320 | tf_op jit(solution)/shard_map/while/body/eval_jaxpr/ppermute | solution.py:20
  784.5 41.6 %conditional.13 = ((f32[1,2,256,256]{3,2,1,0:T(8,128)S(1)}, f32[2,2,512,1024]{3,2,0,1:T(8,128)}, f32[2,256,256]{2,1,0:T(8,128)})) conditional(s32[]{:T(128)} %convert_element_type.131, (f32[1,2,256,256]{3,2,1,0:T(8,128)S(1)}, f32[2,2,512,1024]{3,2,0,1:T(8,128)}, f32[2,256,256]{2,1,0:T(8,128)}) %tuple.259, (f32[2,2,512,1024]{3,2,0,1:T(8,128)}, ...), branch_computations={%region_7.7_spmd, %region_8.10_spmd.clone} | conditional | flops 6449856512 | bytes 76022144 | solution.py:191
  794.9 5.5 conditional.9
  814.6 11.5 dynamic_update_slice.12
  828.3 9.9 collective-permute-done.1
  838.2 38.4 %conditional.13 = ((f32[1,2,256,256]{3,2,1,0:T(8,128)S(1)}, f32[2,2,512,1024]{3,2,0,1:T(8,128)}, f32[2,256,256]{2,1,0:T(8,128)})) conditional(s32[]{:T(128)} %convert_element_type.131, (f32[1,2,256,256]{3,2,1,0:T(8,128)S(1)}, f32[2,2,512,1024]{3,2,0,1:T(8,128)}, f32[2,256,256]{2,1,0:T(8,128)}) %tuple.259, (f32[2,2,512,1024]{3,2,0,1:T(8,128)}, ...), branch_computations={%region_7.7_spmd, %region_8.10_spmd.clone} | conditional | flops 6449856512 | bytes 76022144 | solution.py:191
  842.1 4.3 fusion.106
  848.5 5.5 conditional.9
  868.1 8.4 dynamic_update_slice.12
  881.0 7.5 collective-permute-done.1
  895.4 391.9 %all-reduce.3.cloned.1.call-done = f32[2,256,256]{2,1,0:T(8,128)} async-done(((f32[2,256,256]{2,1,0:T(8,128)}), f32[2,256,256]{2,1,0:T(8,128)}) %all-reduce.3.cloned.1.call-update) | async-done | bytes 524304 | tf_op jit(solution)/shard_map/psum | solution.py:205
  1288.1 79.5 %all-reduce.5.cloned.1.call-done = f32[2,256,256]{2,1,0:T(8,128)} async-done(((f32[2,256,256]{2,1,0:T(8,128)}), f32[2,256,256]{2,1,0:T(8,128)}) %all-reduce.5.cloned.1.call-update) | async-done | bytes 524304 | tf_op jit(solution)/shard_map/psum | solution.py:25
  1369.1 6.8 slice_add_fusion.18
  (265 shorter events, 136.1 us)
Async XLA Ops:
  7.2 14.3 %copy-start.4 = (f32[256,256]{1,0:T(8,128)S(1)}, f32[256,256]{1,0:T(8,128)}, u32[]{:S(2)}) copy-start(f32[256,256]{1,0:T(8,128)} %param.23) | copy-start | bytes 786436
  7.2 14.4 %copy-start.3 = (f32[2,256,256]{2,1,0:T(8,128)S(1)}, f32[2,256,256]{2,1,0:T(8,128)}, u32[]{:S(2)}) copy-start(f32[2,256,256]{2,1,0:T(8,128)} %param.22) | copy-start | bytes 1572868
  7.2 1280.1 %all-reduce.3.cloned.1.call-start = ((), (), s32[]{:S(2)}) async-start(), calls=%async_computation | async-start | bytes 1048576 | tf_op jit(solution)/shard_map/psum | solution.py:205
  14.2 96.7 %collective-permute-start.2 = (f32[2,2,256,1024]{3,2,0,1:T(8,128)}, f32[2,2,256,1024]{3,2,0,1:T(8,128)}, u32[]{:S(2)}, u32[]{:S(2)}) collective-permute-start(f32[2,2,256,1024]{3,2,0,1:T(8,128)} %get-tuple-element.1519), channel_id=1, source_target_pairs={{0,248},{8,0},{16,8},{24,16},{32,24},{40,32},{48,40},{56,48},{64,5... | collective-permute-start | bytes 12582920 | tf_op jit(solution)/shard_map/ppermute | solution.py:14
  115.6 12.2 copy-start.5
  129.4 12.7 collective-permute-start
  143.4 31.3 %collective-permute-start = (f32[1,2,256,256]{2,3,1,0:T(8,128)S(1)}, f32[1,2,256,256]{2,3,1,0:T(8,128)S(1)}, u32[]{:S(2)}, u32[]{:S(2)}) collective-permute-start(f32[1,2,256,256]{2,3,1,0:T(8,128)S(1)} %copy.31), channel_id=1, source_target_pairs={{0,1},{1,2},{2,3},{3,4},{4,5},{5,6},{6,7},{8,9},{9,10},{10,11},{11... | collective-permute-start | bytes 1572872 | tf_op jit(solution)/shard_map/while/body/eval_jaxpr/ppermute | solution.py:20
  189.8 1.6 copy-start
  191.5 2.6 copy-start.1
  192.2 2.0 copy-start.2
  200.2 11.1 collective-permute-start
  226.3 1.6 copy-start
  228.0 2.6 copy-start.1
  228.7 2.0 copy-start.2
  236.7 13.4 collective-permute-start
  251.5 34.5 %collective-permute-start = (f32[1,2,256,256]{2,3,1,0:T(8,128)S(1)}, f32[1,2,256,256]{2,3,1,0:T(8,128)S(1)}, u32[]{:S(2)}, u32[]{:S(2)}) collective-permute-start(f32[1,2,256,256]{2,3,1,0:T(8,128)S(1)} %copy.31), channel_id=1, source_target_pairs={{0,1},{1,2},{2,3},{3,4},{4,5},{5,6},{6,7},{8,9},{9,10},{10,11},{11... | collective-permute-start | bytes 1572872 | tf_op jit(solution)/shard_map/while/body/eval_jaxpr/ppermute | solution.py:20
  287.2 14.2 %collective-permute-start = (f32[1,2,256,256]{2,3,1,0:T(8,128)S(1)}, f32[1,2,256,256]{2,3,1,0:T(8,128)S(1)}, u32[]{:S(2)}, u32[]{:S(2)}) collective-permute-start(f32[1,2,256,256]{2,3,1,0:T(8,128)S(1)} %copy.31), channel_id=1, source_target_pairs={{0,1},{1,2},{2,3},{3,4},{4,5},{5,6},{6,7},{8,9},{9,10},{10,11},{11... | collective-permute-start | bytes 1572872 | tf_op jit(solution)/shard_map/while/body/eval_jaxpr/ppermute | solution.py:20
  302.7 36.4 %collective-permute-start = (f32[1,2,256,256]{2,3,1,0:T(8,128)S(1)}, f32[1,2,256,256]{2,3,1,0:T(8,128)S(1)}, u32[]{:S(2)}, u32[]{:S(2)}) collective-permute-start(f32[1,2,256,256]{2,3,1,0:T(8,128)S(1)} %copy.31), channel_id=1, source_target_pairs={{0,1},{1,2},{2,3},{3,4},{4,5},{5,6},{6,7},{8,9},{9,10},{10,11},{11... | collective-permute-start | bytes 1572872 | tf_op jit(solution)/shard_map/while/body/eval_jaxpr/ppermute | solution.py:20
  340.4 16.5 %collective-permute-start = (f32[1,2,256,256]{2,3,1,0:T(8,128)S(1)}, f32[1,2,256,256]{2,3,1,0:T(8,128)S(1)}, u32[]{:S(2)}, u32[]{:S(2)}) collective-permute-start(f32[1,2,256,256]{2,3,1,0:T(8,128)S(1)} %copy.31), channel_id=1, source_target_pairs={{0,1},{1,2},{2,3},{3,4},{4,5},{5,6},{6,7},{8,9},{9,10},{10,11},{11... | collective-permute-start | bytes 1572872 | tf_op jit(solution)/shard_map/while/body/eval_jaxpr/ppermute | solution.py:20
  358.2 28.2 %collective-permute-start = (f32[1,2,256,256]{2,3,1,0:T(8,128)S(1)}, f32[1,2,256,256]{2,3,1,0:T(8,128)S(1)}, u32[]{:S(2)}, u32[]{:S(2)}) collective-permute-start(f32[1,2,256,256]{2,3,1,0:T(8,128)S(1)} %copy.31), channel_id=1, source_target_pairs={{0,1},{1,2},{2,3},{3,4},{4,5},{5,6},{6,7},{8,9},{9,10},{10,11},{11... | collective-permute-start | bytes 1572872 | tf_op jit(solution)/shard_map/while/body/eval_jaxpr/ppermute | solution.py:20
  405.7 12.7 collective-permute-start.1
  418.4 34.0 %collective-permute-start.1 = (f32[1,2,256,256]{3,2,1,0:T(8,128)S(1)}, f32[1,2,256,256]{3,2,1,0:T(8,128)S(1)}, u32[]{:S(2)}, u32[]{:S(2)}) collective-permute-start(f32[1,2,256,256]{3,2,1,0:T(8,128)S(1)} %get-tuple-element.1780), channel_id=1, source_target_pairs={{1,0},{2,1},{3,2},{4,3},{5,4},{6,5},{7,6},{9,8},{10,9},{11,10},{12... | collective-permute-start | bytes 1572872 | tf_op jit(solution)/shard_map/while/body/eval_jaxpr/ppermute | solution.py:20
  452.5 12.0 collective-permute-start.1
  464.6 34.9 %collective-permute-start.1 = (f32[1,2,256,256]{3,2,1,0:T(8,128)S(1)}, f32[1,2,256,256]{3,2,1,0:T(8,128)S(1)}, u32[]{:S(2)}, u32[]{:S(2)}) collective-permute-start(f32[1,2,256,256]{3,2,1,0:T(8,128)S(1)} %get-tuple-element.1780), channel_id=1, source_target_pairs={{1,0},{2,1},{3,2},{4,3},{5,4},{6,5},{7,6},{9,8},{10,9},{11,10},{12... | collective-permute-start | bytes 1572872 | tf_op jit(solution)/shard_map/while/body/eval_jaxpr/ppermute | solution.py:20
  499.5 15.2 %collective-permute-start.1 = (f32[1,2,256,256]{3,2,1,0:T(8,128)S(1)}, f32[1,2,256,256]{3,2,1,0:T(8,128)S(1)}, u32[]{:S(2)}, u32[]{:S(2)}) collective-permute-start(f32[1,2,256,256]{3,2,1,0:T(8,128)S(1)} %get-tuple-element.1780), channel_id=1, source_target_pairs={{1,0},{2,1},{3,2},{4,3},{5,4},{6,5},{7,6},{9,8},{10,9},{11,10},{12... | collective-permute-start | bytes 1572872 | tf_op jit(solution)/shard_map/while/body/eval_jaxpr/ppermute | solution.py:20
  514.8 16.3 %collective-permute-start.1 = (f32[1,2,256,256]{3,2,1,0:T(8,128)S(1)}, f32[1,2,256,256]{3,2,1,0:T(8,128)S(1)}, u32[]{:S(2)}, u32[]{:S(2)}) collective-permute-start(f32[1,2,256,256]{3,2,1,0:T(8,128)S(1)} %get-tuple-element.1780), channel_id=1, source_target_pairs={{1,0},{2,1},{3,2},{4,3},{5,4},{6,5},{7,6},{9,8},{10,9},{11,10},{12... | collective-permute-start | bytes 1572872 | tf_op jit(solution)/shard_map/while/body/eval_jaxpr/ppermute | solution.py:20
  531.2 253.3 %collective-permute-start.1 = (f32[1,2,256,256]{3,2,1,0:T(8,128)S(1)}, f32[1,2,256,256]{3,2,1,0:T(8,128)S(1)}, u32[]{:S(2)}, u32[]{:S(2)}) collective-permute-start(f32[1,2,256,256]{3,2,1,0:T(8,128)S(1)} %get-tuple-element.1780), channel_id=1, source_target_pairs={{1,0},{2,1},{3,2},{4,3},{5,4},{6,5},{7,6},{9,8},{10,9},{11,10},{12... | collective-permute-start | bytes 1572872 | tf_op jit(solution)/shard_map/while/body/eval_jaxpr/ppermute | solution.py:20
  826.2 12.0 collective-permute-start.1
  876.6 12.0 collective-permute-start.1
  895.3 473.8 %collective-permute-start.3 = (f32[2,2,256,1024]{3,2,1,0:T(8,128)}, f32[2,2,256,1024]{3,2,1,0:T(8,128)}, u32[]{:S(2)}, u32[]{:S(2)}) collective-permute-start(f32[2,2,256,1024]{3,2,1,0:T(8,128)} %slice.699), channel_id=1, source_target_pairs={{0,8},{8,16},{16,24},{24,32},{32,40},{40,48},{48,56},{56,64},{64,7... | collective-permute-start | bytes 12582920 | tf_op jit(solution)/shard_map/ppermute | solution.py:14
  895.4 472.3 %all-reduce.5.cloned.1.call-start = ((), (), s32[]{:S(2)}) async-start(), calls=%async_computation.1 | async-start | bytes 1048576 | tf_op jit(solution)/shard_map/psum | solution.py:25
Sparse Core Ops, SparseCore 0:
  895.5 391.7 all-reduce.2
  1290.1 77.5 all-reduce.4
where the time goes:
time: 1390 us; the launch traced here: 1380 us
  waiting for transfers between devices  1040 us (75%)
  starting transfers between devices  129 us (9%)
  local copies, waits for them, and re-layouts  99.1 us (7%)
  matrix products  40.3 us (3%)
  loops' own time  34.6 us (2%)
  other arithmetic  30.1 us (2%)
  between operations  14.3 us (1%)
    ppermute x18, waiting for transfers between devices, from_behind_2(): return lax.ppermute(block, axis, route)  477 us
    psum x1, waiting for transfers between devices, shards(): summed = lax.psum(probe_part, 'scan')  392 us
    ppermute x18, starting transfers between devices, from_behind_2(): return lax.ppermute(block, axis, route)  121 us
    ppermute x2, waiting for transfers between devices, from_behind(): return lax.ppermute(value, axis, pairs)  88 us
    psum x1, waiting for transfers between devices, broadcast(): return lax.psum(block, axis)  79.5 us
    dot_general x64, matrix products, matmul(): jnp.dot(left_op, right_op, precision=accurate, preferred_element_type=jnp...  40.3 us
  transfers between devices with their start and end apart: 22, of which 21 were waited for; matrix products, arithmetic and copies ran while one was open for 0% of the time, Pallas kernels for 0%

commit v1 on v0

v1 whole, which is shorter than its diff:
```python
import math

import jax
import jax.numpy as jnp
import ml_dtypes
import numpy as np
from jax import lax
from jax.experimental import pallas as pl
from jax.experimental.pallas import tpu as pltpu
from jax.sharding import PartitionSpec as P


AXES = ("scan", "cuts")
N = 256
H = 128
BF = jnp.bfloat16
F32 = jnp.float32


def dft_constants():
    k = np.arange(H)[:, None].astype(np.float64)
    j = np.arange(H)[None, :].astype(np.float64)
    even = np.exp(-2j * np.pi * j * k / H) / math.sqrt(N)
    odd = np.exp(-2j * np.pi * j * (2 * k + 1) / N) / math.sqrt(N)

    def real_form(c):
        return np.block([[c.real, -c.imag], [c.imag, c.real]])

    def parts(m):
        hi = m.astype(np.float32).astype(ml_dtypes.bfloat16)
        lo = (m - hi.astype(np.float64)).astype(np.float32).astype(ml_dtypes.bfloat16)
        return hi, hi, lo

    def wide(m):
        return np.concatenate(parts(m), axis=1)

    def tall(m):
        return np.concatenate(parts(m), axis=0)

    e, o = real_form(even), real_form(odd)
    left = np.stack([wide(e), wide(o), wide(e.T), wide(o.T)])
    right = np.stack([tall(e.T), tall(o.T), tall(e), tall(o)])
    return left, right


def split(x):
    hi = x.astype(BF)
    lo = (x - hi.astype(F32)).astype(BF)
    return hi, lo


def left_dot(m, x):
    hi, lo = split(x)
    return jnp.dot(m, jnp.concatenate([hi, lo, hi], axis=0), preferred_element_type=F32)


def right_dot(x, m):
    hi, lo = split(x)
    return jnp.dot(jnp.concatenate([hi, lo, hi], axis=1), m, preferred_element_type=F32)


def cat0(a, b):
    return jnp.concatenate([a, b], axis=0)


def cat1(a, b):
    return jnp.concatenate([a, b], axis=1)


def dft(re, im, lm, rm):
    u = cat0(re[:H] + re[H:], im[:H] + im[H:])
    v = cat0(re[:H] - re[H:], im[:H] - im[H:])
    ye = left_dot(lm[0], u)
    yo = left_dot(lm[1], v)

    def cols(y):
        r, i = y[:H], y[H:]
        return (
            cat1(r[:, :H] + r[:, H:], i[:, :H] + i[:, H:]),
            cat1(r[:, :H] - r[:, H:], i[:, :H] - i[:, H:]),
        )

    ue, ve = cols(ye)
    uo, vo = cols(yo)
    return right_dot(cat0(ue, uo), rm[0]), right_dot(cat0(ve, vo), rm[1])


def idft(pe, po, lm, rm):
    e = right_dot(pe, rm[2])
    o = right_dot(po, rm[3])
    lt, rt = e + o, e - o
    re = cat1(lt[:, :H], rt[:, :H])
    im = cat1(lt[:, H:], rt[:, H:])
    a = left_dot(lm[2], cat0(re[:H], im[:H]))
    b = left_dot(lm[3], cat0(re[H:], im[H:]))
    t, w = a + b, a - b
    return cat0(t[:H], w[:H]), cat0(t[H:], w[H:])


def times_kernel(p, kr, ki, sign):
    r, i = p[:, :H], p[:, H:]
    if sign > 0:
        return cat1(r * kr - i * ki, r * ki + i * kr)
    return cat1(r * kr + i * ki, i * kr - r * ki)


def chain_body(meta, probe_in, lm, rm, kr, ki, target, own, k1, k2, k3, g1, g2, g3,
               pieces, probe_out, w, hist, psi, out, in_sem, out_sem):
    hubx, plane, active = meta[0], meta[1], meta[2]

    def propagate(re, im, sign):
        pe, po = dft(re, im, lm, rm)
        return idft(times_kernel(pe, kr[0], ki[0], sign), times_kernel(po, kr[1], ki[1], sign), lm, rm)

    @pl.when(active == 1)
    def _():
        sources = [(0, own, None), (1, k1, g1), (2, k2, g2), (3, k3, g3)]
        copies = []
        for d, keep, got in sources:
            x = lax.rem(hubx + d, 4)
            for which in range(2):
                s = 4 * x + 2 * (plane if which == 0 else 1 - plane)
                src = keep.at[which] if d == 0 else (keep if which == 0 else got)
                c = pltpu.make_async_copy(src, w.at[pl.ds(s, 2)], in_sem.at[2 * d + which])
                c.start()
                copies.append(c)
        for c in copies:
            c.wait()
        psi[...] = probe_in[...]

        def chi_of(s):
            wr, wi, pr, pi = w[s, 0], w[s, 1], psi[0], psi[1]
            return wr * pr - wi * pi, wr * pi + wi * pr

        def forward(s, c):
            hist[s] = psi[...]
            re, im = chi_of(s)
            re, im = propagate(re, im, 1)
            psi[0] = re
            psi[1] = im
            return c

        lax.fori_loop(0, 15, forward, 0)
        re, im = chi_of(15)
        pe, po = dft(re, im, lm, rm)

        def detect(p, m):
            r, i = p[:, :H], p[:, H:]
            f = r * r + i * i - m
            return cat1(r * f, i * f)

        re, im = idft(detect(pe, target[0]), detect(po, target[1]), lm, rm)

        def emit(s, gr, gi, pr, pi):
            out[s, 0] = pr * gr + pi * gi
            out[s, 1] = pr * gi - pi * gr
            wr, wi = w[s, 0], w[s, 1]
            return wr * gr + wi * gi, wr * gi - wi * gr

        nr, ni = emit(15, re, im, psi[0], psi[1])
        psi[0] = nr
        psi[1] = ni

        def backward(q, c):
            s = 14 - q
            re, im = propagate(psi[0], psi[1], -1)
            nr, ni = emit(s, re, im, hist[s, 0], hist[s, 1])
            psi[0] = nr
            psi[1] = ni
            return c

        lax.fori_loop(0, 15, backward, 0)
        probe_out[...] = psi[...]
        outs = []
        for d in range(4):
            x = lax.rem(hubx + d, 4)
            for which in range(2):
                s = 4 * x + 2 * (plane if which == 0 else 1 - plane)
                c = pltpu.make_async_copy(
                    out.at[pl.ds(s, 2)], pieces.at[d, which], out_sem.at[2 * d + which]
                )
                c.start()
                outs.append(c)
        for c in outs:
            c.wait()

    @pl.when(active == 0)
    def _():
        probe_out[...] = jnp.zeros_like(probe_out)


def run_chain(meta, probe_in, lm, rm, kr, ki, target, own, k1, k2, k3, g1, g2, g3):
    vm = pl.BlockSpec(memory_space=pltpu.VMEM)
    hbm = pl.BlockSpec(memory_space=pl.ANY)
    return pl.pallas_call(
        chain_body,
        out_shape=(
            jax.ShapeDtypeStruct((4, 2, 2, 2, N, N), F32),
            jax.ShapeDtypeStruct((2, N, N), F32),
        ),
        in_specs=[pl.BlockSpec(memory_space=pltpu.SMEM)] + [vm] * 6 + [hbm] * 7,
        out_specs=(hbm, vm),
        scratch_shapes=[
            pltpu.VMEM((16, 2, N, N), F32),
            pltpu.VMEM((15, 2, N, N), F32),
            pltpu.VMEM((2, N, N), F32),
            pltpu.VMEM((16, 2, N, N), F32),
            pltpu.SemaphoreType.DMA((8,)),
            pltpu.SemaphoreType.DMA((8,)),
        ],
        compiler_params=pltpu.CompilerParams(vmem_limit_bytes=56 * 1024 * 1024),
    )(meta, probe_in, lm, rm, kr, ki, target, own, k1, k2, k3, g1, g2, g3)


def spectral(x):
    return x.reshape(H, 2, H, 2).transpose(3, 1, 0, 2).reshape(2, N, H)


def shards(positions, probe, prop_phase, transmission, measured):
    scan_count = lax.axis_size("scan")
    cut_count = lax.axis_size("cuts")
    scan = lax.axis_index("scan")
    cut = lax.axis_index("cuts")
    core = scan % 2
    x, z = cut // 2, cut % 2
    hubx = jnp.where(core == 0, 0, 2)
    is_hub = x == hubx

    def send(value, route, where=lambda t, c: True):
        pairs = []
        for t in range(scan_count):
            for c in range(cut_count):
                if where(t, c):
                    tt, cc = route(t, c)
                    pairs.append((t * cut_count + c, (tt % scan_count) * cut_count + cc))
        return lax.ppermute(value, AXES, pairs)

    def hub_of(t):
        return 0 if t % 2 == 0 else 2

    def to_hub(value, d):
        return send(
            value,
            lambda t, c: (t, 2 * hub_of(t) + c % 2),
            lambda t, c: c // 2 == (hub_of(t) + d) % 4,
        )

    def from_hub(value, d):
        return send(
            value,
            lambda t, c: (t, 2 * ((hub_of(t) + d) % 4) + c % 2),
            lambda t, c: c // 2 == hub_of(t),
        )

    def swap_planes(value):
        return send(value, lambda t, c: (t, c ^ 1))

    def next_tile(value):
        return send(value, lambda t, c: (t + 1, c))

    def previous_tile(value):
        return send(value, lambda t, c: (t - 1, c))

    first_is_a = (positions[0, 0] == N - 1) & (positions[1, 1] == 768)
    a_index = jnp.where(first_is_a, 0, 1)
    b_index = 1 - a_index
    left_own = positions[a_index, 1]
    top_b = positions[b_index, 0]

    field = transmission.transpose(1, 0, 2, 3)
    last_row = field[:, :, N - 1 :, :]
    packed = jnp.concatenate(
        [last_row.reshape(-1), jnp.full((128,), left_own.astype(F32))]
    )
    packed_prev = next_tile(packed)
    row_prev = packed_prev[:4096].reshape(2, 2, 1, 1024)
    left_a = packed_prev[4096].astype(jnp.int32)
    target_a = send(
        measured[a_index], lambda t, c: (t + 1, c), lambda t, c: c == 2 * hub_of(t + 1)
    )
    rim = previous_tile(field[:, :, :, 768:])

    rows = lax.broadcasted_iota(jnp.int32, (N, N), 0)
    columns = lax.broadcasted_iota(jnp.int32, (N, N), 1)

    block_a = left_a // N
    shift_a = left_a % N
    block_a2 = jnp.minimum(block_a + 1, 3)

    def pick(array):
        size = array.shape[:3] + (N,)
        one = lax.dynamic_slice(array, (0, 0, 0, block_a * N), size)
        two = lax.dynamic_slice(array, (0, 0, 0, block_a2 * N), size)
        return jnp.where(columns[: size[2]] >= shift_a, one, two)

    window_a = jnp.where(rows == N - 1, pick(row_prev), pick(field))
    window_b = jnp.where(rows >= top_b, field[:, :, :, 768:], rim)
    keep = jnp.where(z == 0, window_a, window_b)
    give = jnp.where(z == 0, window_b, window_a)
    k = [to_hub(keep, d) for d in (1, 2, 3)]
    got = swap_planes(give)
    g = [to_hub(got, d) for d in (1, 2, 3)]

    roll_row = jnp.where(z == 0, N - 1, top_b)
    roll_col = jnp.where(z == 0, shift_a, 0)
    probe_in = jnp.roll(probe, (roll_row, roll_col), (1, 2))
    phase = spectral(prop_phase)
    target = spectral(jnp.where(z == 0, target_a, measured[b_index]))
    left, right = dft_constants()
    meta = jnp.stack([hubx, z, is_hub.astype(jnp.int32)]).astype(jnp.int32)
    pieces, probe_part = run_chain(
        meta, probe_in, jnp.asarray(left), jnp.asarray(right), jnp.cos(phase), jnp.sin(phase),
        target, jnp.stack([keep, got]), *k, *g,
    )
    probe_part = jnp.roll(probe_part, (-roll_row, -roll_col), (1, 2))

    spread = lax.all_to_all(probe_part, "cuts", 1, 1, tiled=True)
    own_rows = N // cut_count
    total = jnp.sum(spread.reshape(2, cut_count, own_rows, N), axis=1)
    total = total + send(total, lambda t, c: (t ^ 1, c))
    for stride in (2, 8):
        base = [
            send(
                total,
                lambda t, c: (t - (t // stride % 4) * stride + ((t // stride % 4 + turn) % 4) * stride, c),
            )
            for turn in (1, 2, 3)
        ]
        total = total + base[0] + base[1] + base[2]
    probe_grad = total

    back = [from_hub(pieces[d], d) for d in (1, 2, 3)]
    mine = jnp.where(is_hub, pieces[0], 0.0) + back[0] + back[1] + back[2]
    kept = mine[0]
    swapped = swap_planes(mine[1])
    grad_a = jnp.where(z == 0, kept, swapped)
    grad_b = jnp.where(z == 0, swapped, kept)
    low_b = next_tile(jnp.where(rows < top_b, grad_b, 0.0))
    top_row = previous_tile(grad_a[:, :, N - 1 :, :])

    block_own = left_own // N
    shift_own = left_own % N

    def place(value, block, shift, index):
        cols = columns[: value.shape[2]]
        return jnp.where((block == index) & (cols >= shift), value, 0.0) + jnp.where(
            (block + 1 == index) & (cols < shift), value, 0.0
        )

    parts = []
    for index in range(4):
        part = jnp.where(rows < N - 1, place(grad_a, block_a, shift_a, index), 0.0)
        extra = jnp.broadcast_to(place(top_row, block_own, shift_own, index), part.shape)
        part = part + jnp.where(rows == N - 1, extra, 0.0)
        if index == 3:
            part = part + jnp.where(rows >= top_b, grad_b, 0.0) + low_b
        parts.append(part)
    object_grad = jnp.concatenate(parts, axis=3).transpose(1, 0, 2, 3)
    return object_grad, probe_grad


def solution(mesh):
    in_specs = (P("scan", None), P(), P(), P(None, "cuts", "scan", None), P("scan", None, None))
    out_specs = (P(None, "cuts", "scan", None), P(None, "cuts", None))
    return jax.shard_map(shards, mesh=mesh, in_specs=in_specs, out_specs=out_specs, check_vma=False)
```

time: 1390 us -> 337 us (0.24)
  waiting for transfers between devices: 1040 us -> 107 us
  starting transfers between devices: 129 us -> 47.4 us
  Pallas kernels: 0 us -> 54.5 us
  matrix products: 40.3 us -> 0 us
  loops' own time: 34.6 us -> 0 us
  other arithmetic: 30.1 us -> 16.2 us
    psum x2 -> x0, waiting for transfers between devices: 471 us -> none  [the longest x1 392 us: shards(): summed = lax.psum(probe_part, 'scan')]
    ppermute x20 -> x23, waiting for transfers between devices: 565 us -> 102 us  [send(): return lax.ppermute(value, AXES, pairs)]
    ppermute x20 -> x23, starting transfers between devices: 128 us -> 42.2 us  [send(): return lax.ppermute(value, AXES, pairs)]
    pallas_call x0 -> x1, Pallas kernels: none -> 54.5 us  [run_chain(): pl.pallas_call(chain_body, out_shape=(jax.ShapeDtypeStruct((4, 2, 2, 2, N...]
    dot_general x64 -> x0, matrix products: 40.3 us -> none  [matmul(): jnp.dot(left_op, right_op, precision=accurate, preferred_element_type=jnp...]
    another operation x24 -> x0, loops' own time: 34.6 us -> none  [the longest x9 13.8 us: backward_step(): lax.cond(active, backward_work, lambda current: current, (outgoing, gradi...]
    sin x0 -> x3, local copies, waits for them, and re-layouts: none -> 29.7 us  [shards(): jnp.sin(phase)]
    cos x0 -> x2, local copies, waits for them, and re-layouts: none -> 28.7 us  [shards(): jnp.cos(phase)]
  transfers between devices with their start and end apart: 22 -> 24, of which waited for: 21 -> 13; matrix products, arithmetic and copies ran while one was open for 0% -> 30% of each run, Pallas kernels for 0% -> 0%
where the time goes in v1:
time: 337 us; the launch traced here: 335 us
  waiting for transfers between devices  107 us (32%)
  local copies, waits for them, and re-layouts  103 us (31%)
  Pallas kernels  54.5 us (16%)
  starting transfers between devices  47.4 us (14%)
  other arithmetic  16.2 us (5%)
  between operations  7.03 us (2%)
    ppermute x23, waiting for transfers between devices, send(): return lax.ppermute(value, AXES, pairs)  102 us
    pallas_call x1, Pallas kernels, run_chain(): pl.pallas_call(chain_body, out_shape=(jax.ShapeDtypeStruct((4, 2, 2, 2, N...  54.5 us
    ppermute x23, starting transfers between devices, send(): return lax.ppermute(value, AXES, pairs)  42.2 us
    sin x3, local copies, waits for them, and re-layouts, shards(): jnp.sin(phase)  29.7 us
    cos x2, local copies, waits for them, and re-layouts, shards(): jnp.cos(phase)  28.7 us
    reshape x1, local copies, waits for them, and re-layouts, spectral(): return x.reshape(H, 2, H, 2).transpose(3, 1, 0, 2).reshape(2, N, H)  18.1 us
    transpose x1, local copies, waits for them, and re-layouts, spectral(): return x.reshape(H, 2, H, 2).transpose(3, 1, 0, 2).reshape(2, N, H)  10.6 us
  transfers between devices with their start and end apart: 24, of which 13 were waited for; matrix products, arithmetic and copies ran while one was open for 30% of the time, Pallas kernels for 0%

profile of v1, /device:TPU:32, one launch (start us, length us, event | category | flops | bytes accessed | tf_op | source)
XLA Modules:
  0.0 335.4 jit_solution(5342766567638032495)
XLA Ops:
  0.6 2.5 copy.53
  3.3 7.4 %collective-permute-start.2 = (f32[2,2,256,256]{3,2,1,0:T(8,128)S(1)}, f32[2,2,256,256]{3,2,1,0:T(8,128)S(1)}, u32[]{:S(2)}, u32[]{:S(2)}) collective-permute-start(f32[2,2,256,256]{3,2,1,0:T(8,128)S(1)} %slice.61), channel_id=1, source_target_pairs={{0,248},{1,249},{2,250},{3,251},{4,252},{5,253},{6,254},{7,255},{8... | collective-permute-start | bytes 3145736 | tf_op jit(solution)/shard_map/ppermute | solution.py:236
  14.6 6.8 %collective-permute-done = f32[4224]{0:T(1024)S(1)} collective-permute-done((f32[4224]{0:T(1024)S(1)}, f32[4224]{0:T(1024)S(1)}, u32[]{:S(2)}, u32[]{:S(2)}) %collective-permute-start) | collective-permute-done | bytes 16928 | tf_op jit(solution)/shard_map/ppermute | solution.py:236
  22.6 9.6 %collective-permute-done.2 = f32[2,2,256,256]{3,2,1,0:T(8,128)S(1)} collective-permute-done((f32[2,2,256,256]{3,2,1,0:T(8,128)S(1)}, f32[2,2,256,256]{3,2,1,0:T(8,128)S(1)}, u32[]{:S(2)}, u32[]{:S(2)}) %collective-permute-start.2) | collective-permute-done | bytes 1048608 | tf_op jit(solution)/shard_map/ppermute | solution.py:236
  32.2 2.2 broadcast_select_fusion.3
  34.4 3.1 collective-permute-start.3
  37.5 1.3 collective-permute-start.4
  39.6 1.3 collective-permute-start.5
  40.9 1.3 collective-permute-start.6
  42.2 17.1 %collective-permute-done.3 = f32[2,2,256,256]{3,2,1,0:T(8,128)} collective-permute-done((f32[2,2,256,256]{3,2,1,0:T(8,128)S(1)}, f32[2,2,256,256]{3,2,1,0:T(8,128)}, u32[]{:S(2)}, u32[]{:S(2)}) %collective-permute-start.3) | collective-permute-done | bytes 1048608 | tf_op jit(solution)/shard_map/ppermute | solution.py:236
  59.2 1.3 collective-permute-start.7
  60.6 1.3 collective-permute-start.8
  61.9 1.3 collective-permute-start.9
  63.9 1.0 fusion.25
  64.9 18.1 %cos.10 = f32[128,2,128,2]{3,2,1,0:T(8,128)} reshape(f32[256,256]{1,0:T(8,128)S(1)} %get-tuple-element.28) | data formatting | bytes 524288 | tf_op jit(solution)/shard_map/cos | solution.py:312
  82.9 10.6 %copy.31 = f32[2,2,128,128]{3,2,1,0:T(8,128)} copy(f32[2,2,128,128]{0,3,1,2:T(8,128)} %bitcast.83) | data formatting | bytes 524288 | tf_op jit(solution)/shard_map/cos | solution.py:312
  93.6 18.1 %sin.10 = f32[128,2,128,2]{3,2,1,0:T(8,128)} reshape(f32[256,256]{1,0:T(8,128)S(1)} %get-tuple-element.27) | data formatting | bytes 524288 | tf_op jit(solution)/shard_map/sin | solution.py:312
  111.6 10.7 %copy.32 = f32[2,2,128,128]{3,2,1,0:T(8,128)} copy(f32[2,2,128,128]{0,3,1,2:T(8,128)} %bitcast.84) | data formatting | bytes 524288 | tf_op jit(solution)/shard_map/sin | solution.py:312
  123.1 1.2 fusion.6.probe_in
  124.4 18.1 %reshape.71 = f32[128,2,128,2]{3,2,1,0:T(8,128)} reshape(f32[256,256]{1,0:T(8,128)S(1)} %bitcast_select_fusion.1) | data formatting | bytes 524288 | tf_op jit(solution)/shard_map/reshape | solution.py:216
  142.4 10.6 %copy.33 = f32[2,2,128,128]{3,2,1,0:T(8,128)} copy(f32[2,2,128,128]{0,3,1,2:T(8,128)} %bitcast.85) | data formatting | bytes 524288 | tf_op jit(solution)/shard_map/transpose | solution.py:216
  153.1 2.7 pad_maximum_fusion.own
  155.8 54.5 %shard_map.86 = (f32[4,2,2,2,256,256]{5,4,3,2,1,0:T(8,128)}, f32[2,256,256]{2,1,0:T(8,128)}) custom-call(s32[3]{0:T(128)} %pad_add_fusion.meta, f32[2,256,256]{2,1,0:T(8,128)} %fusion.6.probe_in, bf16[4,256,768]{2,1,0:T(8,128)(2,1)} %constant.114.clone.lm, bf16[4,768,256]{2,1,0:T(8,128)(2,1)} %constant.115.clone.rm, f32[2,256,128]{2,1,0:T(8,128)} %bitcast.90, ...), custom_call_target="tpu_custom_call" | custom-call | tf_op jit(solution)/shard_map/pallas_call | solution.py:195
  210.3 5.7 %slice_bitcast_fusion.2 = (f32[2,2,2,256,256]{4,3,2,1,0:T(8,128)}, f32[2,2,2,256,256]{4,3,2,1,0:T(8,128)}, f32[2,2,2,256,256]{4,3,2,1,0:T(8,128)}) fusion(f32[4,2,2,2,256,256]{5,4,3,2,1,0:T(8,128)} %get-tuple-element.5), kind=kLoop, calls=%fused_computation.7 | loop fusion | bytes 12582912 | tf_op jit(solution)/shard_map/squeeze | solution.py:332
  216.0 1.4 collective-permute-start.12
  217.5 2.6 collective-permute-start.11
  220.1 2.7 collective-permute-start.10
  222.9 18.2 %collective-permute-done.12 = f32[2,2,2,256,256]{4,3,2,1,0:T(8,128)S(1)} collective-permute-done((f32[2,2,2,256,256]{4,3,2,1,0:T(8,128)}, f32[2,2,2,256,256]{4,3,2,1,0:T(8,128)S(1)}, u32[]{:S(2)}, u32[]{:S(2)}) %collective-permute-start.12) | collective-permute-done | bytes 2097184 | tf_op jit(solution)/shard_map/ppermute | solution.py:236
  241.2 1.4 collective-permute-done.11
  242.6 22.5 %collective-permute-done.10 = f32[2,2,2,256,256]{4,3,2,1,0:T(8,128)} collective-permute-done((f32[2,2,2,256,256]{4,3,2,1,0:T(8,128)}, f32[2,2,2,256,256]{4,3,2,1,0:T(8,128)}, u32[]{:S(2)}, u32[]{:S(2)}) %collective-permute-start.10) | collective-permute-done | bytes 2097184 | tf_op jit(solution)/shard_map/ppermute | solution.py:236
  265.1 4.1 %fusion.1 = f32[2,2,2,256,256]{4,3,2,1,0:T(8,128)S(1)} fusion(f32[2,2,2,256,256]{4,3,2,1,0:T(8,128)} %copy-done.1, f32[2,2,2,256,256]{4,3,2,1,0:T(8,128)} %collective-permute-done.11, f32[2,2,2,256,256]{4,3,2,1,0:T(8,128)} %collective-permute-done.10, f32[4,2,2,2,256,256]{5,4,3,2,1,0:T(8,128)} %get-tuple-element.5, pred[]{:T(512)S(6)} %eq.100), kind=kLoop, calls=%fused_computation.4 | loop fusion | flops 2097152 | bytes 10485761 | tf_op jit(solution)/shard_map/add | solution.py:333
  269.2 1.0 slice_bitcast_fusion.3
  270.2 5.5 %collective-permute-start.13 = (f32[2,2,256,256]{3,2,1,0:T(8,128)}, f32[2,2,256,256]{3,2,1,0:T(8,128)S(1)}, u32[]{:S(2)}, u32[]{:S(2)}) collective-permute-start(f32[2,2,256,256]{3,2,1,0:T(8,128)} %slice_bitcast_fusion.3), channel_id=1, source_target_pairs={{0,1},{1,0},{2,3},{3,2},{4,5},{5,4},{6,7},{7,6},{8,9},{9,8},{10,11... | collective-permute-start | bytes 3145736 | tf_op jit(solution)/shard_map/ppermute | solution.py:236
  276.0 1.2 copy.36
  277.3 5.2 %all-to-all-start = ((f32[2,256,256]{2,0,1:T(2,128)}), f32[2,256,256]{2,0,1:T(2,128)}, u32[]{:S(2)}, u32[]{:S(2)}) async-start(f32[2,256,256]{2,0,1:T(2,128)} %copy.36), calls=%async_computation | async-start | bytes 1048576 | tf_op jit(solution)/shard_map/all_to_all | solution.py:317
  285.8 5.8 %all-to-all-done = f32[2,256,256]{2,0,1:T(2,128)} async-done(((f32[2,256,256]{2,0,1:T(2,128)}), f32[2,256,256]{2,0,1:T(2,128)}, u32[]{:S(2)}, u32[]{:S(2)}) %all-to-all-start) | async-done | bytes 524320 | tf_op jit(solution)/shard_map/all_to_all | solution.py:317
  291.6 1.2 reduce_sum.9
  292.9 1.2 collective-permute-done.16
  294.2 1.3 collective-permute-start.19
  295.7 2.8 collective-permute-start.17
  298.8 2.3 collective-permute-done.19
  301.2 3.0 collective-permute-done.18
  304.2 3.4 %collective-permute-start.22 = (f32[2,32,256]{2,0,1:T(2,128)S(1)}, f32[2,32,256]{2,0,1:T(2,128)S(1)}, u32[]{:S(2)}, u32[]{:S(2)}) collective-permute-start(f32[2,32,256]{2,0,1:T(2,128)S(1)} %bitcast.93), channel_id=1, source_target_pairs={{0,192},{1,193},{2,194},{3,195},{4,196},{5,197},{6,198},{7,199},{8... | collective-permute-start | bytes 196616 | tf_op jit(solution)/shard_map/ppermute | solution.py:236
  308.0 0.9 collective-permute-start.20
  309.0 1.7 collective-permute-start.14
  310.7 3.6 %collective-permute-done.21 = f32[2,32,256]{2,0,1:T(2,128)S(1)} collective-permute-done((f32[2,32,256]{2,0,1:T(2,128)S(1)}, f32[2,32,256]{2,0,1:T(2,128)S(1)}, u32[]{:S(2)}, u32[]{:S(2)}) %collective-permute-start.21) | collective-permute-done | bytes 65568 | tf_op jit(solution)/shard_map/ppermute | solution.py:236
  316.3 15.4 %collective-permute-done.15 = f32[2,2,256,256]{3,2,1,0:T(8,128)S(1)} collective-permute-done((f32[2,2,256,256]{3,2,1,0:T(8,128)S(1)}, f32[2,2,256,256]{3,2,1,0:T(8,128)S(1)}, u32[]{:S(2)}, u32[]{:S(2)}) %collective-permute-start.15) | collective-permute-done | bytes 1048608 | tf_op jit(solution)/shard_map/ppermute | solution.py:236
  332.8 2.6 copy.37
  (79 shorter events, 9.5 us)
Async XLA Ops:
  3.1 7.5 %copy-start = (f32[2,2,256,1024]{3,2,0,1:T(8,128)}, f32[2,2,256,1024]{3,2,0,1:T(8,128)S(1)}, u32[]{:S(2)}) copy-start(f32[2,2,256,1024]{3,2,0,1:T(8,128)S(1)} %copy.53) | copy-start | bytes 12582916
  3.1 7.5 %copy-start.9 = (s32[2,2]{1,0:T(2,128)S(1)}, s32[2,2]{1,0:T(2,128)}, u32[]{:S(2)}) copy-start(s32[2,2]{1,0:T(2,128)} %param.9) | copy-start | bytes 52
  3.3 28.9 %collective-permute-start.2 = (f32[2,2,256,256]{3,2,1,0:T(8,128)S(1)}, f32[2,2,256,256]{3,2,1,0:T(8,128)S(1)}, u32[]{:S(2)}, u32[]{:S(2)}) collective-permute-start(f32[2,2,256,256]{3,2,1,0:T(8,128)S(1)} %slice.61), channel_id=1, source_target_pairs={{0,248},{1,249},{2,250},{3,251},{4,252},{5,253},{6,254},{7,255},{8... | collective-permute-start | bytes 3145736 | tf_op jit(solution)/shard_map/ppermute | solution.py:236
  13.9 7.5 %collective-permute-start = (f32[4224]{0:T(1024)S(1)}, f32[4224]{0:T(1024)S(1)}, u32[]{:S(2)}, u32[]{:S(2)}) collective-permute-start(f32[4224]{0:T(1024)S(1)} %concatenate.18), channel_id=1, source_target_pairs={{0,8},{1,9},{2,10},{3,11},{4,12},{5,13},{6,14},{7,15},{8,16},{9,17... | collective-permute-start | bytes 50696 | tf_op jit(solution)/shard_map/ppermute | solution.py:236
  32.2 6.6 %copy-start.3 = (f32[2,256,256]{2,1,0:T(8,128)S(1)}, f32[2,256,256]{2,1,0:T(8,128)}, u32[]{:S(2)}) copy-start(f32[2,256,256]{2,1,0:T(8,128)} %param.13) | copy-start | bytes 1572868
  32.2 31.7 %copy-start.6 = (f32[256,256]{1,0:T(8,128)S(1)}, f32[256,256]{1,0:T(8,128)}, u32[]{:S(2)}) copy-start(f32[256,256]{1,0:T(8,128)} %param.11) | copy-start | bytes 786436
  34.4 24.8 %collective-permute-start.3 = (f32[2,2,256,256]{3,2,1,0:T(8,128)S(1)}, f32[2,2,256,256]{3,2,1,0:T(8,128)}, u32[]{:S(2)}, u32[]{:S(2)}) collective-permute-start(f32[2,2,256,256]{3,2,1,0:T(8,128)S(1)} %get-tuple-element.16), channel_id=1, source_target_pairs={{0,1},{1,0},{2,3},{3,2},{4,5},{5,4},{6,7},{7,6},{8,9},{9,8},{10,11... | collective-permute-start | bytes 3145736 | tf_op jit(solution)/shard_map/ppermute | solution.py:236
  37.5 24.3 %collective-permute-start.4 = (f32[2,2,256,256]{3,2,1,0:T(8,128)S(1)}, f32[2,2,256,256]{3,2,1,0:T(8,128)S(1)}, u32[]{:S(2)}, u32[]{:S(2)}) collective-permute-start(f32[2,2,256,256]{3,2,1,0:T(8,128)S(1)} %get-tuple-element.15), channel_id=1, source_target_pairs={{2,0},{3,1},{14,12},{15,13},{18,16},{19,17},{30,28},{31,29},{34,32... | collective-permute-start | bytes 3145736 | tf_op jit(solution)/shard_map/ppermute | solution.py:236
  38.9 21.7 %collective-permute-start.1 = (f32[256,256]{1,0:T(8,128)S(1)}, f32[256,256]{1,0:T(8,128)S(1)}, u32[]{:S(2)}, u32[]{:S(2)}) collective-permute-start(f32[256,256]{1,0:T(8,128)S(1)} %dynamic-slice_bitcast_fusion), channel_id=1, source_target_pairs={{4,12},{8,16},{20,28},{24,32},{36,44},{40,48},{52,60},{56,64},{68,... | collective-permute-start | bytes 786440 | tf_op jit(solution)/shard_map/ppermute | solution.py:236
  39.6 116.2 %collective-permute-start.5 = (f32[2,2,256,256]{3,2,1,0:T(8,128)S(1)}, f32[2,2,256,256]{3,2,1,0:T(8,128)}, u32[]{:S(2)}, u32[]{:S(2)}) collective-permute-start(f32[2,2,256,256]{3,2,1,0:T(8,128)S(1)} %get-tuple-element.15), channel_id=1, source_target_pairs={{4,0},{5,1},{8,12},{9,13},{20,16},{21,17},{24,28},{25,29},{36,32},... | collective-permute-start | bytes 3145736 | tf_op jit(solution)/shard_map/ppermute | solution.py:236
  40.9 114.9 %collective-permute-start.6 = (f32[2,2,256,256]{3,2,1,0:T(8,128)S(1)}, f32[2,2,256,256]{3,2,1,0:T(8,128)}, u32[]{:S(2)}, u32[]{:S(2)}) collective-permute-start(f32[2,2,256,256]{3,2,1,0:T(8,128)S(1)} %get-tuple-element.15), channel_id=1, source_target_pairs={{6,0},{7,1},{10,12},{11,13},{22,16},{23,17},{26,28},{27,29},{38,32... | collective-permute-start | bytes 3145736 | tf_op jit(solution)/shard_map/ppermute | solution.py:236
  59.2 96.6 %collective-permute-start.7 = (f32[2,2,256,256]{3,2,1,0:T(8,128)}, f32[2,2,256,256]{3,2,1,0:T(8,128)}, u32[]{:S(2)}, u32[]{:S(2)}) collective-permute-start(f32[2,2,256,256]{3,2,1,0:T(8,128)} %collective-permute-done.3), channel_id=1, source_target_pairs={{2,0},{3,1},{14,12},{15,13},{18,16},{19,17},{30,28},{31,29},{34,32... | collective-permute-start | bytes 3145736 | tf_op jit(solution)/shard_map/ppermute | solution.py:236
  60.5 3.3 copy-start.7
  60.6 95.3 %collective-permute-start.8 = (f32[2,2,256,256]{3,2,1,0:T(8,128)}, f32[2,2,256,256]{3,2,1,0:T(8,128)}, u32[]{:S(2)}, u32[]{:S(2)}) collective-permute-start(f32[2,2,256,256]{3,2,1,0:T(8,128)} %collective-permute-done.3), channel_id=1, source_target_pairs={{4,0},{5,1},{8,12},{9,13},{20,16},{21,17},{24,28},{25,29},{36,32},... | collective-permute-start | bytes 3145736 | tf_op jit(solution)/shard_map/ppermute | solution.py:236
  61.9 21.1 %copy-start.2 = (f32[2,2,256,256]{3,2,1,0:T(8,128)}, f32[2,2,256,256]{3,2,1,0:T(8,128)S(1)}, u32[]{:S(2)}) copy-start(f32[2,2,256,256]{3,2,1,0:T(8,128)S(1)} %collective-permute-done.4.k1) | copy-start | bytes 3145732
  61.9 93.9 %collective-permute-start.9 = (f32[2,2,256,256]{3,2,1,0:T(8,128)}, f32[2,2,256,256]{3,2,1,0:T(8,128)}, u32[]{:S(2)}, u32[]{:S(2)}) collective-permute-start(f32[2,2,256,256]{3,2,1,0:T(8,128)} %collective-permute-done.3), channel_id=1, source_target_pairs={{6,0},{7,1},{10,12},{11,13},{22,16},{23,17},{26,28},{27,29},{38,32... | collective-permute-start | bytes 3145736 | tf_op jit(solution)/shard_map/ppermute | solution.py:236
  111.6 11.3 %copy-start.4 = (f32[2,256,256]{2,1,0:T(8,128)S(1)}, f32[2,256,256]{2,1,0:T(8,128)}, u32[]{:S(2)}) copy-start(f32[2,256,256]{2,1,0:T(8,128)} %param.10) | copy-start | bytes 1572868
  122.3 2.0 copy-start.8
  210.3 12.5 %copy-start.5 = (f32[2,256,256]{2,1,0:T(8,128)S(1)}, f32[2,256,256]{2,1,0:T(8,128)}, u32[]{:S(2)}) copy-start(f32[2,256,256]{2,1,0:T(8,128)} %get-tuple-element.6) | copy-start | bytes 1572868
  216.0 25.1 %collective-permute-start.12 = (f32[2,2,2,256,256]{4,3,2,1,0:T(8,128)}, f32[2,2,2,256,256]{4,3,2,1,0:T(8,128)S(1)}, u32[]{:S(2)}, u32[]{:S(2)}) collective-permute-start(f32[2,2,2,256,256]{4,3,2,1,0:T(8,128)} %get-tuple-element.18), channel_id=1, source_target_pairs={{0,6},{1,7},{12,10},{13,11},{16,22},{17,23},{28,26},{29,27},{32,38... | collective-permute-start | bytes 6291464 | tf_op jit(solution)/shard_map/ppermute | solution.py:236
  217.5 25.1 %collective-permute-start.11 = (f32[2,2,2,256,256]{4,3,2,1,0:T(8,128)}, f32[2,2,2,256,256]{4,3,2,1,0:T(8,128)}, u32[]{:S(2)}, u32[]{:S(2)}) collective-permute-start(f32[2,2,2,256,256]{4,3,2,1,0:T(8,128)} %get-tuple-element.19), channel_id=1, source_target_pairs={{0,4},{1,5},{12,8},{13,9},{16,20},{17,21},{28,24},{29,25},{32,36},... | collective-permute-start | bytes 6291464 | tf_op jit(solution)/shard_map/ppermute | solution.py:236
  220.1 45.0 %collective-permute-start.10 = (f32[2,2,2,256,256]{4,3,2,1,0:T(8,128)}, f32[2,2,2,256,256]{4,3,2,1,0:T(8,128)}, u32[]{:S(2)}, u32[]{:S(2)}) collective-permute-start(f32[2,2,2,256,256]{4,3,2,1,0:T(8,128)} %get-tuple-element.17), channel_id=1, source_target_pairs={{0,2},{1,3},{12,14},{13,15},{16,18},{17,19},{28,30},{29,31},{32,34... | collective-permute-start | bytes 6291464 | tf_op jit(solution)/shard_map/ppermute | solution.py:236
  241.2 1.4 copy-start.1
  270.2 28.3 %collective-permute-start.13 = (f32[2,2,256,256]{3,2,1,0:T(8,128)}, f32[2,2,256,256]{3,2,1,0:T(8,128)S(1)}, u32[]{:S(2)}, u32[]{:S(2)}) collective-permute-start(f32[2,2,256,256]{3,2,1,0:T(8,128)} %slice_bitcast_fusion.3), channel_id=1, source_target_pairs={{0,1},{1,0},{2,3},{3,2},{4,5},{5,4},{6,7},{7,6},{8,9},{9,8},{10,11... | collective-permute-start | bytes 3145736 | tf_op jit(solution)/shard_map/ppermute | solution.py:236
  277.3 14.3 %all-to-all-start = ((f32[2,256,256]{2,0,1:T(2,128)}), f32[2,256,256]{2,0,1:T(2,128)}, u32[]{:S(2)}, u32[]{:S(2)}) async-start(f32[2,256,256]{2,0,1:T(2,128)} %copy.36), calls=%async_computation | async-start | bytes 1048576 | tf_op jit(solution)/shard_map/all_to_all | solution.py:317
  292.8 1.3 collective-permute-start.16
  294.2 7.0 %collective-permute-start.19 = (f32[2,32,256]{2,0,1:T(2,128)S(1)}, f32[2,32,256]{2,0,1:T(2,128)S(1)}, u32[]{:S(2)}, u32[]{:S(2)}) collective-permute-start(f32[2,32,256]{2,0,1:T(2,128)S(1)} %add.159), channel_id=1, source_target_pairs={{0,48},{1,49},{2,50},{3,51},{4,52},{5,53},{6,54},{7,55},{8,56},{9,... | collective-permute-start | bytes 196616 | tf_op jit(solution)/shard_map/ppermute | solution.py:236
  295.5 8.6 %collective-permute-start.18 = (f32[2,32,256]{2,0,1:T(2,128)S(1)}, f32[2,32,256]{2,0,1:T(2,128)S(1)}, u32[]{:S(2)}, u32[]{:S(2)}) collective-permute-start(f32[2,32,256]{2,0,1:T(2,128)S(1)} %add.159), channel_id=1, source_target_pairs={{0,32},{1,33},{2,34},{3,35},{4,36},{5,37},{6,38},{7,39},{8,40},{9,... | collective-permute-start | bytes 196616 | tf_op jit(solution)/shard_map/ppermute | solution.py:236
  295.7 8.5 %collective-permute-start.17 = (f32[2,32,256]{2,0,1:T(2,128)S(1)}, f32[2,32,256]{2,0,1:T(2,128)S(1)}, u32[]{:S(2)}, u32[]{:S(2)}) collective-permute-start(f32[2,32,256]{2,0,1:T(2,128)S(1)} %add.159), channel_id=1, source_target_pairs={{0,16},{1,17},{2,18},{3,19},{4,20},{5,21},{6,22},{7,23},{8,24},{9,... | collective-permute-start | bytes 196616 | tf_op jit(solution)/shard_map/ppermute | solution.py:236
  298.7 33.0 %collective-permute-start.15 = (f32[2,2,256,256]{3,2,1,0:T(8,128)S(1)}, f32[2,2,256,256]{3,2,1,0:T(8,128)S(1)}, u32[]{:S(2)}, u32[]{:S(2)}) collective-permute-start(f32[2,2,256,256]{3,2,1,0:T(8,128)S(1)} %get-tuple-element.23), channel_id=1, source_target_pairs={{0,8},{1,9},{2,10},{3,11},{4,12},{5,13},{6,14},{7,15},{8,16},{9,17... | collective-permute-start | bytes 3145736 | tf_op jit(solution)/shard_map/ppermute | solution.py:236
  304.2 6.5 %collective-permute-start.22 = (f32[2,32,256]{2,0,1:T(2,128)S(1)}, f32[2,32,256]{2,0,1:T(2,128)S(1)}, u32[]{:S(2)}, u32[]{:S(2)}) collective-permute-start(f32[2,32,256]{2,0,1:T(2,128)S(1)} %bitcast.93), channel_id=1, source_target_pairs={{0,192},{1,193},{2,194},{3,195},{4,196},{5,197},{6,198},{7,199},{8... | collective-permute-start | bytes 196616 | tf_op jit(solution)/shard_map/ppermute | solution.py:236
  307.6 6.7 %collective-permute-start.21 = (f32[2,32,256]{2,0,1:T(2,128)S(1)}, f32[2,32,256]{2,0,1:T(2,128)S(1)}, u32[]{:S(2)}, u32[]{:S(2)}) collective-permute-start(f32[2,32,256]{2,0,1:T(2,128)S(1)} %bitcast.94), channel_id=1, source_target_pairs={{0,128},{1,129},{2,130},{3,131},{4,132},{5,133},{6,134},{7,135},{8... | collective-permute-start | bytes 196616 | tf_op jit(solution)/shard_map/ppermute | solution.py:236
  308.0 6.9 %collective-permute-start.20 = (f32[2,32,256]{2,0,1:T(2,128)S(1)}, f32[2,32,256]{2,0,1:T(2,128)S(1)}, u32[]{:S(2)}, u32[]{:S(2)}) collective-permute-start(f32[2,32,256]{2,0,1:T(2,128)S(1)} %bitcast.95), channel_id=1, source_target_pairs={{0,64},{1,65},{2,66},{3,67},{4,68},{5,69},{6,70},{7,71},{8,72},{9,... | collective-permute-start | bytes 196616 | tf_op jit(solution)/shard_map/ppermute | solution.py:236
  309.0 6.6 %collective-permute-start.14 = (f32[2,2,1,256]{3,2,1,0:T(1,128)S(1)}, f32[2,2,1,256]{3,2,1,0:T(1,128)S(1)}, u32[]{:S(2)}, u32[]{:S(2)}) collective-permute-start(f32[2,2,1,256]{3,2,1,0:T(1,128)S(1)} %slice.64), channel_id=1, source_target_pairs={{0,248},{1,249},{2,250},{3,251},{4,252},{5,253},{6,254},{7,255},{8... | collective-permute-start | bytes 12296 | tf_op jit(solution)/shard_map/ppermute | solution.py:236

commit v2 on v1

v2 whole, which is shorter than its diff:
```python
import math

import jax
import jax.numpy as jnp
import ml_dtypes
import numpy as np
from jax import lax
from jax.experimental import pallas as pl
from jax.experimental.pallas import tpu as pltpu
from jax.sharding import PartitionSpec as P


AXES = ("scan", "cuts")
N = 256
H = 128
BF = jnp.bfloat16
F32 = jnp.float32


def dft_constants():
    k = np.arange(H)[:, None].astype(np.float64)
    j = np.arange(H)[None, :].astype(np.float64)
    even = np.exp(-2j * np.pi * j * k / H) / math.sqrt(N)
    odd = np.exp(-2j * np.pi * j * (2 * k + 1) / N) / math.sqrt(N)

    def real_form(c):
        return np.block([[c.real, -c.imag], [c.imag, c.real]])

    def parts(m):
        hi = m.astype(np.float32).astype(ml_dtypes.bfloat16)
        lo = (m - hi.astype(np.float64)).astype(np.float32).astype(ml_dtypes.bfloat16)
        return hi, lo

    e, o = real_form(even), real_form(odd)
    tables = [parts(m) for m in (e, o, e.T, o.T)]
    order = np.zeros((N, N), np.float32)
    order[np.arange(N), np.concatenate([np.arange(0, N, 2), np.arange(1, N, 2)])] = 1.0
    return np.stack([np.stack(t) for t in tables]), order


def split(x):
    hi = x.astype(BF)
    lo = (x - hi.astype(F32)).astype(BF)
    return hi, lo


def left_dot(mats, index, x):
    hi, lo = split(x)
    m = jnp.concatenate([mats[index, 0], mats[index, 0], mats[index, 1]], axis=1)
    return jnp.dot(m, jnp.concatenate([hi, lo, hi], axis=0), preferred_element_type=F32)


def right_dot(x, mats, index):
    hi, lo = split(x)
    m = jnp.concatenate([mats[index, 0], mats[index, 0], mats[index, 1]], axis=0)
    return jnp.dot(jnp.concatenate([hi, lo, hi], axis=1), m, preferred_element_type=F32)


def cat0(a, b):
    return jnp.concatenate([a, b], axis=0)


def cat1(a, b):
    return jnp.concatenate([a, b], axis=1)


def dft(re, im, mats):
    u = cat0(re[:H] + re[H:], im[:H] + im[H:])
    v = cat0(re[:H] - re[H:], im[:H] - im[H:])
    ye = left_dot(mats, 0, u)
    yo = left_dot(mats, 1, v)

    def cols(y):
        r, i = y[:H], y[H:]
        return (
            cat1(r[:, :H] + r[:, H:], i[:, :H] + i[:, H:]),
            cat1(r[:, :H] - r[:, H:], i[:, :H] - i[:, H:]),
        )

    ue, ve = cols(ye)
    uo, vo = cols(yo)
    return right_dot(cat0(ue, uo), mats, 2), right_dot(cat0(ve, vo), mats, 3)


def idft(pe, po, mats):
    e = right_dot(pe, mats, 0)
    o = right_dot(po, mats, 1)
    lt, rt = e + o, e - o
    re = cat1(lt[:, :H], rt[:, :H])
    im = cat1(lt[:, H:], rt[:, H:])
    a = left_dot(mats, 2, cat0(re[:H], im[:H]))
    b = left_dot(mats, 3, cat0(re[H:], im[H:]))
    t, w = a + b, a - b
    return cat0(t[:H], w[:H]), cat0(t[H:], w[H:])


def times_kernel(p, kr, ki, sign):
    r, i = p[:, :H], p[:, H:]
    if sign > 0:
        return cat1(r * kr - i * ki, r * ki + i * kr)
    return cat1(r * kr + i * ki, i * kr - r * ki)


BLOCK = 4 * N


def chain_body(forward, backward, meta, *refs):
    refs = list(refs)
    fixed = [refs.pop(0) for _ in range(5 if forward and backward else 4)]
    windows = [refs.pop(0) for _ in range(8)]
    old = refs.pop(0) if not forward else None
    if not forward:
        refs = refs[4:]
    wave_out = refs.pop(0)
    past_out = refs.pop(0) if not backward else None
    pieces = [refs.pop(0) for _ in range(4)] if backward else None
    w, hist, psi, out, wave_in, mats, kr, ki, target, in_sem, past_sem, out_sem, fixed_sem = refs
    plane, block, row, col = meta[0], meta[1], meta[2], meta[3]
    active = meta[5] if forward and backward else meta[4]
    slots = [
        4 * b + 2 * s + layer
        for b, s in (
            (block, plane), (block, 1 - plane), (1 - block, plane), (1 - block, 1 - plane)
        )
        for layer in range(2)
    ]

    def propagate(re, im, sign):
        pe, po = dft(re, im, mats)
        pe = times_kernel(pe, kr[:, :H], ki[:, :H], sign)
        po = times_kernel(po, kr[:, H:], ki[:, H:], sign)
        return idft(pe, po, mats)

    def past_copy(s):
        if forward:
            return pltpu.make_async_copy(hist.at[s], past_out.at[s], past_sem.at[s])
        return pltpu.make_async_copy(old.at[s], hist.at[s], past_sem.at[s])

    def wait_window(s):
        pltpu.make_async_copy(windows[0], w.at[s], in_sem.at[s]).wait()

    @pl.when(active == 1)
    def _():
        for i in range(8):
            pltpu.make_async_copy(windows[i], w.at[slots[i]], in_sem.at[slots[i]]).start()
        if not forward:
            for s in range(7, -1, -1):
                past_copy(s).start()
        for i, (source, place) in enumerate(zip(fixed, (wave_in, mats, kr, ki, target))):
            pltpu.make_async_copy(source, place, fixed_sem.at[i]).start()
        for i, (source, place) in enumerate(zip(fixed, (wave_in, mats, kr, ki, target))):
            pltpu.make_async_copy(source, place, fixed_sem.at[i]).wait()
        if forward and not backward:
            for part in range(2):
                psi[part] = pltpu.roll(pltpu.roll(wave_in[part], row, 0), col, 1)
        else:
            psi[...] = wave_in[...]

        def chi_of(s):
            wr, wi, pr, pi = w[s, 0], w[s, 1], psi[0], psi[1]
            return wr * pr - wi * pi, wr * pi + wi * pr

        def step(s, c):
            wait_window(s)
            hist[s] = psi[...]
            re, im = chi_of(s)
            re, im = propagate(re, im, 1)
            psi[0] = re
            psi[1] = im
            return c

        def emit(s, gr, gi):
            pr, pi = hist[s, 0], hist[s, 1]
            out[s, 0] = pr * gr + pi * gi
            out[s, 1] = pr * gi - pi * gr
            wr, wi = w[s, 0], w[s, 1]
            psi[0] = wr * gr + wi * gi
            psi[1] = wr * gi - wi * gr

        def piece_copy(s, i, part):
            span = pl.ds((i % 2 * 2 + part) * N, N)
            return pltpu.make_async_copy(
                out.at[s, part], pieces[i // 2].at[span], out_sem.at[2 * i + part]
            )

        def leave(s):
            for i in range(8):

                @pl.when(s == slots[i])
                def _():
                    for part in range(2):
                        piece_copy(s, i, part).start()

        def step_back(count):
            def run(q, c):
                s = count - 1 - q
                if not forward:
                    wait_window(s)
                    past_copy(s).wait()

                re, im = propagate(psi[0], psi[1], -1)
                emit(s, re, im)
                leave(s)
                return c

            return run

        if forward and not backward:

            def run(s, c):
                step(s, c)
                past_copy(s).start()
                return c

            lax.fori_loop(0, 8, run, 0)
            wave_out[...] = psi[...]
            for s in range(8):
                past_copy(s).wait()
        if forward and backward:
            lax.fori_loop(0, 7, step, 0)
            wait_window(7)
            hist[7] = psi[...]
            re, im = chi_of(7)
            pe, po = dft(re, im, mats)

            def detect(p, m):
                r, i = p[:, :H], p[:, H:]
                f = r * r + i * i - m
                return cat1(r * f, i * f)

            re, im = idft(detect(pe, target[:, :H]), detect(po, target[:, H:]), mats)
            emit(7, re, im)
            leave(7)
            lax.fori_loop(0, 7, step_back(7), 0)
            wave_out[...] = psi[...]
        if backward and not forward:
            lax.fori_loop(0, 8, step_back(8), 0)
            for part in range(2):
                undone = pltpu.roll(psi[part], lax.rem(N - row, N), 0)
                wave_out[part] = pltpu.roll(undone, lax.rem(N - col, N), 1)
        if backward:
            for i in range(8):
                for part in range(2):
                    piece_copy(0, i, part).wait()

    if not forward:

        @pl.when(active == 0)
        def _():
            wave_out[...] = jnp.zeros_like(wave_out)


def run_chain(forward, backward, meta, wave, tables, target, windows, old, pieces):
    vm = pl.BlockSpec(memory_space=pltpu.VMEM)
    hbm = pl.BlockSpec(memory_space=pl.ANY)
    far = pl.BlockSpec(memory_space=pltpu.HBM)
    operands, specs = [meta, wave, *tables], [pl.BlockSpec(memory_space=pltpu.SMEM)] + [hbm] * 4
    if forward and backward:
        operands, specs = operands + [target], specs + [hbm]
    operands, specs = operands + list(windows), specs + [hbm] * 8
    aliases = {}
    if not forward:
        operands, specs = operands + [old, *pieces], specs + [far] * 5
        aliases = {len(operands) - 4 + i: 1 + i for i in range(4)}
    shapes, outs = [jax.ShapeDtypeStruct((2, N, N), F32)], [vm]
    if not backward:
        shapes, outs = shapes + [jax.ShapeDtypeStruct((8, 2, N, N), F32)], outs + [far]
    else:
        shapes += [jax.ShapeDtypeStruct((BLOCK, N), F32)] * 4
        outs = outs + [far] * 4
    return pl.pallas_call(
        lambda *refs: chain_body(forward, backward, *refs),
        out_shape=tuple(shapes),
        in_specs=specs,
        out_specs=tuple(outs),
        input_output_aliases=aliases,
        scratch_shapes=[
            pltpu.VMEM((8, 2, N, N), F32),
            pltpu.VMEM((8, 2, N, N), F32),
            pltpu.VMEM((2, N, N), F32),
            pltpu.VMEM((8, 2, N, N), F32),
            pltpu.VMEM((2, N, N), F32),
            pltpu.VMEM((4, 2, N, N), BF),
            pltpu.VMEM((N, N), F32),
            pltpu.VMEM((N, N), F32),
            pltpu.VMEM((N, N), F32),
            pltpu.SemaphoreType.DMA((8,)),
            pltpu.SemaphoreType.DMA((8,)),
            pltpu.SemaphoreType.DMA((16,)),
            pltpu.SemaphoreType.DMA((5,)),
        ],
        compiler_params=pltpu.CompilerParams(vmem_limit_bytes=22 * 1024 * 1024),
        cost_estimate=pl.CostEstimate(
            flops=10_000_000, bytes_accessed=1024 * 1024, transcendentals=0
        ),
    )(*operands)


def shards(positions, probe, prop_phase, transmission, measured):
    scan_count = lax.axis_size("scan")
    cut_count = lax.axis_size("cuts")
    scan = lax.axis_index("scan")
    cut = lax.axis_index("cuts")
    core = scan % 2
    x, z = cut // 2, cut % 2
    half = x // 2
    hubx = jnp.where(core == 0, 1 + half, 3 * half)
    is_hub = x == hubx

    def send(value, route, where=lambda t, c: True):
        pairs = []
        for t in range(scan_count):
            for c in range(cut_count):
                if where(t, c):
                    tt, cc = route(t, c)
                    pairs.append((t * cut_count + c, (tt % scan_count) * cut_count + cc))
        return lax.ppermute(value, AXES, pairs)

    def hub_of(t, h):
        return 1 + h if t % 2 == 0 else 3 * h

    def beside(t, c):
        return t, c ^ 1

    def along(t, c):
        return t, c ^ 2

    def across(t, c):
        return t, c ^ 3

    def at_hub(t, c):
        return c // 2 == hub_of(t, c // 4)

    def off_hub(t, c):
        return not at_hub(t, c)

    def to_other_half(t, c):
        return t, 2 * hub_of(t, 1 - c // 4) + c % 2

    def next_tile(value):
        return send(value, lambda t, c: (t + 1, c))

    def previous_tile(value):
        return send(value, lambda t, c: (t - 1, c))

    edge = [transmission[:, layer, :, 768:] for layer in range(2)]
    rim = [previous_tile(part) for part in edge]
    positions, edge = lax.optimization_barrier((positions, edge))

    first_is_a = (positions[0, 0] == N - 1) & (positions[1, 1] == 768)
    a_index = jnp.where(first_is_a, 0, 1)
    b_index = 1 - a_index
    left_own = positions[a_index, 1]
    top_b = positions[b_index, 0]

    rows = lax.broadcasted_iota(jnp.int32, (N, N), 0)
    columns = lax.broadcasted_iota(jnp.int32, (N, N), 1)

    packed = jnp.concatenate(
        [transmission[:, :, N - 1, :].reshape(-1), jnp.full((128,), left_own.astype(F32))]
    )
    packed_prev = next_tile(packed)
    row_prev = packed_prev[:4096].reshape(2, 2, 1, 1024)
    left_a = packed_prev[4096].astype(jnp.int32)
    target_a = send(
        measured[a_index], lambda t, c: (t + 1, c), lambda t, c: c == 2 * hub_of(t + 1, 1)
    )

    block_a = left_a // N
    shift_a = left_a % N
    block_a2 = jnp.minimum(block_a + 1, 3)

    def pick(array, layer):
        size = (2, 1, array.shape[2], N)
        one = lax.dynamic_slice(array, (0, layer, 0, block_a * N), size)
        two = lax.dynamic_slice(array, (0, layer, 0, block_a2 * N), size)
        return jnp.where(columns[: size[2]] >= shift_a, one, two)[:, 0]

    window_a = [
        jnp.where(rows == N - 1, pick(row_prev, layer), pick(transmission, layer))
        for layer in range(2)
    ]
    roll_row = jnp.where(z == 0, N - 1, top_b)
    roll_col = jnp.where(z == 0, shift_a, 0)
    mats, order = dft_constants()

    def spectral(value):
        value = jnp.dot(order, value, precision=lax.Precision.HIGHEST)
        return jnp.dot(value, order.T, precision=lax.Precision.HIGHEST)

    phase = spectral(prop_phase)
    target = spectral(jnp.where(z == 0, target_a, measured[b_index]))
    tables = (jnp.asarray(mats), jnp.cos(phase), jnp.sin(phase))
    meta = jnp.stack(
        [z, hubx % 2, roll_row, roll_col, is_hub & (half == 0), is_hub & (half == 1)]
    ).astype(jnp.int32)

    rim[0], window_a, target, tables = lax.optimization_barrier(
        (rim[0], window_a, target, tables)
    )
    windows = [[], [], [], []]
    for layer in range(2):
        window_b = jnp.where(rows >= top_b, edge[layer], rim[layer])
        keep = jnp.where(z == 0, window_a[layer], window_b)
        give = jnp.where(z == 0, window_b, window_a[layer])
        windows[0].append(keep)
        windows[1].append(send(give, beside, at_hub))
        windows[2].append(send(keep, along, off_hub))
        windows[3].append(send(give, across, off_hub))
    windows = sum(windows, [])
    wave, past = run_chain(True, False, meta, probe, tables, None, windows, None, None)
    wave = send(wave, to_other_half, lambda t, c: c < 4 and at_hub(t, c))
    wave, *pieces = run_chain(True, True, meta, wave, tables, target, windows, None, None)
    wave = send(wave, to_other_half, lambda t, c: c >= 4 and at_hub(t, c))
    wave, *pieces = run_chain(False, True, meta, wave, tables, None, windows, past, pieces)

    spread = lax.all_to_all(wave, "cuts", 1, 1, tiled=True)
    own_rows = N // cut_count
    total = jnp.sum(spread.reshape(2, cut_count, own_rows, N), axis=1)
    total = total + send(total, lambda t, c: (t ^ 1, c))
    for stride in (2, 8):

        def turned(t, turn):
            digit = t // stride % 4
            return t + ((digit + turn) % 4 - digit) * stride

        turns = [send(total, lambda t, c: (turned(t, turn), c)) for turn in (1, 2, 3)]
        total = total + turns[0] + turns[1] + turns[2]
    probe_grad = total

    lent = send(pieces[1], beside, at_hub)
    kept_far = send(pieces[2], along, at_hub)
    lent_far = send(pieces[3], across, at_hub)
    kept = jnp.where(is_hub, pieces[0], kept_far).reshape(2, 2, N, N)
    lent = jnp.where(is_hub, lent, lent_far).reshape(2, 2, N, N)
    grad_a = jnp.where(z == 0, kept, lent)
    grad_b = jnp.where(z == 0, lent, kept)
    low_b = next_tile(jnp.where(rows < top_b, grad_b, 0.0))
    top_row = previous_tile(grad_a[:, :, N - 1 :])

    block_own = left_own // N
    shift_own = left_own % N

    def place(value, block, shift, index):
        cols = columns[: value.shape[1]]
        return jnp.where((block == index) & (cols >= shift), value, 0.0) + jnp.where(
            (block + 1 == index) & (cols < shift), value, 0.0
        )

    whole = []
    for layer in range(2):
        parts = []
        for index in range(4):
            part = jnp.where(rows < N - 1, place(grad_a[layer], block_a, shift_a, index), 0.0)
            extra = place(top_row[layer], block_own, shift_own, index)
            part = part + jnp.where(rows == N - 1, extra, 0.0)
            if index == 3:
                part = part + jnp.where(rows >= top_b, grad_b[layer], 0.0) + low_b[layer]
            parts.append(part)
        whole.append(jnp.concatenate(parts, axis=2))
    object_grad = jnp.stack(whole, axis=1)
    return object_grad, probe_grad


def solution(mesh):
    in_specs = (P("scan", None), P(), P(), P(None, "cuts", "scan", None), P("scan", None, None))
    out_specs = (P(None, "cuts", "scan", None), P(None, "cuts", None))
    return jax.shard_map(shards, mesh=mesh, in_specs=in_specs, out_specs=out_specs, check_vma=False)
```

time: 337 us -> 225 us (0.67)
  local copies, waits for them, and re-layouts: 103 us -> 16.4 us
  starting transfers between devices: 47.4 us -> 124 us
  Pallas kernels: 54.5 us -> 2.89 us
  waiting for transfers between devices: 107 us -> 58.9 us
  other arithmetic: 16.2 us -> 9.99 us
  matrix products: 0 us -> 4.47 us
    all_to_all x1, starting transfers between devices: 5.22 us -> 71.3 us  [shards(): spread = lax.all_to_all(wave, 'cuts', 1, 1, tiled=True)]
    pallas_call x1 -> x3, Pallas kernels: 54.5 us -> 2.89 us  [run_chain(): pl.pallas_call(lambda *refs: chain_body(forward, backward, *refs), out_sh...]
    ppermute x23 -> x24, waiting for transfers between devices: 102 us -> 58.1 us  [send(): return lax.ppermute(value, AXES, pairs)]
    sin x3 -> x0, local copies, waits for them, and re-layouts: 29.7 us -> none  [shards(): jnp.sin(phase)]
    cos x2 -> x0, local copies, waits for them, and re-layouts: 28.7 us -> none  [shards(): jnp.cos(phase)]
    reshape x1 -> x0, local copies, waits for them, and re-layouts: 18.1 us -> none  [spectral(): return x.reshape(H, 2, H, 2).transpose(3, 1, 0, 2).reshape(2, N, H)]
    ppermute x23 -> x24, starting transfers between devices: 42.2 us -> 52.9 us  [send(): return lax.ppermute(value, AXES, pairs)]
    transpose x1 -> x0, local copies, waits for them, and re-layouts: 10.6 us -> none  [spectral(): return x.reshape(H, 2, H, 2).transpose(3, 1, 0, 2).reshape(2, N, H)]
  transfers between devices with their start and end apart: 24 -> 25, of which waited for: 13 -> 11; matrix products, arithmetic and copies ran while one was open for 30% -> 6% of each run, Pallas kernels for 0% -> 0%
where the time goes in v2:
time: 225 us; the launch traced here: 223 us
  starting transfers between devices  124 us (55%)
  waiting for transfers between devices  58.9 us (26%)
  local copies, waits for them, and re-layouts  16.4 us (7%)
  other arithmetic  9.99 us (4%)
  between operations  6.71 us (3%)
  matrix products  4.47 us (2%)
  Pallas kernels  2.89 us (1%)
    all_to_all x1, starting transfers between devices, shards(): spread = lax.all_to_all(wave, 'cuts', 1, 1, tiled=True)  71.3 us
    ppermute x24, waiting for transfers between devices, send(): return lax.ppermute(value, AXES, pairs)  58.1 us
    ppermute x24, starting transfers between devices, send(): return lax.ppermute(value, AXES, pairs)  52.9 us
    unnamed x42, local copies, waits for them, and re-layouts  10.9 us
  transfers between devices with their start and end apart: 25, of which 11 were waited for; matrix products, arithmetic and copies ran while one was open for 6% of the time, Pallas kernels for 0%

profile of v2, /device:TPU:32, one launch (start us, length us, event | category | flops | bytes accessed | tf_op | source)
XLA Modules:
  0.0 223.5 jit_solution(5561293545921059343)
XLA Ops:
  0.7 1.4 slice_bitcast_fusion.2
  2.1 7.4 %collective-permute-start.1 = (f32[2,256,256]{2,1,0:T(8,128)S(1)}, f32[2,256,256]{2,1,0:T(8,128)S(1)}, u32[]{:S(2)}, u32[]{:S(2)}) collective-permute-start(f32[2,256,256]{2,1,0:T(8,128)S(1)} %get-tuple-element.29), channel_id=1, source_target_pairs={{0,248},{1,249},{2,250},{3,251},{4,252},{5,253},{6,254},{7,255},{8... | collective-permute-start | bytes 1572872 | tf_op jit(solution)/shard_map/ppermute | solution.py:317
  10.1 0.9 slice.36
  15.4 2.2 fusion.24
  18.2 3.4 %collective-permute-done = f32[4224]{0:T(1024)S(1)} collective-permute-done((f32[4224]{0:T(1024)S(1)}, f32[4224]{0:T(1024)S(1)}, u32[]{:S(2)}, u32[]{:S(2)}) %collective-permute-start) | collective-permute-done | bytes 16928 | tf_op jit(solution)/shard_map/ppermute | solution.py:317
  23.0 1.7 fusion.3
  25.3 1.3 fusion.26.refs_5_
  26.6 0.8 copy-done.17
  27.4 3.6 %collective-permute-done.3 = f32[2,256,256]{2,1,0:T(8,128)} collective-permute-done((f32[2,256,256]{2,1,0:T(8,128)S(1)}, f32[2,256,256]{2,1,0:T(8,128)}, u32[]{:S(2)}, u32[]{:S(2)}) %collective-permute-start.3) | collective-permute-done | bytes 524320 | tf_op jit(solution)/shard_map/ppermute | solution.py:317
  31.0 2.4 %broadcast_select_fusion.7 = (f32[2,256,256]{2,1,0:T(8,128)}, f32[2,256,256]{2,1,0:T(8,128)S(1)}, f32[2,256,256]{2,1,0:T(8,128)S(1)}, f32[2,256,256]{2,1,0:T(8,128)}) fusion(f32[2,256,256]{2,1,0:T(8,128)S(1)} %get-tuple-element.31, pred[]{:T(512)S(6)} %eq.135, f32[2,256,256]{2,1,0:T(8,128)S(1)} %get-tuple-element.32, ...), kind=kLoop, calls=%fused_computation.32 | loop fusion | flops 786432 | bytes 5243137 | tf_op jit(solution)/shard_map/jit(_where)/select_n | solution.py:405
  34.1 7.1 %collective-permute-start.8 = (f32[2,256,256]{2,1,0:T(8,128)}, f32[2,256,256]{2,1,0:T(8,128)S(1)}, u32[]{:S(2)}, u32[]{:S(2)}) collective-permute-start(f32[2,256,256]{2,1,0:T(8,128)} %get-tuple-element.101), channel_id=1, source_target_pairs={{0,3},{1,2},{6,5},{7,4},{10,9},{11,8},{12,15},{13,14},{16,19},{17,... | collective-permute-start | bytes 1572872 | tf_op jit(solution)/shard_map/ppermute | solution.py:317
  41.2 1.5 collective-permute-start.5
  42.7 3.1 %collective-permute-start.6 = (f32[2,256,256]{2,1,0:T(8,128)S(1)}, f32[2,256,256]{2,1,0:T(8,128)}, u32[]{:S(2)}, u32[]{:S(2)}) collective-permute-start(f32[2,256,256]{2,1,0:T(8,128)S(1)} %get-tuple-element.100.refs_5_.refs_6_), channel_id=1, source_target_pairs={{0,2},{1,3},{6,4},{7,5},{10,8},{11,9},{12,14},{13,15},{16,18},{17,... | collective-permute-start | bytes 1572872 | tf_op jit(solution)/shard_map/ppermute | solution.py:317
  45.8 2.1 collective-permute-start.7
  47.9 8.6 %collective-permute-start.9 = (f32[2,256,256]{2,1,0:T(8,128)}, f32[2,256,256]{2,1,0:T(8,128)}, u32[]{:S(2)}, u32[]{:S(2)}) collective-permute-start(f32[2,256,256]{2,1,0:T(8,128)} %get-tuple-element.60), channel_id=1, source_target_pairs={{0,3},{1,2},{6,5},{7,4},{10,9},{11,8},{12,15},{13,14},{16,19},{17,... | collective-permute-start | bytes 1572872 | tf_op jit(solution)/shard_map/ppermute | solution.py:317
  57.2 10.3 %collective-permute-done.7.refs_10_.refs_11_ = f32[2,256,256]{2,1,0:T(8,128)} collective-permute-done((f32[2,256,256]{2,1,0:T(8,128)S(1)}, f32[2,256,256]{2,1,0:T(8,128)}, u32[]{:S(2)}, u32[]{:S(2)}) %collective-permute-start.7) | collective-permute-done | bytes 524320 | tf_op jit(solution)/shard_map/ppermute | solution.py:317
  67.5 0.9 copy-done.2
  68.5 0.9 copy-done.4
  69.4 1.0 copy-done.13
  70.5 0.9 shard_map.104
  71.3 0.7 collective-permute-start.10
  72.1 1.1 shard_map.105
  73.2 0.7 collective-permute-start.11
  73.9 0.9 shard_map.106
  74.8 1.0 copy-done.6
  75.8 1.0 copy-done.8
  76.8 1.0 copy-done.10
  77.8 1.0 copy-done.11
  78.8 1.2 copy.47
  80.0 71.3 %all-to-all-start = ((f32[2,256,256]{2,0,1:T(2,128)}), f32[2,256,256]{2,0,1:T(2,128)S(1)}, u32[]{:S(2)}, u32[]{:S(2)}) async-start(f32[2,256,256]{2,0,1:T(2,128)} %copy.47), calls=%async_computation | async-start | bytes 1048576 | tf_op jit(solution)/shard_map/all_to_all | solution.py:417
  151.3 1.3 collective-permute-start.12
  152.6 1.6 collective-permute-start.13
  154.2 1.3 collective-permute-start.14
  158.5 0.8 all-to-all-done
  159.6 1.2 collective-permute-done.17
  160.9 2.3 %collective-permute-start.18 = (f32[2,32,256]{2,0,1:T(2,128)S(1)}, f32[2,32,256]{2,0,1:T(2,128)S(1)}, u32[]{:S(2)}, u32[]{:S(2)}) collective-permute-start(f32[2,32,256]{2,0,1:T(2,128)S(1)} %add.249), channel_id=1, source_target_pairs={{0,16},{1,17},{2,18},{3,19},{4,20},{5,21},{6,22},{7,23},{8,24},{9,... | collective-permute-start | bytes 196616 | tf_op jit(solution)/shard_map/ppermute | solution.py:317
  163.2 3.1 %collective-permute-start.20 = (f32[2,32,256]{2,0,1:T(2,128)S(1)}, f32[2,32,256]{2,0,1:T(2,128)S(1)}, u32[]{:S(2)}, u32[]{:S(2)}) collective-permute-start(f32[2,32,256]{2,0,1:T(2,128)S(1)} %add.249), channel_id=1, source_target_pairs={{0,48},{1,49},{2,50},{3,51},{4,52},{5,53},{6,54},{7,55},{8,56},{9,... | collective-permute-start | bytes 196616 | tf_op jit(solution)/shard_map/ppermute | solution.py:317
  166.3 2.3 %collective-permute-done.12 = f32[1024,256]{1,0:T(8,128)} collective-permute-done((f32[1024,256]{1,0:T(8,128)}, f32[1024,256]{1,0:T(8,128)}, u32[]{:S(2)}, u32[]{:S(2)}) %collective-permute-start.12) | collective-permute-done | bytes 1048608 | tf_op jit(solution)/shard_map/ppermute | solution.py:317
  168.6 1.8 collective-permute-start.19
  170.4 18.6 %collective-permute-done.14 = f32[1024,256]{1,0:T(8,128)} collective-permute-done((f32[1024,256]{1,0:T(8,128)}, f32[1024,256]{1,0:T(8,128)}, u32[]{:S(2)}, u32[]{:S(2)}) %collective-permute-start.14) | collective-permute-done | bytes 1048608 | tf_op jit(solution)/shard_map/ppermute | solution.py:317
  189.0 1.8 broadcast_select_fusion.4
  191.2 6.0 %collective-permute-start.15 = (f32[2,2,1,256]{3,1,2,0:T(2,128)S(1)}, f32[2,2,1,256]{3,1,2,0:T(2,128)S(1)}, u32[]{:S(2)}, u32[]{:S(2)}) collective-permute-start(f32[2,2,1,256]{3,1,2,0:T(2,128)S(1)} %copy.58), channel_id=1, source_target_pairs={{0,248},{1,249},{2,250},{3,251},{4,252},{5,253},{6,254},{7,255},{8... | collective-permute-start | bytes 12296 | tf_op jit(solution)/shard_map/ppermute | solution.py:317
  197.5 1.9 collective-permute-start.21
  199.9 1.8 collective-permute-done.23
  201.7 1.6 collective-permute-done.22
  203.3 1.0 collective-permute-done.21
  205.0 14.2 %collective-permute-done.16 = f32[2,2,256,256]{3,2,1,0:T(8,128)S(1)} collective-permute-done((f32[2,2,256,256]{3,2,1,0:T(8,128)S(1)}, f32[2,2,256,256]{3,2,1,0:T(8,128)S(1)}, u32[]{:S(2)}, u32[]{:S(2)}) %collective-permute-start.16) | collective-permute-done | bytes 1048608 | tf_op jit(solution)/shard_map/ppermute | solution.py:317
  220.9 2.5 %copy.48 = f32[2,2,256,1024]{3,2,1,0:T(8,128)} copy(f32[2,2,256,1024]{3,2,0,1:T(8,128)S(1)} %pad_maximum_fusion) | data formatting | bytes 8388608
  (93 shorter events, 10.2 us)
Async XLA Ops:
  0.6 14.3 %copy-start = (f32[256,256]{1,0:T(8,128)S(1)}, f32[256,256]{1,0:T(8,128)}, u32[]{:S(2)}) copy-start(f32[256,256]{1,0:T(8,128)} %param.11) | copy-start | bytes 786436
  0.6 14.3 %copy-start.14 = (f32[256,256]{1,0:T(8,128)S(1)}, f32[256,256]{1,0:T(8,128)}, u32[]{:S(2)}) copy-start(f32[256,256]{1,0:T(8,128)} %constant.105.clone) | copy-start | bytes 786436
  0.7 14.7 %copy-start.15 = (f32[256,256]{1,0:T(8,128)S(1)}, f32[256,256]{1,0:T(8,128)}, u32[]{:S(2)}) copy-start(f32[256,256]{1,0:T(8,128)} %constant.106.clone) | copy-start | bytes 786436
  0.7 10.4 %copy-start.18 = (s32[2,2]{1,0:T(2,128)S(1)}, s32[2,2]{1,0:T(2,128)}, u32[]{:S(2)}) copy-start(s32[2,2]{1,0:T(2,128)} %param.9) | copy-start | bytes 52
  0.7 13.5 %copy-start.16 = (f32[2,256,256]{2,1,0:T(8,128)S(1)}, f32[2,256,256]{2,1,0:T(8,128)}, u32[]{:S(2)}) copy-start(f32[2,256,256]{2,1,0:T(8,128)} %param.13) | copy-start | bytes 1572868
  2.1 24.5 %collective-permute-start.1 = (f32[2,256,256]{2,1,0:T(8,128)S(1)}, f32[2,256,256]{2,1,0:T(8,128)S(1)}, u32[]{:S(2)}, u32[]{:S(2)}) collective-permute-start(f32[2,256,256]{2,1,0:T(8,128)S(1)} %get-tuple-element.29), channel_id=1, source_target_pairs={{0,248},{1,249},{2,250},{3,251},{4,252},{5,253},{6,254},{7,255},{8... | collective-permute-start | bytes 1572872 | tf_op jit(solution)/shard_map/ppermute | solution.py:317
  9.5 21.5 %collective-permute-start.3 = (f32[2,256,256]{2,1,0:T(8,128)S(1)}, f32[2,256,256]{2,1,0:T(8,128)}, u32[]{:S(2)}, u32[]{:S(2)}) collective-permute-start(f32[2,256,256]{2,1,0:T(8,128)S(1)} %get-tuple-element.32), channel_id=1, source_target_pairs={{0,248},{1,249},{2,250},{3,251},{4,252},{5,253},{6,254},{7,255},{8... | collective-permute-start | bytes 1572872 | tf_op jit(solution)/shard_map/ppermute | solution.py:317
  14.1 7.5 %collective-permute-start = (f32[4224]{0:T(1024)S(1)}, f32[4224]{0:T(1024)S(1)}, u32[]{:S(2)}, u32[]{:S(2)}) collective-permute-start(f32[4224]{0:T(1024)S(1)} %concatenate.9), channel_id=1, source_target_pairs={{0,8},{1,9},{2,10},{3,11},{4,12},{5,13},{6,14},{7,15},{8,16},{9,17... | collective-permute-start | bytes 50696 | tf_op jit(solution)/shard_map/ppermute | solution.py:317
  14.2 10.5 %collective-permute-start.2 = (f32[256,256]{1,0:T(8,128)S(1)}, f32[256,256]{1,0:T(8,128)S(1)}, u32[]{:S(2)}, u32[]{:S(2)}) collective-permute-start(f32[256,256]{1,0:T(8,128)S(1)} %dynamic-slice_bitcast_fusion), channel_id=1, source_target_pairs={{6,14},{12,20},{22,30},{28,36},{38,46},{44,52},{54,62},{60,68},{70... | collective-permute-start | bytes 786440 | tf_op jit(solution)/shard_map/ppermute | solution.py:317
  26.6 0.8 copy-start.17
  27.4 40.1 %copy-start.1 = (bf16[4,2,256,256]{3,2,1,0:T(8,128)(2,1)S(1)}, bf16[4,2,256,256]{3,2,1,0:T(8,128)(2,1)}, u32[]{:S(2)}) copy-start(bf16[4,2,256,256]{3,2,1,0:T(8,128)(2,1)} %constant.107.clone.refs_2_) | copy-start | bytes 3145732
  33.4 14.4 %collective-permute-start.4 = (f32[2,256,256]{2,1,0:T(8,128)}, f32[2,256,256]{2,1,0:T(8,128)S(1)}, u32[]{:S(2)}, u32[]{:S(2)}) collective-permute-start(f32[2,256,256]{2,1,0:T(8,128)} %get-tuple-element.101), channel_id=1, source_target_pairs={{2,3},{3,2},{4,5},{5,4},{8,9},{9,8},{14,15},{15,14},{18,19},{19,18... | collective-permute-start | bytes 1572872 | tf_op jit(solution)/shard_map/ppermute | solution.py:317
  34.1 33.4 %collective-permute-start.8 = (f32[2,256,256]{2,1,0:T(8,128)}, f32[2,256,256]{2,1,0:T(8,128)S(1)}, u32[]{:S(2)}, u32[]{:S(2)}) collective-permute-start(f32[2,256,256]{2,1,0:T(8,128)} %get-tuple-element.101), channel_id=1, source_target_pairs={{0,3},{1,2},{6,5},{7,4},{10,9},{11,8},{12,15},{13,14},{16,19},{17,... | collective-permute-start | bytes 1572872 | tf_op jit(solution)/shard_map/ppermute | solution.py:317
  41.2 15.9 %collective-permute-start.5 = (f32[2,256,256]{2,1,0:T(8,128)}, f32[2,256,256]{2,1,0:T(8,128)}, u32[]{:S(2)}, u32[]{:S(2)}) collective-permute-start(f32[2,256,256]{2,1,0:T(8,128)} %get-tuple-element.60), channel_id=1, source_target_pairs={{2,3},{3,2},{4,5},{5,4},{8,9},{9,8},{14,15},{15,14},{18,19},{19,18... | collective-permute-start | bytes 1572872 | tf_op jit(solution)/shard_map/ppermute | solution.py:317
  42.7 14.5 %collective-permute-start.6 = (f32[2,256,256]{2,1,0:T(8,128)S(1)}, f32[2,256,256]{2,1,0:T(8,128)}, u32[]{:S(2)}, u32[]{:S(2)}) collective-permute-start(f32[2,256,256]{2,1,0:T(8,128)S(1)} %get-tuple-element.100.refs_5_.refs_6_), channel_id=1, source_target_pairs={{0,2},{1,3},{6,4},{7,5},{10,8},{11,9},{12,14},{13,15},{16,18},{17,... | collective-permute-start | bytes 1572872 | tf_op jit(solution)/shard_map/ppermute | solution.py:317
  45.8 21.7 %collective-permute-start.7 = (f32[2,256,256]{2,1,0:T(8,128)S(1)}, f32[2,256,256]{2,1,0:T(8,128)}, u32[]{:S(2)}, u32[]{:S(2)}) collective-permute-start(f32[2,256,256]{2,1,0:T(8,128)S(1)} %get-tuple-element.61.refs_6_.refs_7_), channel_id=1, source_target_pairs={{0,2},{1,3},{6,4},{7,5},{10,8},{11,9},{12,14},{13,15},{16,18},{17,... | collective-permute-start | bytes 1572872 | tf_op jit(solution)/shard_map/ppermute | solution.py:317
  47.9 19.6 %collective-permute-start.9 = (f32[2,256,256]{2,1,0:T(8,128)}, f32[2,256,256]{2,1,0:T(8,128)}, u32[]{:S(2)}, u32[]{:S(2)}) collective-permute-start(f32[2,256,256]{2,1,0:T(8,128)} %get-tuple-element.60), channel_id=1, source_target_pairs={{0,3},{1,2},{6,5},{7,4},{10,9},{11,8},{12,15},{13,14},{16,19},{17,... | collective-permute-start | bytes 1572872 | tf_op jit(solution)/shard_map/ppermute | solution.py:317
  67.5 1.0 copy-start.2
  68.5 0.9 copy-start.4
  69.4 1.0 copy-start.13
  70.5 1.6 copy-start.3
  70.5 1.6 copy-start.5
  70.5 1.6 copy-start.12
  71.3 0.7 collective-permute-start.10
  73.2 0.7 collective-permute-start.11
  74.8 1.0 copy-start.6
  75.8 1.0 copy-start.8
  76.8 1.0 copy-start.10
  77.8 1.0 copy-start.11
  78.8 73.8 %copy-start.9 = (f32[1024,256]{1,0:T(8,128)S(1)}, f32[1024,256]{1,0:T(8,128)}, u32[]{:S(2)}) copy-start(f32[1024,256]{1,0:T(8,128)} %copy-done.8) | copy-start | bytes 3145732
  78.8 110.2 %copy-start.7 = (f32[1024,256]{1,0:T(8,128)S(1)}, f32[1024,256]{1,0:T(8,128)}, u32[]{:S(2)}) copy-start(f32[1024,256]{1,0:T(8,128)} %copy-done.6) | copy-start | bytes 3145732
  80.0 79.3 %all-to-all-start = ((f32[2,256,256]{2,0,1:T(2,128)}), f32[2,256,256]{2,0,1:T(2,128)S(1)}, u32[]{:S(2)}, u32[]{:S(2)}) async-start(f32[2,256,256]{2,0,1:T(2,128)} %copy.47), calls=%async_computation | async-start | bytes 1048576 | tf_op jit(solution)/shard_map/all_to_all | solution.py:417
  151.3 17.4 %collective-permute-start.12 = (f32[1024,256]{1,0:T(8,128)}, f32[1024,256]{1,0:T(8,128)}, u32[]{:S(2)}, u32[]{:S(2)}) collective-permute-start(f32[1024,256]{1,0:T(8,128)} %copy-done.10), channel_id=1, source_target_pairs={{2,0},{3,1},{4,6},{5,7},{8,10},{9,11},{14,12},{15,13},{18,16},{19,... | collective-permute-start | bytes 3145736 | tf_op jit(solution)/shard_map/ppermute | solution.py:317
  152.6 17.9 %collective-permute-start.13 = (f32[1024,256]{1,0:T(8,128)S(1)}, f32[1024,256]{1,0:T(8,128)}, u32[]{:S(2)}, u32[]{:S(2)}) collective-permute-start(f32[1024,256]{1,0:T(8,128)S(1)} %copy-done.9), channel_id=1, source_target_pairs={{2,3},{3,2},{4,5},{5,4},{8,9},{9,8},{14,15},{15,14},{18,19},{19,18... | collective-permute-start | bytes 3145736 | tf_op jit(solution)/shard_map/ppermute | solution.py:317
  154.2 34.8 %collective-permute-start.14 = (f32[1024,256]{1,0:T(8,128)}, f32[1024,256]{1,0:T(8,128)}, u32[]{:S(2)}, u32[]{:S(2)}) collective-permute-start(f32[1024,256]{1,0:T(8,128)} %copy-done.11), channel_id=1, source_target_pairs={{2,1},{3,0},{4,7},{5,6},{8,11},{9,10},{14,13},{15,12},{18,17},{19,... | collective-permute-start | bytes 3145736 | tf_op jit(solution)/shard_map/ppermute | solution.py:317
  159.5 1.3 collective-permute-start.17
  160.9 36.4 %collective-permute-start.18 = (f32[2,32,256]{2,0,1:T(2,128)S(1)}, f32[2,32,256]{2,0,1:T(2,128)S(1)}, u32[]{:S(2)}, u32[]{:S(2)}) collective-permute-start(f32[2,32,256]{2,0,1:T(2,128)S(1)} %add.249), channel_id=1, source_target_pairs={{0,16},{1,17},{2,18},{3,19},{4,20},{5,21},{6,22},{7,23},{8,24},{9,... | collective-permute-start | bytes 196616 | tf_op jit(solution)/shard_map/ppermute | solution.py:317
  163.2 34.1 %collective-permute-start.20 = (f32[2,32,256]{2,0,1:T(2,128)S(1)}, f32[2,32,256]{2,0,1:T(2,128)S(1)}, u32[]{:S(2)}, u32[]{:S(2)}) collective-permute-start(f32[2,32,256]{2,0,1:T(2,128)S(1)} %add.249), channel_id=1, source_target_pairs={{0,48},{1,49},{2,50},{3,51},{4,52},{5,53},{6,54},{7,55},{8,56},{9,... | collective-permute-start | bytes 196616 | tf_op jit(solution)/shard_map/ppermute | solution.py:317
  168.6 28.7 %collective-permute-start.19 = (f32[2,32,256]{2,0,1:T(2,128)S(1)}, f32[2,32,256]{2,0,1:T(2,128)S(1)}, u32[]{:S(2)}, u32[]{:S(2)}) collective-permute-start(f32[2,32,256]{2,0,1:T(2,128)S(1)} %add.249), channel_id=1, source_target_pairs={{0,32},{1,33},{2,34},{3,35},{4,36},{5,37},{6,38},{7,39},{8,40},{9,... | collective-permute-start | bytes 196616 | tf_op jit(solution)/shard_map/ppermute | solution.py:317
  191.1 28.1 %collective-permute-start.16 = (f32[2,2,256,256]{3,2,1,0:T(8,128)S(1)}, f32[2,2,256,256]{3,2,1,0:T(8,128)S(1)}, u32[]{:S(2)}, u32[]{:S(2)}) collective-permute-start(f32[2,2,256,256]{3,2,1,0:T(8,128)S(1)} %broadcast_select_fusion), channel_id=1, source_target_pairs={{0,8},{1,9},{2,10},{3,11},{4,12},{5,13},{6,14},{7,15},{8,16},{9,17... | collective-permute-start | bytes 3145736 | tf_op jit(solution)/shard_map/ppermute | solution.py:317
  191.2 8.2 %collective-permute-start.15 = (f32[2,2,1,256]{3,1,2,0:T(2,128)S(1)}, f32[2,2,1,256]{3,1,2,0:T(2,128)S(1)}, u32[]{:S(2)}, u32[]{:S(2)}) collective-permute-start(f32[2,2,1,256]{3,1,2,0:T(2,128)S(1)} %copy.58), channel_id=1, source_target_pairs={{0,248},{1,249},{2,250},{3,251},{4,252},{5,253},{6,254},{7,255},{8... | collective-permute-start | bytes 12296 | tf_op jit(solution)/shard_map/ppermute | solution.py:317
  197.3 4.3 %collective-permute-start.23 = (f32[2,32,256]{2,0,1:T(2,128)S(1)}, f32[2,32,256]{2,0,1:T(2,128)S(1)}, u32[]{:S(2)}, u32[]{:S(2)}) collective-permute-start(f32[2,32,256]{2,0,1:T(2,128)S(1)} %bitcast.118), channel_id=1, source_target_pairs={{0,192},{1,193},{2,194},{3,195},{4,196},{5,197},{6,198},{7,199},{8... | collective-permute-start | bytes 196616 | tf_op jit(solution)/shard_map/ppermute | solution.py:317
  197.4 5.9 %collective-permute-start.22 = (f32[2,32,256]{2,0,1:T(2,128)S(1)}, f32[2,32,256]{2,0,1:T(2,128)S(1)}, u32[]{:S(2)}, u32[]{:S(2)}) collective-permute-start(f32[2,32,256]{2,0,1:T(2,128)S(1)} %bitcast.119), channel_id=1, source_target_pairs={{0,128},{1,129},{2,130},{3,131},{4,132},{5,133},{6,134},{7,135},{8... | collective-permute-start | bytes 196616 | tf_op jit(solution)/shard_map/ppermute | solution.py:317
  197.5 6.8 %collective-permute-start.21 = (f32[2,32,256]{2,0,1:T(2,128)S(1)}, f32[2,32,256]{2,0,1:T(2,128)S(1)}, u32[]{:S(2)}, u32[]{:S(2)}) collective-permute-start(f32[2,32,256]{2,0,1:T(2,128)S(1)} %bitcast.120), channel_id=1, source_target_pairs={{0,64},{1,65},{2,66},{3,67},{4,68},{5,69},{6,70},{7,71},{8,72},{9,... | collective-permute-start | bytes 196616 | tf_op jit(solution)/shard_map/ppermute | solution.py:317

commit v3 on v2

--- a/solution.py
+++ b/solution.py
@@ -101,13 +101,10 @@
     return cat1(r * kr + i * ki, i * kr - r * ki)
 
 
-BLOCK = 4 * N
-
-
 def chain_body(forward, backward, meta, *refs):
     refs = list(refs)
     fixed = [refs.pop(0) for _ in range(5 if forward and backward else 4)]
-    windows = [refs.pop(0) for _ in range(8)]
+    windows = [refs.pop(0) for _ in range(4)]
     old = refs.pop(0) if not forward else None
     if not forward:
         refs = refs[4:]
@@ -137,12 +134,14 @@
         return pltpu.make_async_copy(old.at[s], hist.at[s], past_sem.at[s])
 
     def wait_window(s):
-        pltpu.make_async_copy(windows[0], w.at[s], in_sem.at[s]).wait()
+        pltpu.make_async_copy(windows[0].at[:, 0], w.at[s], in_sem.at[s]).wait()
 
     @pl.when(active == 1)
     def _():
         for i in range(8):
-            pltpu.make_async_copy(windows[i], w.at[slots[i]], in_sem.at[slots[i]]).start()
+            pltpu.make_async_copy(
+                windows[i // 2].at[:, i % 2], w.at[slots[i]], in_sem.at[slots[i]]
+            ).start()
         if not forward:
             for s in range(7, -1, -1):
                 past_copy(s).start()
@@ -177,19 +176,15 @@
             psi[0] = wr * gr + wi * gi
             psi[1] = wr * gi - wi * gr
 
-        def piece_copy(s, i, part):
-            span = pl.ds((i % 2 * 2 + part) * N, N)
-            return pltpu.make_async_copy(
-                out.at[s, part], pieces[i // 2].at[span], out_sem.at[2 * i + part]
-            )
+        def piece_copy(s, i):
+            return pltpu.make_async_copy(out.at[s], pieces[i // 2].at[:, i % 2], out_sem.at[i])
 
         def leave(s):
             for i in range(8):
 
                 @pl.when(s == slots[i])
                 def _():
-                    for part in range(2):
-                        piece_copy(s, i, part).start()
+                    piece_copy(s, i).start()
 
         def step_back(count):
             def run(q, c):
@@ -240,14 +235,17 @@
                 wave_out[part] = pltpu.roll(undone, lax.rem(N - col, N), 1)
         if backward:
             for i in range(8):
-                for part in range(2):
-                    piece_copy(0, i, part).wait()
+                piece_copy(0, i).wait()
 
     if not forward:
 
         @pl.when(active == 0)
         def _():
             wave_out[...] = jnp.zeros_like(wave_out)
+
+
+def in_hbm(value):
+    return pltpu.with_memory_space_constraint(value, pltpu.HBM)
 
 
 def run_chain(forward, backward, meta, wave, tables, target, windows, old, pieces):
@@ -257,16 +255,16 @@
     operands, specs = [meta, wave, *tables], [pl.BlockSpec(memory_space=pltpu.SMEM)] + [hbm] * 4
     if forward and backward:
         operands, specs = operands + [target], specs + [hbm]
-    operands, specs = operands + list(windows), specs + [hbm] * 8
+    operands, specs = operands + list(windows), specs + [hbm] * 4
     aliases = {}
     if not forward:
-        operands, specs = operands + [old, *pieces], specs + [far] * 5
+        operands, specs = operands + [old, *map(in_hbm, pieces)], specs + [far] * 5
         aliases = {len(operands) - 4 + i: 1 + i for i in range(4)}
     shapes, outs = [jax.ShapeDtypeStruct((2, N, N), F32)], [vm]
     if not backward:
         shapes, outs = shapes + [jax.ShapeDtypeStruct((8, 2, N, N), F32)], outs + [far]
     else:
-        shapes += [jax.ShapeDtypeStruct((BLOCK, N), F32)] * 4
+        shapes += [pltpu.HBM((2, 2, N, N), F32)] * 4
         outs = outs + [far] * 4
     return pl.pallas_call(
         lambda *refs: chain_body(forward, backward, *refs),
@@ -286,10 +284,10 @@
             pltpu.VMEM((N, N), F32),
             pltpu.SemaphoreType.DMA((8,)),
             pltpu.SemaphoreType.DMA((8,)),
-            pltpu.SemaphoreType.DMA((16,)),
+            pltpu.SemaphoreType.DMA((8,)),
             pltpu.SemaphoreType.DMA((5,)),
         ],
-        compiler_params=pltpu.CompilerParams(vmem_limit_bytes=22 * 1024 * 1024),
+        compiler_params=pltpu.CompilerParams(vmem_limit_bytes=17 * 1024 * 1024),
         cost_estimate=pl.CostEstimate(
             flops=10_000_000, bytes_accessed=1024 * 1024, transcendentals=0
         ),
@@ -343,8 +341,15 @@
     def previous_tile(value):
         return send(value, lambda t, c: (t - 1, c))
 
-    edge = [transmission[:, layer, :, 768:] for layer in range(2)]
-    rim = [previous_tile(part) for part in edge]
+    edge = transmission[:, :, :, 768:]
+    rim_chip = send(edge, lambda t, c: (t - 1, c), lambda t, c: t % 2 == 1)
+    rim_near = send(edge, lambda t, c: (t - 1, c), lambda t, c: t % 2 == 0 and c % 2 == 1)
+    rim_beside = send(
+        edge, lambda t, c: (t - 1, c ^ 1), lambda t, c: t % 2 == 0 and c in (0, 6)
+    )
+    rim_across = send(
+        edge, lambda t, c: (t - 1, c ^ 3), lambda t, c: t % 2 == 0 and c in (2, 4)
+    )
     positions, edge = lax.optimization_barrier((positions, edge))
 
     first_is_a = (positions[0, 0] == N - 1) & (positions[1, 1] == 768)
@@ -357,11 +362,16 @@
     columns = lax.broadcasted_iota(jnp.int32, (N, N), 1)
 
     packed = jnp.concatenate(
-        [transmission[:, :, N - 1, :].reshape(-1), jnp.full((128,), left_own.astype(F32))]
+        [
+            transmission[:, :, N - 1, :].reshape(-1),
+            jnp.full((64,), left_own.astype(F32)),
+            jnp.full((64,), top_b.astype(F32)),
+        ]
     )
     packed_prev = next_tile(packed)
     row_prev = packed_prev[:4096].reshape(2, 2, 1, 1024)
     left_a = packed_prev[4096].astype(jnp.int32)
+    top_prev = packed_prev[4160].astype(jnp.int32)
     target_a = send(
         measured[a_index], lambda t, c: (t + 1, c), lambda t, c: c == 2 * hub_of(t + 1, 1)
     )
@@ -370,16 +380,13 @@
     shift_a = left_a % N
     block_a2 = jnp.minimum(block_a + 1, 3)
 
-    def pick(array, layer):
-        size = (2, 1, array.shape[2], N)
-        one = lax.dynamic_slice(array, (0, layer, 0, block_a * N), size)
-        two = lax.dynamic_slice(array, (0, layer, 0, block_a2 * N), size)
-        return jnp.where(columns[: size[2]] >= shift_a, one, two)[:, 0]
-
-    window_a = [
-        jnp.where(rows == N - 1, pick(row_prev, layer), pick(transmission, layer))
-        for layer in range(2)
-    ]
+    def pick(array):
+        size = (2, 2, array.shape[2], N)
+        one = lax.dynamic_slice(array, (0, 0, 0, block_a * N), size)
+        two = lax.dynamic_slice(array, (0, 0, 0, block_a2 * N), size)
+        return jnp.where(columns[: size[2]] >= shift_a, one, two)
+
+    window_a = jnp.where(rows == N - 1, pick(row_prev), pick(transmission))
     roll_row = jnp.where(z == 0, N - 1, top_b)
     roll_col = jnp.where(z == 0, shift_a, 0)
     mats, order = dft_constants()
@@ -395,19 +402,20 @@
         [z, hubx % 2, roll_row, roll_col, is_hub & (half == 0), is_hub & (half == 1)]
     ).astype(jnp.int32)
 
-    rim[0], window_a, target, tables = lax.optimization_barrier(
-        (rim[0], window_a, target, tables)
-    )
-    windows = [[], [], [], []]
-    for layer in range(2):
-        window_b = jnp.where(rows >= top_b, edge[layer], rim[layer])
-        keep = jnp.where(z == 0, window_a[layer], window_b)
-        give = jnp.where(z == 0, window_b, window_a[layer])
-        windows[0].append(keep)
-        windows[1].append(send(give, beside, at_hub))
-        windows[2].append(send(keep, along, off_hub))
-        windows[3].append(send(give, across, off_hub))
-    windows = sum(windows, [])
+    above = rows >= top_b
+    give = jnp.where(z == 0, jnp.where((core == 1) | above, edge, rim_chip), window_a)
+    beside_hub, across_hub = send(give, beside, at_hub), send(give, across, off_hub)
+    rim_near, give, tables = lax.optimization_barrier((rim_near, give, tables))
+    rim_own = jnp.where(core == 0, rim_chip, rim_near)
+    keep = jnp.where(z == 0, window_a, jnp.where(above, edge, rim_own))
+    along_hub = send(keep, along, off_hub)
+    unmerged = (core == 1) & (z == 1) & jnp.logical_not(above)
+    windows = [
+        keep,
+        jnp.where(unmerged, rim_beside, beside_hub),
+        along_hub,
+        jnp.where(unmerged, rim_across, across_hub),
+    ]
     wave, past = run_chain(True, False, meta, probe, tables, None, windows, None, None)
     wave = send(wave, to_other_half, lambda t, c: c < 4 and at_hub(t, c))
     wave, *pieces = run_chain(True, True, meta, wave, tables, target, windows, None, None)
@@ -417,48 +425,52 @@
     spread = lax.all_to_all(wave, "cuts", 1, 1, tiled=True)
     own_rows = N // cut_count
     total = jnp.sum(spread.reshape(2, cut_count, own_rows, N), axis=1)
-    total = total + send(total, lambda t, c: (t ^ 1, c))
+    total = total.reshape(2 * own_rows, N)
+    total = total + send(total, lambda t, c: (t ^ 1, c), lambda t, c: t % 2 == 1)
     for stride in (2, 8):
 
         def turned(t, turn):
             digit = t // stride % 4
             return t + ((digit + turn) % 4 - digit) * stride
 
-        turns = [send(total, lambda t, c: (turned(t, turn), c)) for turn in (1, 2, 3)]
+        turns = [
+            send(total, lambda t, c: (turned(t, turn), c), lambda t, c: t % 2 == 0)
+            for turn in (1, 2, 3)
+        ]
         total = total + turns[0] + turns[1] + turns[2]
-    probe_grad = total
+    other = send(total, lambda t, c: (t ^ 1, c), lambda t, c: t % 2 == 0)
+    probe_grad = jnp.where(core == 0, total, other).reshape(2, own_rows, N)
 
     lent = send(pieces[1], beside, at_hub)
     kept_far = send(pieces[2], along, at_hub)
     lent_far = send(pieces[3], across, at_hub)
-    kept = jnp.where(is_hub, pieces[0], kept_far).reshape(2, 2, N, N)
-    lent = jnp.where(is_hub, lent, lent_far).reshape(2, 2, N, N)
+
+    kept = jnp.where(is_hub, pieces[0], kept_far)
+    lent = jnp.where(is_hub, lent, lent_far)
     grad_a = jnp.where(z == 0, kept, lent)
     grad_b = jnp.where(z == 0, lent, kept)
-    low_b = next_tile(jnp.where(rows < top_b, grad_b, 0.0))
+    low = next_tile(grad_b)
     top_row = previous_tile(grad_a[:, :, N - 1 :])
 
     block_own = left_own // N
     shift_own = left_own % N
 
     def place(value, block, shift, index):
-        cols = columns[: value.shape[1]]
+        cols = columns[: value.shape[2]]
         return jnp.where((block == index) & (cols >= shift), value, 0.0) + jnp.where(
             (block + 1 == index) & (cols < shift), value, 0.0
         )
 
-    whole = []
-    for layer in range(2):
-        parts = []
-        for index in range(4):
-            part = jnp.where(rows < N - 1, place(grad_a[layer], block_a, shift_a, index), 0.0)
-            extra = place(top_row[layer], block_own, shift_own, index)
-            part = part + jnp.where(rows == N - 1, extra, 0.0)
-            if index == 3:
-                part = part + jnp.where(rows >= top_b, grad_b[layer], 0.0) + low_b[layer]
-            parts.append(part)
-        whole.append(jnp.concatenate(parts, axis=2))
-    object_grad = jnp.stack(whole, axis=1)
+    low_b = jnp.where(rows < top_prev, low, 0.0)
+    parts = []
+    for index in range(4):
+        part = jnp.where(rows < N - 1, place(grad_a, block_a, shift_a, index), 0.0)
+        extra = place(top_row, block_own, shift_own, index)
+        part = part + jnp.where(rows == N - 1, extra, 0.0)
+        if index == 3:
+            part = part + jnp.where(above, grad_b, 0.0) + low_b
+        parts.append(part)
+    object_grad = jnp.concatenate(parts, axis=3)
     return object_grad, probe_grad
 
 

time: 225 us -> 213 us (0.947)
  waiting for transfers between devices: 58.9 us -> 38 us
  other arithmetic: 9.99 us -> 22.6 us
  local copies, waits for them, and re-layouts: 16.4 us -> 9.73 us
    ppermute x24, waiting for transfers between devices: 58.1 us -> 38 us  [send(): return lax.ppermute(value, AXES, pairs)]
    unnamed x42 -> x24, local copies, waits for them, and re-layouts: 10.9 us -> 0.07 us
    select_n x4, other arithmetic: 4.38 us -> 8.39 us  [the longest x1 3.12 us: shards(): jnp.where(z == 0, jnp.where((core == 1) | above, edge, rim_chip), window_a)]
    concatenate x0 -> x1, other arithmetic: none -> 2.66 us  [shards(): object_grad = jnp.concatenate(parts, axis=3)]
    slice x3 -> x2, local copies, waits for them, and re-layouts: 0.65 us -> 2.93 us  [the longest x1 2.33 us: shards(): edge = transmission[:, :, :, 768:]]
  transfers between devices with their start and end apart: 25 -> 25, of which waited for: 11 -> 8; matrix products, arithmetic and copies ran while one was open for 6% -> 14% of each run, Pallas kernels for 0% -> 0%
where the time goes in v3:
time: 213 us; the launch traced here: 212 us
  starting transfers between devices  125 us (59%)
  waiting for transfers between devices  38 us (18%)
  other arithmetic  22.6 us (11%)
  local copies, waits for them, and re-layouts  9.73 us (5%)
  between operations  8.43 us (4%)
  matrix products  5.67 us (3%)
  Pallas kernels  2.67 us (1%)
    all_to_all x1, starting transfers between devices, shards(): spread = lax.all_to_all(wave, 'cuts', 1, 1, tiled=True)  69.7 us
    ppermute x24, starting transfers between devices, send(): return lax.ppermute(value, AXES, pairs)  55.1 us
    ppermute x24, waiting for transfers between devices, send(): return lax.ppermute(value, AXES, pairs)  38 us
  transfers between devices with their start and end apart: 25, of which 8 were waited for; matrix products, arithmetic and copies ran while one was open for 14% of the time, Pallas kernels for 0%

profile of v3, /device:TPU:32, one launch (start us, length us, event | category | flops | bytes accessed | tf_op | source)
XLA Modules:
  0.0 211.8 jit_solution(7463733820769281845)
XLA Ops:
  0.6 2.3 %slice.30 = f32[2,2,256,256]{3,2,1,0:T(8,128)} slice(f32[2,2,256,1024]{3,2,1,0:T(8,128)} %param.12), slice={[0:2], [0:2], [0:256], [768:1024]} | slice | bytes 2097152 | tf_op jit(solution)/shard_map/slice | solution.py:344
  3.0 1.3 collective-permute-start.2
  4.3 1.6 collective-permute-start.3
  5.9 1.6 collective-permute-start.6
  7.6 9.9 %collective-permute-start.1 = (f32[2,2,256,256]{3,2,1,0:T(8,128)}, f32[2,2,256,256]{3,2,1,0:T(8,128)S(1)}, u32[]{:S(2)}, u32[]{:S(2)}) collective-permute-start(f32[2,2,256,256]{3,2,1,0:T(8,128)} %slice.30), channel_id=1, source_target_pairs={{1,249},{3,251},{5,253},{7,255},{17,9},{19,11},{21,13},{23,15},{33... | collective-permute-start | bytes 3145736 | tf_op jit(solution)/shard_map/ppermute | solution.py:315
  17.5 0.9 slice.29
  18.4 1.3 fusion.22
  21.0 1.4 constant_dynamic-slice_fusion.1
  23.8 1.3 fusion.23
  25.2 3.1 %fusion.20 = (f32[256,256]{1,0:T(8,128)}, f32[256,256]{1,0:T(8,128)}) fusion(f32[256,256]{1,0:T(8,128)S(1)} %fusion.23, f32[256,256]{1,0:T(8,128)} %constant.106.clone), kind=kOutput, calls=%fused_computation.69 | convolution fusion | flops 201326592 | bytes 1048576 | tf_op jit(solution)/shard_map/dot_general | solution.py:396
  29.0 2.2 %collective-permute-done = f32[4224]{0:T(1024)S(1)} collective-permute-done((f32[4224]{0:T(1024)S(1)}, f32[4224]{0:T(1024)S(1)}, u32[]{:S(2)}, u32[]{:S(2)}) %collective-permute-start) | collective-permute-done | bytes 16928 | tf_op jit(solution)/shard_map/ppermute | solution.py:315
  32.7 3.1 %select_select_fusion.2 = f32[2,2,256,256]{3,2,1,0:T(8,128)} fusion(f32[2,2,256,256]{3,2,1,0:T(8,128)} %slice.30, f32[2,2,256,256]{3,2,1,0:T(8,128)S(1)} %collective-permute-done.2, pred[256]{0:T(512)(128)(4,1)S(1)} %broadcast_or_fusion, pred[]{:T(512)S(6)} %eq.111, f32[2,2,256,1024]{3,2,1,0:T(8,128)} %param.12, s32[]{:T(128)S(6)} %select_n.244, ...), kind=kLoop, calls=%fused_computation.7 | loop fusion | flops 1048576 | bytes 5247753 | tf_op jit(solution)/shard_map/jit(_where)/select_n | solution.py:406
  35.8 1.6 collective-permute-start.4
  37.4 6.8 %collective-permute-start.7 = (f32[2,2,256,256]{3,2,1,0:T(8,128)}, f32[2,2,256,256]{3,2,1,0:T(8,128)}, u32[]{:S(2)}, u32[]{:S(2)}) collective-permute-start(f32[2,2,256,256]{3,2,1,0:T(8,128)} %select_select_fusion.2), channel_id=1, source_target_pairs={{0,3},{1,2},{6,5},{7,4},{10,9},{11,8},{12,15},{13,14},{16,19},{17,... | collective-permute-start | bytes 3145736 | tf_op jit(solution)/shard_map/ppermute | solution.py:315
  44.9 2.2 %select_select_fusion.refs_5_.refs_6_ = f32[2,2,256,256]{3,2,1,0:T(8,128)S(1)} fusion(f32[2,2,256,256]{3,2,1,0:T(8,128)} %slice.30, f32[2,2,256,256]{3,2,1,0:T(8,128)S(1)} %collective-permute-done.2, f32[2,2,256,256]{3,2,1,0:T(8,128)S(1)} %collective-permute-done.1, pred[256]{0:T(512)(128)(4,1)S(1)} %iota_compare_fusion.5, pred[]{:T(512)S(6)} %eq.112, ...), kind=kLoop, calls=%fused_computation.5 | loop fusion | flops 1310720 | bytes 6296330 | tf_op jit(solution)/shard_map/jit(_where)/select_n | solution.py:410
  47.1 1.5 collective-permute-start.5
  50.0 1.7 dynamic-slice_bitcast_fusion
  51.8 0.8 collective-permute-start.9
  52.7 3.2 %collective-permute-done.7 = f32[2,2,256,256]{3,2,1,0:T(8,128)} collective-permute-done((f32[2,2,256,256]{3,2,1,0:T(8,128)}, f32[2,2,256,256]{3,2,1,0:T(8,128)}, u32[]{:S(2)}, u32[]{:S(2)}) %collective-permute-start.7) | collective-permute-done | bytes 1048608 | tf_op jit(solution)/shard_map/ppermute | solution.py:315
  55.9 2.5 %broadcast_select_fusion = (f32[2,2,256,256]{3,2,1,0:T(8,128)S(1)}, f32[2,2,256,256]{3,2,1,0:T(8,128)S(1)}) fusion(f32[2,2,256,256]{3,2,1,0:T(8,128)} %collective-permute-done.6, f32[2,2,256,256]{3,2,1,0:T(8,128)} %collective-permute-done.7, pred[256]{0:T(512)(128)(4,1)S(1)} %not_and_fusion, f32[2,2,256,256]{3,2,1,0:T(8,128)} %collective-permute-done.3, ...), kind=kLoop, calls=%fused_computation.8 | loop fusion | flops 524288 | bytes 6291712 | tf_op jit(solution)/shard_map/jit(_where)/select_n | solution.py:417
  58.4 8.5 %collective-permute-done.5.refs_7_.refs_8_ = f32[2,2,256,256]{3,2,1,0:T(8,128)S(1)} collective-permute-done((f32[2,2,256,256]{3,2,1,0:T(8,128)S(1)}, f32[2,2,256,256]{3,2,1,0:T(8,128)S(1)}, u32[]{:S(2)}, u32[]{:S(2)}) %collective-permute-start.5) | collective-permute-done | bytes 1048608 | tf_op jit(solution)/shard_map/ppermute | solution.py:315
  66.9 0.8 shard_map.104
  67.8 0.7 collective-permute-start.8
  69.7 0.8 shard_map.105
  70.6 0.7 collective-permute-start.10
  71.3 1.0 shard_map.106
  72.3 1.2 copy.17
  73.5 69.7 %all-to-all-start = ((f32[2,256,256]{2,0,1:T(2,128)}), f32[2,256,256]{2,0,1:T(2,128)S(1)}, u32[]{:S(2)}, u32[]{:S(2)}) async-start(f32[2,256,256]{2,0,1:T(2,128)} %copy.17), calls=%async_computation | async-start | bytes 1048576 | tf_op jit(solution)/shard_map/all_to_all | solution.py:425
  143.2 1.3 collective-permute-start.11
  144.5 0.7 collective-permute-start.12
  145.3 1.3 collective-permute-start.13
  152.7 1.3 collective-permute-start.16
  154.6 1.3 collective-permute-done.16
  155.9 2.7 %collective-permute-start.17 = (f32[64,256]{1,0:T(8,128)S(1)}, f32[64,256]{1,0:T(8,128)S(1)}, u32[]{:S(2)}, u32[]{:S(2)}) collective-permute-start(f32[64,256]{1,0:T(8,128)S(1)} %bitcast_add_fusion), channel_id=1, source_target_pairs={{0,16},{1,17},{2,18},{3,19},{4,20},{5,21},{6,22},{7,23},{16,32},{1... | collective-permute-start | bytes 196616 | tf_op jit(solution)/shard_map/ppermute | solution.py:315
  158.6 7.4 %collective-permute-start.18 = (f32[64,256]{1,0:T(8,128)S(1)}, f32[64,256]{1,0:T(8,128)}, u32[]{:S(2)}, u32[]{:S(2)}) collective-permute-start(f32[64,256]{1,0:T(8,128)S(1)} %bitcast_add_fusion), channel_id=1, source_target_pairs={{0,32},{1,33},{2,34},{3,35},{4,36},{5,37},{6,38},{7,39},{16,48},{1... | collective-permute-start | bytes 196616 | tf_op jit(solution)/shard_map/ppermute | solution.py:315
  166.0 2.4 %collective-permute-start.19 = (f32[64,256]{1,0:T(8,128)S(1)}, f32[64,256]{1,0:T(8,128)}, u32[]{:S(2)}, u32[]{:S(2)}) collective-permute-start(f32[64,256]{1,0:T(8,128)S(1)} %bitcast_add_fusion), channel_id=1, source_target_pairs={{0,48},{1,49},{2,50},{3,51},{4,52},{5,53},{6,54},{7,55},{16,0},{17... | collective-permute-start | bytes 196616 | tf_op jit(solution)/shard_map/ppermute | solution.py:315
  168.4 7.4 %collective-permute-done.13 = f32[2,2,256,256]{3,2,1,0:T(8,128)} collective-permute-done((f32[2,2,256,256]{3,2,1,0:T(8,128)}, f32[2,2,256,256]{3,2,1,0:T(8,128)}, u32[]{:S(2)}, u32[]{:S(2)}) %collective-permute-start.13) | collective-permute-done | bytes 1048608 | tf_op jit(solution)/shard_map/ppermute | solution.py:315
  175.9 1.5 broadcast_select_fusion.5
  178.1 0.9 add_add_fusion.1
  179.0 1.9 collective-permute-start.20
  180.9 5.0 %collective-permute-start.21 = (f32[64,256]{1,0:T(8,128)S(1)}, f32[64,256]{1,0:T(8,128)S(1)}, u32[]{:S(2)}, u32[]{:S(2)}) collective-permute-start(f32[64,256]{1,0:T(8,128)S(1)} %add_add_fusion.1), channel_id=1, source_target_pairs={{0,128},{1,129},{2,130},{3,131},{4,132},{5,133},{6,134},{7,135},{1... | collective-permute-start | bytes 196616 | tf_op jit(solution)/shard_map/ppermute | solution.py:315
  186.0 3.0 %collective-permute-start.22 = (f32[64,256]{1,0:T(8,128)S(1)}, f32[64,256]{1,0:T(8,128)S(1)}, u32[]{:S(2)}, u32[]{:S(2)}) collective-permute-start(f32[64,256]{1,0:T(8,128)S(1)} %add_add_fusion.1), channel_id=1, source_target_pairs={{0,192},{1,193},{2,194},{3,195},{4,196},{5,197},{6,198},{7,199},{1... | collective-permute-start | bytes 196616 | tf_op jit(solution)/shard_map/ppermute | solution.py:315
  189.1 3.0 %collective-permute-done.22 = f32[64,256]{1,0:T(8,128)S(1)} collective-permute-done((f32[64,256]{1,0:T(8,128)S(1)}, f32[64,256]{1,0:T(8,128)S(1)}, u32[]{:S(2)}, u32[]{:S(2)}) %collective-permute-start.22) | collective-permute-done | bytes 65568 | tf_op jit(solution)/shard_map/ppermute | solution.py:315
  192.1 1.3 collective-permute-start.23
  193.4 0.7 fusion.3
  195.0 12.1 %collective-permute-done.15 = f32[2,2,256,256]{3,2,1,0:T(8,128)S(1)} collective-permute-done((f32[2,2,256,256]{3,2,1,0:T(8,128)S(1)}, f32[2,2,256,256]{3,2,1,0:T(8,128)S(1)}, u32[]{:S(2)}, u32[]{:S(2)}) %collective-permute-start.15) | collective-permute-done | bytes 1048608 | tf_op jit(solution)/shard_map/ppermute | solution.py:315
  207.1 2.1 select_add_fusion.3
  209.2 2.7 %pad_maximum_fusion = f32[2,2,256,1024]{3,2,1,0:T(8,128)} fusion(f32[2,2,256,256]{3,2,1,0:T(8,128)S(1)} %get-tuple-element.43, f32[2,2,256,256]{3,2,1,0:T(8,128)S(1)} %get-tuple-element.42, f32[2,2,256,256]{3,2,1,0:T(8,128)S(1)} %get-tuple-element.41, f32[2,2,256,256]{3,2,1,0:T(8,128)S(1)} %get-tuple-element.40), kind=kLoop, calls=%fused_computation | loop fusion | flops 3145728 | bytes 8388608 | tf_op jit(solution)/shard_map/concatenate | solution.py:473
  (74 shorter events, 9.3 us)
Async XLA Ops:
  0.6 23.2 %copy-start = (f32[256,256]{1,0:T(8,128)S(1)}, f32[256,256]{1,0:T(8,128)}, u32[]{:S(2)}) copy-start(f32[256,256]{1,0:T(8,128)} %param.11) | copy-start | bytes 786436
  3.0 29.7 %collective-permute-start.2 = (f32[2,2,256,256]{3,2,1,0:T(8,128)}, f32[2,2,256,256]{3,2,1,0:T(8,128)S(1)}, u32[]{:S(2)}, u32[]{:S(2)}) collective-permute-start(f32[2,2,256,256]{3,2,1,0:T(8,128)} %slice.30), channel_id=1, source_target_pairs={{8,0},{9,1},{10,2},{11,3},{12,4},{13,5},{14,6},{15,7},{24,16},{25,... | collective-permute-start | bytes 3145736 | tf_op jit(solution)/shard_map/ppermute | solution.py:315
  4.3 47.6 %collective-permute-start.3 = (f32[2,2,256,256]{3,2,1,0:T(8,128)}, f32[2,2,256,256]{3,2,1,0:T(8,128)}, u32[]{:S(2)}, u32[]{:S(2)}) collective-permute-start(f32[2,2,256,256]{3,2,1,0:T(8,128)} %slice.30), channel_id=1, source_target_pairs={{0,249},{6,255},{16,9},{22,15},{32,25},{38,31},{48,41},{54,47},{64... | collective-permute-start | bytes 3145736 | tf_op jit(solution)/shard_map/ppermute | solution.py:315
  5.9 46.7 %collective-permute-start.6 = (f32[2,2,256,256]{3,2,1,0:T(8,128)}, f32[2,2,256,256]{3,2,1,0:T(8,128)}, u32[]{:S(2)}, u32[]{:S(2)}) collective-permute-start(f32[2,2,256,256]{3,2,1,0:T(8,128)} %slice.30), channel_id=1, source_target_pairs={{2,249},{4,255},{18,9},{20,15},{34,25},{36,31},{50,41},{52,47},{66... | collective-permute-start | bytes 3145736 | tf_op jit(solution)/shard_map/ppermute | solution.py:315
  7.6 37.3 %collective-permute-start.1 = (f32[2,2,256,256]{3,2,1,0:T(8,128)}, f32[2,2,256,256]{3,2,1,0:T(8,128)S(1)}, u32[]{:S(2)}, u32[]{:S(2)}) collective-permute-start(f32[2,2,256,256]{3,2,1,0:T(8,128)} %slice.30), channel_id=1, source_target_pairs={{1,249},{3,251},{5,253},{7,255},{17,9},{19,11},{21,13},{23,15},{33... | collective-permute-start | bytes 3145736 | tf_op jit(solution)/shard_map/ppermute | solution.py:315
  23.8 7.4 %collective-permute-start = (f32[4224]{0:T(1024)S(1)}, f32[4224]{0:T(1024)S(1)}, u32[]{:S(2)}, u32[]{:S(2)}) collective-permute-start(f32[4224]{0:T(1024)S(1)} %concatenate.6), channel_id=1, source_target_pairs={{0,8},{1,9},{2,10},{3,11},{4,12},{5,13},{6,14},{7,15},{8,16},{9,17... | collective-permute-start | bytes 50696 | tf_op jit(solution)/shard_map/ppermute | solution.py:315
  35.8 16.9 %collective-permute-start.4 = (f32[2,2,256,256]{3,2,1,0:T(8,128)}, f32[2,2,256,256]{3,2,1,0:T(8,128)}, u32[]{:S(2)}, u32[]{:S(2)}) collective-permute-start(f32[2,2,256,256]{3,2,1,0:T(8,128)} %select_select_fusion.2), channel_id=1, source_target_pairs={{2,3},{3,2},{4,5},{5,4},{8,9},{9,8},{14,15},{15,14},{18,19},{19,18... | collective-permute-start | bytes 3145736 | tf_op jit(solution)/shard_map/ppermute | solution.py:315
  37.4 18.5 %collective-permute-start.7 = (f32[2,2,256,256]{3,2,1,0:T(8,128)}, f32[2,2,256,256]{3,2,1,0:T(8,128)}, u32[]{:S(2)}, u32[]{:S(2)}) collective-permute-start(f32[2,2,256,256]{3,2,1,0:T(8,128)} %select_select_fusion.2), channel_id=1, source_target_pairs={{0,3},{1,2},{6,5},{7,4},{10,9},{11,8},{12,15},{13,14},{16,19},{17,... | collective-permute-start | bytes 3145736 | tf_op jit(solution)/shard_map/ppermute | solution.py:315
  44.9 13.5 %copy-start.9 = (pred[256]{0:T(512)(128)(4,1)}, pred[256]{0:T(512)(128)(4,1)S(1)}, u32[]{:S(2)}) copy-start(pred[256]{0:T(512)(128)(4,1)S(1)} %iota_compare_fusion.5) | copy-start | bytes 772
  47.1 19.8 %copy-start.1 = (bf16[4,2,256,256]{3,2,1,0:T(8,128)(2,1)S(1)}, bf16[4,2,256,256]{3,2,1,0:T(8,128)(2,1)}, u32[]{:S(2)}) copy-start(bf16[4,2,256,256]{3,2,1,0:T(8,128)(2,1)} %constant.107.clone.refs_2_) | copy-start | bytes 3145732
  47.1 19.8 %collective-permute-start.5 = (f32[2,2,256,256]{3,2,1,0:T(8,128)S(1)}, f32[2,2,256,256]{3,2,1,0:T(8,128)S(1)}, u32[]{:S(2)}, u32[]{:S(2)}) collective-permute-start(f32[2,2,256,256]{3,2,1,0:T(8,128)S(1)} %select_select_fusion.refs_5_.refs_6_), channel_id=1, source_target_pairs={{0,2},{1,3},{6,4},{7,5},{10,8},{11,9},{12,14},{13,15},{16,18},{17,... | collective-permute-start | bytes 3145736 | tf_op jit(solution)/shard_map/ppermute | solution.py:315
  51.8 15.1 %copy-start.2 = (f32[256,256]{1,0:T(8,128)S(1)}, f32[256,256]{1,0:T(8,128)}, u32[]{:S(2)}) copy-start(f32[256,256]{1,0:T(8,128)} %get-tuple-element.24.refs_4_) | copy-start | bytes 786436
  51.8 15.1 %copy-start.3 = (f32[256,256]{1,0:T(8,128)S(1)}, f32[256,256]{1,0:T(8,128)}, u32[]{:S(2)}) copy-start(f32[256,256]{1,0:T(8,128)} %get-tuple-element.23.refs_3_) | copy-start | bytes 786436
  51.8 15.1 %copy-start.4 = (f32[2,256,256]{2,1,0:T(8,128)S(1)}, f32[2,256,256]{2,1,0:T(8,128)}, u32[]{:S(2)}) copy-start(f32[2,256,256]{2,1,0:T(8,128)} %refs_1_.1) | copy-start | bytes 1572868
  51.8 16.6 %collective-permute-start.9 = (f32[256,256]{1,0:T(8,128)}, f32[256,256]{1,0:T(8,128)S(1)}, u32[]{:S(2)}, u32[]{:S(2)}) collective-permute-start(f32[256,256]{1,0:T(8,128)} %dynamic-slice_bitcast_fusion), channel_id=1, source_target_pairs={{6,14},{12,20},{22,30},{28,36},{38,46},{44,52},{54,62},{60,68},{70... | collective-permute-start | bytes 786440 | tf_op jit(solution)/shard_map/ppermute | solution.py:315
  58.4 10.1 %copy-start.5 = (f32[256,256]{1,0:T(8,128)S(1)}, f32[256,256]{1,0:T(8,128)}, u32[]{:S(2)}) copy-start(f32[256,256]{1,0:T(8,128)} %constant.105.clone) | copy-start | bytes 786436
  58.4 10.1 %copy-start.8 = (f32[2,256,256]{2,1,0:T(8,128)S(1)}, f32[2,256,256]{2,1,0:T(8,128)}, u32[]{:S(2)}) copy-start(f32[2,256,256]{2,1,0:T(8,128)} %param.13) | copy-start | bytes 1572868
  58.4 10.7 %copy-start.6 = (f32[256,256]{1,0:T(8,128)S(1)}, f32[256,256]{1,0:T(8,128)}, u32[]{:S(2)}) copy-start(f32[256,256]{1,0:T(8,128)} %constant.106.clone) | copy-start | bytes 786436
  67.8 2.0 collective-permute-start.8
  70.6 0.7 collective-permute-start.10
  73.5 79.0 %all-to-all-start = ((f32[2,256,256]{2,0,1:T(2,128)}), f32[2,256,256]{2,0,1:T(2,128)S(1)}, u32[]{:S(2)}, u32[]{:S(2)}) async-start(f32[2,256,256]{2,0,1:T(2,128)} %copy.17), calls=%async_computation | async-start | bytes 1048576 | tf_op jit(solution)/shard_map/all_to_all | solution.py:425
  143.2 22.8 %collective-permute-start.11 = (f32[2,2,256,256]{3,2,1,0:T(8,128)}, f32[2,2,256,256]{3,2,1,0:T(8,128)S(1)}, u32[]{:S(2)}, u32[]{:S(2)}) collective-permute-start(f32[2,2,256,256]{3,2,1,0:T(8,128)} %get-tuple-element.34), channel_id=1, source_target_pairs={{2,0},{3,1},{4,6},{5,7},{8,10},{9,11},{14,12},{15,13},{18,16},{19,... | collective-permute-start | bytes 3145736 | tf_op jit(solution)/shard_map/ppermute | solution.py:315
  144.5 23.9 %collective-permute-start.12 = (f32[2,2,256,256]{3,2,1,0:T(8,128)}, f32[2,2,256,256]{3,2,1,0:T(8,128)S(1)}, u32[]{:S(2)}, u32[]{:S(2)}) collective-permute-start(f32[2,2,256,256]{3,2,1,0:T(8,128)} %get-tuple-element.35), channel_id=1, source_target_pairs={{2,3},{3,2},{4,5},{5,4},{8,9},{9,8},{14,15},{15,14},{18,19},{19,18... | collective-permute-start | bytes 3145736 | tf_op jit(solution)/shard_map/ppermute | solution.py:315
  145.3 30.6 %collective-permute-start.13 = (f32[2,2,256,256]{3,2,1,0:T(8,128)}, f32[2,2,256,256]{3,2,1,0:T(8,128)}, u32[]{:S(2)}, u32[]{:S(2)}) collective-permute-start(f32[2,2,256,256]{3,2,1,0:T(8,128)} %get-tuple-element.36), channel_id=1, source_target_pairs={{2,1},{3,0},{4,7},{5,6},{8,11},{9,10},{14,13},{15,12},{18,17},{19,... | collective-permute-start | bytes 3145736 | tf_op jit(solution)/shard_map/ppermute | solution.py:315
  152.7 3.1 %collective-permute-start.16 = (f32[64,256]{1,0:T(8,128)S(1)}, f32[64,256]{1,0:T(8,128)S(1)}, u32[]{:S(2)}, u32[]{:S(2)}) collective-permute-start(f32[64,256]{1,0:T(8,128)S(1)} %bitcast.43), channel_id=1, source_target_pairs={{8,0},{9,1},{10,2},{11,3},{12,4},{13,5},{14,6},{15,7},{24,16},{25,... | collective-permute-start | bytes 196616 | tf_op jit(solution)/shard_map/ppermute | solution.py:315
  155.9 22.2 %collective-permute-start.17 = (f32[64,256]{1,0:T(8,128)S(1)}, f32[64,256]{1,0:T(8,128)S(1)}, u32[]{:S(2)}, u32[]{:S(2)}) collective-permute-start(f32[64,256]{1,0:T(8,128)S(1)} %bitcast_add_fusion), channel_id=1, source_target_pairs={{0,16},{1,17},{2,18},{3,19},{4,20},{5,21},{6,22},{7,23},{16,32},{1... | collective-permute-start | bytes 196616 | tf_op jit(solution)/shard_map/ppermute | solution.py:315
  158.6 19.4 %collective-permute-start.18 = (f32[64,256]{1,0:T(8,128)S(1)}, f32[64,256]{1,0:T(8,128)}, u32[]{:S(2)}, u32[]{:S(2)}) collective-permute-start(f32[64,256]{1,0:T(8,128)S(1)} %bitcast_add_fusion), channel_id=1, source_target_pairs={{0,32},{1,33},{2,34},{3,35},{4,36},{5,37},{6,38},{7,39},{16,48},{1... | collective-permute-start | bytes 196616 | tf_op jit(solution)/shard_map/ppermute | solution.py:315
  166.0 12.0 %collective-permute-start.19 = (f32[64,256]{1,0:T(8,128)S(1)}, f32[64,256]{1,0:T(8,128)}, u32[]{:S(2)}, u32[]{:S(2)}) collective-permute-start(f32[64,256]{1,0:T(8,128)S(1)} %bitcast_add_fusion), channel_id=1, source_target_pairs={{0,48},{1,49},{2,50},{3,51},{4,52},{5,53},{6,54},{7,55},{16,0},{17... | collective-permute-start | bytes 196616 | tf_op jit(solution)/shard_map/ppermute | solution.py:315
  168.4 7.4 %copy-start.7 = (f32[2,2,256,256]{3,2,1,0:T(8,128)}, f32[2,2,256,256]{3,2,1,0:T(8,128)S(1)}, u32[]{:S(2)}) copy-start(f32[2,2,256,256]{3,2,1,0:T(8,128)S(1)} %collective-permute-done.12) | copy-start | bytes 3145732
  177.4 29.7 %collective-permute-start.15 = (f32[2,2,256,256]{3,2,1,0:T(8,128)S(1)}, f32[2,2,256,256]{3,2,1,0:T(8,128)S(1)}, u32[]{:S(2)}, u32[]{:S(2)}) collective-permute-start(f32[2,2,256,256]{3,2,1,0:T(8,128)S(1)} %get-tuple-element.39), channel_id=1, source_target_pairs={{0,8},{1,9},{2,10},{3,11},{4,12},{5,13},{6,14},{7,15},{8,16},{9,17... | collective-permute-start | bytes 3145736 | tf_op jit(solution)/shard_map/ppermute | solution.py:315
  179.0 10.1 %collective-permute-start.20 = (f32[64,256]{1,0:T(8,128)S(1)}, f32[64,256]{1,0:T(8,128)S(1)}, u32[]{:S(2)}, u32[]{:S(2)}) collective-permute-start(f32[64,256]{1,0:T(8,128)S(1)} %add_add_fusion.1), channel_id=1, source_target_pairs={{0,64},{1,65},{2,66},{3,67},{4,68},{5,69},{6,70},{7,71},{16,80},{1... | collective-permute-start | bytes 196616 | tf_op jit(solution)/shard_map/ppermute | solution.py:315
  180.9 8.2 %collective-permute-start.21 = (f32[64,256]{1,0:T(8,128)S(1)}, f32[64,256]{1,0:T(8,128)S(1)}, u32[]{:S(2)}, u32[]{:S(2)}) collective-permute-start(f32[64,256]{1,0:T(8,128)S(1)} %add_add_fusion.1), channel_id=1, source_target_pairs={{0,128},{1,129},{2,130},{3,131},{4,132},{5,133},{6,134},{7,135},{1... | collective-permute-start | bytes 196616 | tf_op jit(solution)/shard_map/ppermute | solution.py:315
  186.0 6.2 %collective-permute-start.22 = (f32[64,256]{1,0:T(8,128)S(1)}, f32[64,256]{1,0:T(8,128)S(1)}, u32[]{:S(2)}, u32[]{:S(2)}) collective-permute-start(f32[64,256]{1,0:T(8,128)S(1)} %add_add_fusion.1), channel_id=1, source_target_pairs={{0,192},{1,193},{2,194},{3,195},{4,196},{5,197},{6,198},{7,199},{1... | collective-permute-start | bytes 196616 | tf_op jit(solution)/shard_map/ppermute | solution.py:315
  189.0 4.5 %collective-permute-start.14 = (f32[2,2,1,256]{3,2,1,0:T(1,128)S(1)}, f32[2,2,1,256]{3,2,1,0:T(1,128)S(1)}, u32[]{:S(2)}, u32[]{:S(2)}) collective-permute-start(f32[2,2,1,256]{3,2,1,0:T(1,128)S(1)} %slice.39), channel_id=1, source_target_pairs={{0,248},{1,249},{2,250},{3,251},{4,252},{5,253},{6,254},{7,255},{8... | collective-permute-start | bytes 12296 | tf_op jit(solution)/shard_map/ppermute | solution.py:315
  192.1 2.2 %collective-permute-start.23 = (f32[64,256]{1,0:T(8,128)S(1)}, f32[64,256]{1,0:T(8,128)S(1)}, u32[]{:S(2)}, u32[]{:S(2)}) collective-permute-start(f32[64,256]{1,0:T(8,128)S(1)} %add_add_fusion), channel_id=1, source_target_pairs={{0,8},{1,9},{2,10},{3,11},{4,12},{5,13},{6,14},{7,15},{16,24},{17,... | collective-permute-start | bytes 196616 | tf_op jit(solution)/shard_map/ppermute | solution.py:315

commit v4 on v3

--- a/solution.py
+++ b/solution.py
@@ -232,7 +232,10 @@
             lax.fori_loop(0, 8, step_back(8), 0)
             for part in range(2):
                 undone = pltpu.roll(psi[part], lax.rem(N - row, N), 0)
-                wave_out[part] = pltpu.roll(undone, lax.rem(N - col, N), 1)
+                undone = pltpu.roll(undone, lax.rem(N - col, N), 1)
+                for index in range(wave_out.shape[0]):
+                    size = wave_out.shape[2]
+                    wave_out[index, part] = undone[index * size : (index + 1) * size]
         if backward:
             for i in range(8):
                 piece_copy(0, i).wait()
@@ -248,7 +251,7 @@
     return pltpu.with_memory_space_constraint(value, pltpu.HBM)
 
 
-def run_chain(forward, backward, meta, wave, tables, target, windows, old, pieces):
+def run_chain(forward, backward, cut_count, meta, wave, tables, target, windows, old, pieces):
     vm = pl.BlockSpec(memory_space=pltpu.VMEM)
     hbm = pl.BlockSpec(memory_space=pl.ANY)
     far = pl.BlockSpec(memory_space=pltpu.HBM)
@@ -260,7 +263,8 @@
     if not forward:
         operands, specs = operands + [old, *map(in_hbm, pieces)], specs + [far] * 5
         aliases = {len(operands) - 4 + i: 1 + i for i in range(4)}
-    shapes, outs = [jax.ShapeDtypeStruct((2, N, N), F32)], [vm]
+    wave_shape = (2, N, N) if forward else (cut_count, 2, N // cut_count, N)
+    shapes, outs = [jax.ShapeDtypeStruct(wave_shape, F32)], [vm]
     if not backward:
         shapes, outs = shapes + [jax.ShapeDtypeStruct((8, 2, N, N), F32)], outs + [far]
     else:
@@ -416,15 +420,17 @@
         along_hub,
         jnp.where(unmerged, rim_across, across_hub),
     ]
-    wave, past = run_chain(True, False, meta, probe, tables, None, windows, None, None)
+    wave, past = run_chain(True, False, cut_count, meta, probe, tables, None, windows, None, None)
     wave = send(wave, to_other_half, lambda t, c: c < 4 and at_hub(t, c))
-    wave, *pieces = run_chain(True, True, meta, wave, tables, target, windows, None, None)
+    wave, *pieces = run_chain(True, True, cut_count, meta, wave, tables, target, windows, None, None)
     wave = send(wave, to_other_half, lambda t, c: c >= 4 and at_hub(t, c))
-    wave, *pieces = run_chain(False, True, meta, wave, tables, None, windows, past, pieces)
-
-    spread = lax.all_to_all(wave, "cuts", 1, 1, tiled=True)
+    wave, *pieces = run_chain(
+        False, True, cut_count, meta, wave, tables, None, windows, past, pieces
+    )
+
+    spread = lax.all_to_all(wave, "cuts", 0, 0, tiled=True)
     own_rows = N // cut_count
-    total = jnp.sum(spread.reshape(2, cut_count, own_rows, N), axis=1)
+    total = jnp.sum(spread, axis=0)
     total = total.reshape(2 * own_rows, N)
     total = total + send(total, lambda t, c: (t ^ 1, c), lambda t, c: t % 2 == 1)
     for stride in (2, 8):

time: 213 us -> 212 us (level)
  no operation moved by 1% of the time
where the time goes in v4:
time: 212 us; the launch traced here: 211 us
  starting transfers between devices  125 us (59%)
  waiting for transfers between devices  37.8 us (18%)
  other arithmetic  22.5 us (11%)
  local copies, waits for them, and re-layouts  9.29 us (4%)
  between operations  8.51 us (4%)
  matrix products  5.7 us (3%)
  Pallas kernels  2.67 us (1%)
    all_to_all x1, starting transfers between devices, shards(): spread = lax.all_to_all(wave, 'cuts', 0, 0, tiled=True)  69.7 us
    ppermute x24, starting transfers between devices, send(): return lax.ppermute(value, AXES, pairs)  55.2 us
    ppermute x24, waiting for transfers between devices, send(): return lax.ppermute(value, AXES, pairs)  37.8 us
  transfers between devices with their start and end apart: 25, of which 8 were waited for; matrix products, arithmetic and copies ran while one was open for 14% of the time, Pallas kernels for 0%

profile of v4, /device:TPU:32, one launch (start us, length us, event | category | flops | bytes accessed | tf_op | source)
XLA Modules:
  0.0 211.3 jit_solution(6341947288804204932)
XLA Ops:
  0.6 2.3 %slice.30 = f32[2,2,256,256]{3,2,1,0:T(8,128)} slice(f32[2,2,256,1024]{3,2,1,0:T(8,128)} %param.12), slice={[0:2], [0:2], [0:256], [768:1024]} | slice | bytes 2097152 | tf_op jit(solution)/shard_map/slice | solution.py:348
  3.0 1.3 collective-permute-start.2
  4.3 1.6 collective-permute-start.3
  5.9 1.7 collective-permute-start.6
  7.6 9.9 %collective-permute-start.1 = (f32[2,2,256,256]{3,2,1,0:T(8,128)}, f32[2,2,256,256]{3,2,1,0:T(8,128)S(1)}, u32[]{:S(2)}, u32[]{:S(2)}) collective-permute-start(f32[2,2,256,256]{3,2,1,0:T(8,128)} %slice.30), channel_id=1, source_target_pairs={{1,249},{3,251},{5,253},{7,255},{17,9},{19,11},{21,13},{23,15},{33... | collective-permute-start | bytes 3145736 | tf_op jit(solution)/shard_map/ppermute | solution.py:319
  17.5 0.9 slice.29
  18.4 1.3 fusion.22
  21.0 1.4 constant_dynamic-slice_fusion.1
  23.9 1.3 fusion.23
  25.2 3.2 %fusion.20 = (f32[256,256]{1,0:T(8,128)}, f32[256,256]{1,0:T(8,128)}) fusion(f32[256,256]{1,0:T(8,128)S(1)} %fusion.23, f32[256,256]{1,0:T(8,128)} %constant.106.clone), kind=kOutput, calls=%fused_computation.69 | convolution fusion | flops 201326592 | bytes 1048576 | tf_op jit(solution)/shard_map/dot_general | solution.py:400
  29.1 2.2 %collective-permute-done = f32[4224]{0:T(1024)S(1)} collective-permute-done((f32[4224]{0:T(1024)S(1)}, f32[4224]{0:T(1024)S(1)}, u32[]{:S(2)}, u32[]{:S(2)}) %collective-permute-start) | collective-permute-done | bytes 16928 | tf_op jit(solution)/shard_map/ppermute | solution.py:319
  32.7 3.1 %select_select_fusion.2 = f32[2,2,256,256]{3,2,1,0:T(8,128)} fusion(f32[2,2,256,256]{3,2,1,0:T(8,128)} %slice.30, f32[2,2,256,256]{3,2,1,0:T(8,128)S(1)} %collective-permute-done.2, pred[256]{0:T(512)(128)(4,1)S(1)} %broadcast_or_fusion, pred[]{:T(512)S(6)} %eq.111, f32[2,2,256,1024]{3,2,1,0:T(8,128)} %param.12, s32[]{:T(128)S(6)} %select_n.244, ...), kind=kLoop, calls=%fused_computation.7 | loop fusion | flops 1048576 | bytes 5247753 | tf_op jit(solution)/shard_map/jit(_where)/select_n | solution.py:410
  35.8 1.6 collective-permute-start.4
  37.4 6.8 %collective-permute-start.7 = (f32[2,2,256,256]{3,2,1,0:T(8,128)}, f32[2,2,256,256]{3,2,1,0:T(8,128)}, u32[]{:S(2)}, u32[]{:S(2)}) collective-permute-start(f32[2,2,256,256]{3,2,1,0:T(8,128)} %select_select_fusion.2), channel_id=1, source_target_pairs={{0,3},{1,2},{6,5},{7,4},{10,9},{11,8},{12,15},{13,14},{16,19},{17,... | collective-permute-start | bytes 3145736 | tf_op jit(solution)/shard_map/ppermute | solution.py:319
  44.9 2.2 %select_select_fusion.refs_5_.refs_6_ = f32[2,2,256,256]{3,2,1,0:T(8,128)S(1)} fusion(f32[2,2,256,256]{3,2,1,0:T(8,128)} %slice.30, f32[2,2,256,256]{3,2,1,0:T(8,128)S(1)} %collective-permute-done.2, f32[2,2,256,256]{3,2,1,0:T(8,128)S(1)} %collective-permute-done.1, pred[256]{0:T(512)(128)(4,1)S(1)} %iota_compare_fusion.5, pred[]{:T(512)S(6)} %eq.112, ...), kind=kLoop, calls=%fused_computation.5 | loop fusion | flops 1310720 | bytes 6296330 | tf_op jit(solution)/shard_map/jit(_where)/select_n | solution.py:414
  47.1 1.5 collective-permute-start.5
  50.1 1.7 dynamic-slice_bitcast_fusion
  51.9 0.8 collective-permute-start.9
  52.7 3.2 %collective-permute-done.7 = f32[2,2,256,256]{3,2,1,0:T(8,128)} collective-permute-done((f32[2,2,256,256]{3,2,1,0:T(8,128)}, f32[2,2,256,256]{3,2,1,0:T(8,128)}, u32[]{:S(2)}, u32[]{:S(2)}) %collective-permute-start.7) | collective-permute-done | bytes 1048608 | tf_op jit(solution)/shard_map/ppermute | solution.py:319
  55.9 2.5 %broadcast_select_fusion = (f32[2,2,256,256]{3,2,1,0:T(8,128)S(1)}, f32[2,2,256,256]{3,2,1,0:T(8,128)S(1)}) fusion(f32[2,2,256,256]{3,2,1,0:T(8,128)} %collective-permute-done.6, f32[2,2,256,256]{3,2,1,0:T(8,128)} %collective-permute-done.7, pred[256]{0:T(512)(128)(4,1)S(1)} %not_and_fusion, f32[2,2,256,256]{3,2,1,0:T(8,128)} %collective-permute-done.3, ...), kind=kLoop, calls=%fused_computation.8 | loop fusion | flops 524288 | bytes 6291712 | tf_op jit(solution)/shard_map/jit(_where)/select_n | solution.py:421
  58.4 8.5 %collective-permute-done.5.refs_7_.refs_8_ = f32[2,2,256,256]{3,2,1,0:T(8,128)S(1)} collective-permute-done((f32[2,2,256,256]{3,2,1,0:T(8,128)S(1)}, f32[2,2,256,256]{3,2,1,0:T(8,128)S(1)}, u32[]{:S(2)}, u32[]{:S(2)}) %collective-permute-start.5) | collective-permute-done | bytes 1048608 | tf_op jit(solution)/shard_map/ppermute | solution.py:319
  66.9 0.8 shard_map.104
  67.8 0.7 collective-permute-start.8
  69.7 0.8 shard_map.105
  70.6 0.7 collective-permute-start.10
  71.3 1.0 shard_map.106
  72.3 0.8 copy-done.5
  73.1 69.7 %all-to-all-start = ((f32[8,2,32,256]{3,2,1,0:T(8,128)}), f32[8,2,32,256]{3,2,1,0:T(8,128)S(1)}, u32[]{:S(2)}, u32[]{:S(2)}) async-start(f32[8,2,32,256]{3,2,1,0:T(8,128)} %copy-done.5), calls=%async_computation | async-start | bytes 1048576 | tf_op jit(solution)/shard_map/all_to_all | solution.py:431
  142.8 1.3 collective-permute-start.11
  144.1 0.7 collective-permute-start.12
  144.8 1.3 collective-permute-start.13
  152.2 1.3 collective-permute-start.16
  154.1 1.3 collective-permute-done.16
  155.4 2.8 %collective-permute-start.17 = (f32[64,256]{1,0:T(8,128)S(1)}, f32[64,256]{1,0:T(8,128)S(1)}, u32[]{:S(2)}, u32[]{:S(2)}) collective-permute-start(f32[64,256]{1,0:T(8,128)S(1)} %bitcast_add_fusion), channel_id=1, source_target_pairs={{0,16},{1,17},{2,18},{3,19},{4,20},{5,21},{6,22},{7,23},{16,32},{1... | collective-permute-start | bytes 196616 | tf_op jit(solution)/shard_map/ppermute | solution.py:319
  158.2 7.3 %collective-permute-start.18 = (f32[64,256]{1,0:T(8,128)S(1)}, f32[64,256]{1,0:T(8,128)}, u32[]{:S(2)}, u32[]{:S(2)}) collective-permute-start(f32[64,256]{1,0:T(8,128)S(1)} %bitcast_add_fusion), channel_id=1, source_target_pairs={{0,32},{1,33},{2,34},{3,35},{4,36},{5,37},{6,38},{7,39},{16,48},{1... | collective-permute-start | bytes 196616 | tf_op jit(solution)/shard_map/ppermute | solution.py:319
  165.5 2.4 %collective-permute-start.19 = (f32[64,256]{1,0:T(8,128)S(1)}, f32[64,256]{1,0:T(8,128)}, u32[]{:S(2)}, u32[]{:S(2)}) collective-permute-start(f32[64,256]{1,0:T(8,128)S(1)} %bitcast_add_fusion), channel_id=1, source_target_pairs={{0,48},{1,49},{2,50},{3,51},{4,52},{5,53},{6,54},{7,55},{16,0},{17... | collective-permute-start | bytes 196616 | tf_op jit(solution)/shard_map/ppermute | solution.py:319
  168.0 7.4 %collective-permute-done.13 = f32[2,2,256,256]{3,2,1,0:T(8,128)} collective-permute-done((f32[2,2,256,256]{3,2,1,0:T(8,128)}, f32[2,2,256,256]{3,2,1,0:T(8,128)}, u32[]{:S(2)}, u32[]{:S(2)}) %collective-permute-start.13) | collective-permute-done | bytes 1048608 | tf_op jit(solution)/shard_map/ppermute | solution.py:319
  175.4 1.5 broadcast_select_fusion.5
  177.6 0.9 add_add_fusion.1
  178.5 1.9 collective-permute-start.20
  180.4 5.1 %collective-permute-start.21 = (f32[64,256]{1,0:T(8,128)S(1)}, f32[64,256]{1,0:T(8,128)S(1)}, u32[]{:S(2)}, u32[]{:S(2)}) collective-permute-start(f32[64,256]{1,0:T(8,128)S(1)} %add_add_fusion.1), channel_id=1, source_target_pairs={{0,128},{1,129},{2,130},{3,131},{4,132},{5,133},{6,134},{7,135},{1... | collective-permute-start | bytes 196616 | tf_op jit(solution)/shard_map/ppermute | solution.py:319
  185.5 3.0 %collective-permute-start.22 = (f32[64,256]{1,0:T(8,128)S(1)}, f32[64,256]{1,0:T(8,128)S(1)}, u32[]{:S(2)}, u32[]{:S(2)}) collective-permute-start(f32[64,256]{1,0:T(8,128)S(1)} %add_add_fusion.1), channel_id=1, source_target_pairs={{0,192},{1,193},{2,194},{3,195},{4,196},{5,197},{6,198},{7,199},{1... | collective-permute-start | bytes 196616 | tf_op jit(solution)/shard_map/ppermute | solution.py:319
  188.6 3.0 %collective-permute-done.22 = f32[64,256]{1,0:T(8,128)S(1)} collective-permute-done((f32[64,256]{1,0:T(8,128)S(1)}, f32[64,256]{1,0:T(8,128)S(1)}, u32[]{:S(2)}, u32[]{:S(2)}) %collective-permute-start.22) | collective-permute-done | bytes 65568 | tf_op jit(solution)/shard_map/ppermute | solution.py:319
  191.7 1.3 collective-permute-start.23
  193.0 0.7 fusion.3
  194.5 12.1 %collective-permute-done.15 = f32[2,2,256,256]{3,2,1,0:T(8,128)S(1)} collective-permute-done((f32[2,2,256,256]{3,2,1,0:T(8,128)S(1)}, f32[2,2,256,256]{3,2,1,0:T(8,128)S(1)}, u32[]{:S(2)}, u32[]{:S(2)}) %collective-permute-start.15) | collective-permute-done | bytes 1048608 | tf_op jit(solution)/shard_map/ppermute | solution.py:319
  206.6 2.1 select_add_fusion.3
  208.7 2.7 %pad_maximum_fusion = f32[2,2,256,1024]{3,2,1,0:T(8,128)} fusion(f32[2,2,256,256]{3,2,1,0:T(8,128)S(1)} %get-tuple-element.43, f32[2,2,256,256]{3,2,1,0:T(8,128)S(1)} %get-tuple-element.42, f32[2,2,256,256]{3,2,1,0:T(8,128)S(1)} %get-tuple-element.41, f32[2,2,256,256]{3,2,1,0:T(8,128)S(1)} %get-tuple-element.40), kind=kLoop, calls=%fused_computation | loop fusion | flops 3145728 | bytes 8388608 | tf_op jit(solution)/shard_map/concatenate | solution.py:479
  (74 shorter events, 9.2 us)
Async XLA Ops:
  0.6 23.2 %copy-start = (f32[256,256]{1,0:T(8,128)S(1)}, f32[256,256]{1,0:T(8,128)}, u32[]{:S(2)}) copy-start(f32[256,256]{1,0:T(8,128)} %param.11) | copy-start | bytes 786436
  3.0 29.7 %collective-permute-start.2 = (f32[2,2,256,256]{3,2,1,0:T(8,128)}, f32[2,2,256,256]{3,2,1,0:T(8,128)S(1)}, u32[]{:S(2)}, u32[]{:S(2)}) collective-permute-start(f32[2,2,256,256]{3,2,1,0:T(8,128)} %slice.30), channel_id=1, source_target_pairs={{8,0},{9,1},{10,2},{11,3},{12,4},{13,5},{14,6},{15,7},{24,16},{25,... | collective-permute-start | bytes 3145736 | tf_op jit(solution)/shard_map/ppermute | solution.py:319
  4.3 47.6 %collective-permute-start.3 = (f32[2,2,256,256]{3,2,1,0:T(8,128)}, f32[2,2,256,256]{3,2,1,0:T(8,128)}, u32[]{:S(2)}, u32[]{:S(2)}) collective-permute-start(f32[2,2,256,256]{3,2,1,0:T(8,128)} %slice.30), channel_id=1, source_target_pairs={{0,249},{6,255},{16,9},{22,15},{32,25},{38,31},{48,41},{54,47},{64... | collective-permute-start | bytes 3145736 | tf_op jit(solution)/shard_map/ppermute | solution.py:319
  5.9 46.8 %collective-permute-start.6 = (f32[2,2,256,256]{3,2,1,0:T(8,128)}, f32[2,2,256,256]{3,2,1,0:T(8,128)}, u32[]{:S(2)}, u32[]{:S(2)}) collective-permute-start(f32[2,2,256,256]{3,2,1,0:T(8,128)} %slice.30), channel_id=1, source_target_pairs={{2,249},{4,255},{18,9},{20,15},{34,25},{36,31},{50,41},{52,47},{66... | collective-permute-start | bytes 3145736 | tf_op jit(solution)/shard_map/ppermute | solution.py:319
  7.6 37.4 %collective-permute-start.1 = (f32[2,2,256,256]{3,2,1,0:T(8,128)}, f32[2,2,256,256]{3,2,1,0:T(8,128)S(1)}, u32[]{:S(2)}, u32[]{:S(2)}) collective-permute-start(f32[2,2,256,256]{3,2,1,0:T(8,128)} %slice.30), channel_id=1, source_target_pairs={{1,249},{3,251},{5,253},{7,255},{17,9},{19,11},{21,13},{23,15},{33... | collective-permute-start | bytes 3145736 | tf_op jit(solution)/shard_map/ppermute | solution.py:319
  23.8 7.4 %collective-permute-start = (f32[4224]{0:T(1024)S(1)}, f32[4224]{0:T(1024)S(1)}, u32[]{:S(2)}, u32[]{:S(2)}) collective-permute-start(f32[4224]{0:T(1024)S(1)} %concatenate.6), channel_id=1, source_target_pairs={{0,8},{1,9},{2,10},{3,11},{4,12},{5,13},{6,14},{7,15},{8,16},{9,17... | collective-permute-start | bytes 50696 | tf_op jit(solution)/shard_map/ppermute | solution.py:319
  35.8 16.9 %collective-permute-start.4 = (f32[2,2,256,256]{3,2,1,0:T(8,128)}, f32[2,2,256,256]{3,2,1,0:T(8,128)}, u32[]{:S(2)}, u32[]{:S(2)}) collective-permute-start(f32[2,2,256,256]{3,2,1,0:T(8,128)} %select_select_fusion.2), channel_id=1, source_target_pairs={{2,3},{3,2},{4,5},{5,4},{8,9},{9,8},{14,15},{15,14},{18,19},{19,18... | collective-permute-start | bytes 3145736 | tf_op jit(solution)/shard_map/ppermute | solution.py:319
  37.4 18.5 %collective-permute-start.7 = (f32[2,2,256,256]{3,2,1,0:T(8,128)}, f32[2,2,256,256]{3,2,1,0:T(8,128)}, u32[]{:S(2)}, u32[]{:S(2)}) collective-permute-start(f32[2,2,256,256]{3,2,1,0:T(8,128)} %select_select_fusion.2), channel_id=1, source_target_pairs={{0,3},{1,2},{6,5},{7,4},{10,9},{11,8},{12,15},{13,14},{16,19},{17,... | collective-permute-start | bytes 3145736 | tf_op jit(solution)/shard_map/ppermute | solution.py:319
  44.9 13.4 %copy-start.10 = (pred[256]{0:T(512)(128)(4,1)}, pred[256]{0:T(512)(128)(4,1)S(1)}, u32[]{:S(2)}) copy-start(pred[256]{0:T(512)(128)(4,1)S(1)} %iota_compare_fusion.5) | copy-start | bytes 772
  47.1 19.8 %copy-start.1 = (bf16[4,2,256,256]{3,2,1,0:T(8,128)(2,1)S(1)}, bf16[4,2,256,256]{3,2,1,0:T(8,128)(2,1)}, u32[]{:S(2)}) copy-start(bf16[4,2,256,256]{3,2,1,0:T(8,128)(2,1)} %constant.107.clone.refs_2_) | copy-start | bytes 3145732
  47.1 19.8 %collective-permute-start.5 = (f32[2,2,256,256]{3,2,1,0:T(8,128)S(1)}, f32[2,2,256,256]{3,2,1,0:T(8,128)S(1)}, u32[]{:S(2)}, u32[]{:S(2)}) collective-permute-start(f32[2,2,256,256]{3,2,1,0:T(8,128)S(1)} %select_select_fusion.refs_5_.refs_6_), channel_id=1, source_target_pairs={{0,2},{1,3},{6,4},{7,5},{10,8},{11,9},{12,14},{13,15},{16,18},{17,... | collective-permute-start | bytes 3145736 | tf_op jit(solution)/shard_map/ppermute | solution.py:319
  51.9 15.1 %copy-start.2 = (f32[256,256]{1,0:T(8,128)S(1)}, f32[256,256]{1,0:T(8,128)}, u32[]{:S(2)}) copy-start(f32[256,256]{1,0:T(8,128)} %get-tuple-element.24.refs_4_) | copy-start | bytes 786436
  51.9 15.1 %copy-start.3 = (f32[256,256]{1,0:T(8,128)S(1)}, f32[256,256]{1,0:T(8,128)}, u32[]{:S(2)}) copy-start(f32[256,256]{1,0:T(8,128)} %get-tuple-element.23.refs_3_) | copy-start | bytes 786436
  51.9 15.1 %copy-start.4 = (f32[2,256,256]{2,1,0:T(8,128)S(1)}, f32[2,256,256]{2,1,0:T(8,128)}, u32[]{:S(2)}) copy-start(f32[2,256,256]{2,1,0:T(8,128)} %refs_1_.1) | copy-start | bytes 1572868
  51.9 16.6 %collective-permute-start.9 = (f32[256,256]{1,0:T(8,128)}, f32[256,256]{1,0:T(8,128)S(1)}, u32[]{:S(2)}, u32[]{:S(2)}) collective-permute-start(f32[256,256]{1,0:T(8,128)} %dynamic-slice_bitcast_fusion), channel_id=1, source_target_pairs={{6,14},{12,20},{22,30},{28,36},{38,46},{44,52},{54,62},{60,68},{70... | collective-permute-start | bytes 786440 | tf_op jit(solution)/shard_map/ppermute | solution.py:319
  58.4 10.1 %copy-start.6 = (f32[256,256]{1,0:T(8,128)S(1)}, f32[256,256]{1,0:T(8,128)}, u32[]{:S(2)}) copy-start(f32[256,256]{1,0:T(8,128)} %constant.105.clone) | copy-start | bytes 786436
  58.4 10.1 %copy-start.9 = (f32[2,256,256]{2,1,0:T(8,128)S(1)}, f32[2,256,256]{2,1,0:T(8,128)}, u32[]{:S(2)}) copy-start(f32[2,256,256]{2,1,0:T(8,128)} %param.13) | copy-start | bytes 1572868
  58.4 10.7 %copy-start.7 = (f32[256,256]{1,0:T(8,128)S(1)}, f32[256,256]{1,0:T(8,128)}, u32[]{:S(2)}) copy-start(f32[256,256]{1,0:T(8,128)} %constant.106.clone) | copy-start | bytes 786436
  67.8 2.0 collective-permute-start.8
  70.6 0.7 collective-permute-start.10
  72.3 0.8 copy-start.5
  73.1 79.1 %all-to-all-start = ((f32[8,2,32,256]{3,2,1,0:T(8,128)}), f32[8,2,32,256]{3,2,1,0:T(8,128)S(1)}, u32[]{:S(2)}, u32[]{:S(2)}) async-start(f32[8,2,32,256]{3,2,1,0:T(8,128)} %copy-done.5), calls=%async_computation | async-start | bytes 1048576 | tf_op jit(solution)/shard_map/all_to_all | solution.py:431
  142.8 22.7 %collective-permute-start.11 = (f32[2,2,256,256]{3,2,1,0:T(8,128)}, f32[2,2,256,256]{3,2,1,0:T(8,128)S(1)}, u32[]{:S(2)}, u32[]{:S(2)}) collective-permute-start(f32[2,2,256,256]{3,2,1,0:T(8,128)} %get-tuple-element.34), channel_id=1, source_target_pairs={{2,0},{3,1},{4,6},{5,7},{8,10},{9,11},{14,12},{15,13},{18,16},{19,... | collective-permute-start | bytes 3145736 | tf_op jit(solution)/shard_map/ppermute | solution.py:319
  144.1 23.9 %collective-permute-start.12 = (f32[2,2,256,256]{3,2,1,0:T(8,128)}, f32[2,2,256,256]{3,2,1,0:T(8,128)S(1)}, u32[]{:S(2)}, u32[]{:S(2)}) collective-permute-start(f32[2,2,256,256]{3,2,1,0:T(8,128)} %get-tuple-element.35), channel_id=1, source_target_pairs={{2,3},{3,2},{4,5},{5,4},{8,9},{9,8},{14,15},{15,14},{18,19},{19,18... | collective-permute-start | bytes 3145736 | tf_op jit(solution)/shard_map/ppermute | solution.py:319
  144.8 30.5 %collective-permute-start.13 = (f32[2,2,256,256]{3,2,1,0:T(8,128)}, f32[2,2,256,256]{3,2,1,0:T(8,128)}, u32[]{:S(2)}, u32[]{:S(2)}) collective-permute-start(f32[2,2,256,256]{3,2,1,0:T(8,128)} %get-tuple-element.36), channel_id=1, source_target_pairs={{2,1},{3,0},{4,7},{5,6},{8,11},{9,10},{14,13},{15,12},{18,17},{19,... | collective-permute-start | bytes 3145736 | tf_op jit(solution)/shard_map/ppermute | solution.py:319
  152.2 3.1 %collective-permute-start.16 = (f32[64,256]{1,0:T(8,128)S(1)}, f32[64,256]{1,0:T(8,128)S(1)}, u32[]{:S(2)}, u32[]{:S(2)}) collective-permute-start(f32[64,256]{1,0:T(8,128)S(1)} %bitcast.41), channel_id=1, source_target_pairs={{8,0},{9,1},{10,2},{11,3},{12,4},{13,5},{14,6},{15,7},{24,16},{25,... | collective-permute-start | bytes 196616 | tf_op jit(solution)/shard_map/ppermute | solution.py:319
  155.4 22.2 %collective-permute-start.17 = (f32[64,256]{1,0:T(8,128)S(1)}, f32[64,256]{1,0:T(8,128)S(1)}, u32[]{:S(2)}, u32[]{:S(2)}) collective-permute-start(f32[64,256]{1,0:T(8,128)S(1)} %bitcast_add_fusion), channel_id=1, source_target_pairs={{0,16},{1,17},{2,18},{3,19},{4,20},{5,21},{6,22},{7,23},{16,32},{1... | collective-permute-start | bytes 196616 | tf_op jit(solution)/shard_map/ppermute | solution.py:319
  158.2 19.4 %collective-permute-start.18 = (f32[64,256]{1,0:T(8,128)S(1)}, f32[64,256]{1,0:T(8,128)}, u32[]{:S(2)}, u32[]{:S(2)}) collective-permute-start(f32[64,256]{1,0:T(8,128)S(1)} %bitcast_add_fusion), channel_id=1, source_target_pairs={{0,32},{1,33},{2,34},{3,35},{4,36},{5,37},{6,38},{7,39},{16,48},{1... | collective-permute-start | bytes 196616 | tf_op jit(solution)/shard_map/ppermute | solution.py:319
  165.5 12.0 %collective-permute-start.19 = (f32[64,256]{1,0:T(8,128)S(1)}, f32[64,256]{1,0:T(8,128)}, u32[]{:S(2)}, u32[]{:S(2)}) collective-permute-start(f32[64,256]{1,0:T(8,128)S(1)} %bitcast_add_fusion), channel_id=1, source_target_pairs={{0,48},{1,49},{2,50},{3,51},{4,52},{5,53},{6,54},{7,55},{16,0},{17... | collective-permute-start | bytes 196616 | tf_op jit(solution)/shard_map/ppermute | solution.py:319
  168.0 7.4 %copy-start.8 = (f32[2,2,256,256]{3,2,1,0:T(8,128)}, f32[2,2,256,256]{3,2,1,0:T(8,128)S(1)}, u32[]{:S(2)}) copy-start(f32[2,2,256,256]{3,2,1,0:T(8,128)S(1)} %collective-permute-done.12) | copy-start | bytes 3145732
  176.9 29.7 %collective-permute-start.15 = (f32[2,2,256,256]{3,2,1,0:T(8,128)S(1)}, f32[2,2,256,256]{3,2,1,0:T(8,128)S(1)}, u32[]{:S(2)}, u32[]{:S(2)}) collective-permute-start(f32[2,2,256,256]{3,2,1,0:T(8,128)S(1)} %get-tuple-element.39), channel_id=1, source_target_pairs={{0,8},{1,9},{2,10},{3,11},{4,12},{5,13},{6,14},{7,15},{8,16},{9,17... | collective-permute-start | bytes 3145736 | tf_op jit(solution)/shard_map/ppermute | solution.py:319
  178.5 10.1 %collective-permute-start.20 = (f32[64,256]{1,0:T(8,128)S(1)}, f32[64,256]{1,0:T(8,128)S(1)}, u32[]{:S(2)}, u32[]{:S(2)}) collective-permute-start(f32[64,256]{1,0:T(8,128)S(1)} %add_add_fusion.1), channel_id=1, source_target_pairs={{0,64},{1,65},{2,66},{3,67},{4,68},{5,69},{6,70},{7,71},{16,80},{1... | collective-permute-start | bytes 196616 | tf_op jit(solution)/shard_map/ppermute | solution.py:319
  180.4 8.2 %collective-permute-start.21 = (f32[64,256]{1,0:T(8,128)S(1)}, f32[64,256]{1,0:T(8,128)S(1)}, u32[]{:S(2)}, u32[]{:S(2)}) collective-permute-start(f32[64,256]{1,0:T(8,128)S(1)} %add_add_fusion.1), channel_id=1, source_target_pairs={{0,128},{1,129},{2,130},{3,131},{4,132},{5,133},{6,134},{7,135},{1... | collective-permute-start | bytes 196616 | tf_op jit(solution)/shard_map/ppermute | solution.py:319
  185.5 6.2 %collective-permute-start.22 = (f32[64,256]{1,0:T(8,128)S(1)}, f32[64,256]{1,0:T(8,128)S(1)}, u32[]{:S(2)}, u32[]{:S(2)}) collective-permute-start(f32[64,256]{1,0:T(8,128)S(1)} %add_add_fusion.1), channel_id=1, source_target_pairs={{0,192},{1,193},{2,194},{3,195},{4,196},{5,197},{6,198},{7,199},{1... | collective-permute-start | bytes 196616 | tf_op jit(solution)/shard_map/ppermute | solution.py:319
  188.5 4.5 %collective-permute-start.14 = (f32[2,2,1,256]{3,2,1,0:T(1,128)S(1)}, f32[2,2,1,256]{3,2,1,0:T(1,128)S(1)}, u32[]{:S(2)}, u32[]{:S(2)}) collective-permute-start(f32[2,2,1,256]{3,2,1,0:T(1,128)S(1)} %slice.39), channel_id=1, source_target_pairs={{0,248},{1,249},{2,250},{3,251},{4,252},{5,253},{6,254},{7,255},{8... | collective-permute-start | bytes 12296 | tf_op jit(solution)/shard_map/ppermute | solution.py:319
  191.7 2.2 %collective-permute-start.23 = (f32[64,256]{1,0:T(8,128)S(1)}, f32[64,256]{1,0:T(8,128)S(1)}, u32[]{:S(2)}, u32[]{:S(2)}) collective-permute-start(f32[64,256]{1,0:T(8,128)S(1)} %add_add_fusion), channel_id=1, source_target_pairs={{0,8},{1,9},{2,10},{3,11},{4,12},{5,13},{6,14},{7,15},{16,24},{17,... | collective-permute-start | bytes 196616 | tf_op jit(solution)/shard_map/ppermute | solution.py:319
